TPU v7x, 32 devices: a whole 2x2x4 slice. The times are simulated.
32 devices in a mesh: segment: 2 (over x), win: 4 (over z), mp: 4 (over y, core).
Axes of the slice: x: 2, y: 2, z: 4, core: 2. Of those that a mesh axis runs over, the one named last changes fastest.
Arguments:
- feats: bfloat16 [4, 1536, 256], P('win'), may hold values from -6 to 6
- convolution_kernel_weight: bfloat16 [1536, 5, 1536], P('win', None, 'mp'), may hold values from -0.0625 to 0.0625
- conv_bias: float32 [1536], P('mp'), may hold values from -3 to 3
- qkv_weight: bfloat16 [1536, 2560], P('win', 'mp'), may hold values from -0.15625 to 0.15625
- out_weight: bfloat16 [1536, 1536], P('win', 'mp'), may hold values from -0.15625 to 0.15625
- head_weight: bfloat16 [1536, 4096], P('win', 'mp'), may hold values from -0.15625 to 0.15625
- head_bias: float32 [4096], P('mp'), may hold values from -4 to 4
- exon_lists: int32 [3, 4, 8, 8], P(None, 'win'), may hold values from 0 to 256, as said below
Outputs:
- gene_tracks: float32 [64, 4096], P(('segment', 'win'), 'mp')
Inputs may be any that keep to these rules, and one draw needn't show every extreme that they name: `exon_lists`: A slot with equal first and end bin is unused and has gene slot 0; used slots have 1 to 8 bins and a gene slot below 8. In every draw some owners receive 8 used ranges from every window.
All inputs are finite; a program needn't handle non-finite values.
Results may differ from a plain program's by a relative error of at most 0.0025.
Values may be sent and summed in bfloat16 or wider, within the bound.
No kernel may reach another device: no remote copies, remote signals or barrier semaphores. Data moves between devices by JAX's collectives and lax.ppermute only.
A program may use at most 64 MiB of HBM per device.

v0:
```python
import math

import jax
import jax.numpy as jnp
from jax import lax
from jax.sharding import PartitionSpec as P

KEY = 64
VAL = 192
DILATION_STEP = 4
GENE_DEV = 8


def passed_along(x, axis, by):
    devices = lax.axis_size(axis)
    pairs = [(i, i + by) for i in range(devices) if 0 <= i + by < devices]
    return lax.ppermute(x, axis, pairs)


def contract_rows(left, right):
    return lax.dot_general(
        left, right, (((0,), (0,)), ((), ())), preferred_element_type=jnp.float32
    )


def conv_terms(piece, padded_input, window_bin_count):
    running = contract_rows(piece[:, 0, :], padded_input[:, 0:window_bin_count])
    for tap_index in range(1, piece.shape[1]):
        shifted_input = padded_input[
            :, tap_index * DILATION_STEP : tap_index * DILATION_STEP + window_bin_count
        ]
        running = running + contract_rows(piece[:, tap_index, :], shifted_input)
    return running


def make_section_collect(padded_input, window_bin_count, conv_segment, tap_count, out_cols):

    def collect(carried, piece, offset_row):
        conv_acc, packed_full = carried
        conv_piece = piece[:, : tap_count * out_cols].reshape(piece.shape[0], tap_count, out_cols)
        conv_acc = lax.cond(
            conv_segment,
            lambda running: conv_terms(conv_piece, padded_input, window_bin_count),
            lambda running: running,
            conv_acc,
        )
        packed_full = piece
        return (conv_acc, packed_full)

    return collect


def attend(all_chan, qkv_full):
    qkv_rows = contract_rows(qkv_full, all_chan).astype(jnp.bfloat16)
    head_span = 2 * KEY + VAL
    score_scale = 1.0 / math.sqrt(KEY)
    outputs = []
    for head_idx in range(qkv_full.shape[1] // head_span):
        offset = head_idx * head_span
        query_rows = qkv_rows[offset : offset + KEY]
        key_rows = qkv_rows[offset + KEY : offset + 2 * KEY]
        value_rows = qkv_rows[offset + 2 * KEY : offset + head_span]
        scores = contract_rows(query_rows, key_rows) * score_scale
        weights = jnp.exp(scores)
        prob_rows = (weights / jnp.sum(weights, axis=1, keepdims=True)).astype(jnp.bfloat16)
        head_out = lax.dot_general(
            value_rows, prob_rows, (((1,), (1,)), ((), ())), preferred_element_type=jnp.float32
        )
        outputs.append(head_out.astype(jnp.bfloat16))
    return jnp.concatenate(outputs, axis=0)


def project(out_full, joined):
    return lax.dot_general(
        out_full, joined, (((1,), (0,)), ((), ())), preferred_element_type=jnp.float32
    )


def gene_entries(resid, head_full, bias_cols, ranges):
    logits = contract_rows(head_full, resid) + bias_cols[:, None]
    tracks = jax.nn.softplus(logits).astype(jnp.bfloat16)
    position = jnp.arange(resid.shape[1], dtype=jnp.int32)
    starts = ranges[0].reshape(-1)
    end_bins = ranges[1].reshape(-1)
    inside = (position[None, :] >= starts[:, None]) & (position[None, :] < end_bins[:, None])
    return lax.dot_general(
        inside.astype(jnp.bfloat16),
        tracks,
        (((1,), (1,)), ((), ())),
        preferred_element_type=jnp.float32,
    )


def local(
    feats,
    convolution_kernel_weight,
    conv_bias,
    qkv_weight,
    out_weight,
    head_weight,
    head_bias,
    exon_lists,
):
    segment_index = lax.axis_index("segment")
    model_index = lax.axis_index("mp")
    source = feats[0]
    chan_count, window_bin_count = source.shape
    tap_count = convolution_kernel_weight.shape[1]
    out_cols = convolution_kernel_weight.shape[2]
    receptive_reach_bins = (tap_count - 1) // 2 * DILATION_STEP
    padded_input = jnp.pad(source, ((0, 0), (receptive_reach_bins, receptive_reach_bins)))
    ranges = exon_lists[:, 0]
    owners = ranges.shape[1]
    slot_count = ranges.shape[2]
    slot_ids = jnp.arange(GENE_DEV, dtype=jnp.int32)
    gene_slots = ranges[2].astype(jnp.float32)
    conv_segment = segment_index == 0
    local_rows = convolution_kernel_weight.shape[0]
    conv_flat = convolution_kernel_weight.reshape(local_rows, tap_count * out_cols)
    later_flat = jnp.concatenate([qkv_weight, out_weight, head_weight], axis=1)
    packed_width = max(conv_flat.shape[1], later_flat.shape[1])
    conv_flat = jnp.pad(conv_flat, ((0, 0), (0, packed_width - conv_flat.shape[1])))
    packed = jnp.where(conv_segment, conv_flat, later_flat)
    collect = make_section_collect(
        padded_input, window_bin_count, conv_segment, tap_count, out_cols
    )
    start_state = (
        jnp.zeros((out_cols, window_bin_count), jnp.float32),
        jnp.zeros((chan_count, packed_width), jnp.bfloat16),
    )
    conv_acc, packed_full = collect(
        start_state, lax.all_gather(packed, "win", axis=0, tiled=True), jnp.int32(0)
    )
    qkv_cols = qkv_weight.shape[1]
    proj_cols = out_weight.shape[1]
    track_width = head_weight.shape[1]
    qkv_full = packed_full[:, :qkv_cols]
    out_full = packed_full[:, qkv_cols : qkv_cols + proj_cols]
    head_full = packed_full[:, qkv_cols + proj_cols : qkv_cols + proj_cols + track_width]
    own_rows = lax.dynamic_slice_in_dim(source, model_index * out_cols, out_cols, 0)
    conv_out = (own_rows + jax.nn.gelu(conv_acc + conv_bias[:, None])).astype(jnp.bfloat16)
    handed = passed_along(conv_out, "segment", 1)
    all_chan = lax.all_gather(handed, "mp", axis=0, tiled=True)
    attn_segment = segment_index == 1
    partial_value = lax.cond(
        attn_segment,
        lambda: project(out_full, attend(all_chan, qkv_full)),
        lambda: jnp.zeros((chan_count, window_bin_count), jnp.float32),
    )
    summed = lax.psum(partial_value.astype(jnp.bfloat16), "mp").astype(jnp.float32)
    resid = (all_chan.astype(jnp.float32) + summed).astype(jnp.bfloat16)
    track_cols = head_full.shape[1]
    entries = lax.cond(
        attn_segment,
        lambda: gene_entries(resid, head_full, head_bias, ranges),
        lambda: jnp.zeros((owners * slot_count, track_cols), jnp.float32),
    )
    entry_rows = entries.reshape(owners, slot_count, track_cols)
    got_rows, got_slots = (
        lax.all_to_all(
            entry_rows.astype(jnp.bfloat16),
            ("segment", "win"),
            split_axis=0,
            concat_axis=0,
            tiled=True,
        ).astype(entry_rows.dtype),
        lax.all_to_all(
            gene_slots.astype(jnp.bfloat16),
            ("segment", "win"),
            split_axis=0,
            concat_axis=0,
            tiled=True,
        ).astype(gene_slots.dtype),
    )
    onehot = (got_slots.reshape(-1).astype(jnp.int32)[:, None] == slot_ids[None, :]).astype(
        jnp.float32
    )
    gene_sum = lax.dot_general(
        onehot,
        got_rows.reshape(owners * slot_count, track_cols),
        (((0,), (0,)), ((), ())),
        precision=lax.Precision.HIGHEST,
        preferred_element_type=jnp.float32,
    )
    return jnp.log1p(gene_sum)


def solution(mesh):
    in_specs = (
        P("win", None, None),
        P("win", None, "mp"),
        P("mp"),
        P("win", "mp"),
        P("win", "mp"),
        P("win", "mp"),
        P("mp"),
        P(None, "win", None, None),
    )
    out_specs = P(("segment", "win"), "mp")
    return jax.shard_map(local, mesh=mesh, in_specs=in_specs, out_specs=out_specs, check_vma=False)
```

profile of v0, /device:TPU:0, one launch (start us, length us, event | category | flops | bytes accessed | tf_op | source)
XLA Modules:
  0.0 239.2 jit_solution(13340747138413626250)
XLA Ops:
  6.5 0.0 copy-start.1
  6.5 0.0 all-gather.2.cloned.1.call-start
  6.5 2.7 %copy.35 = bf16[384,5,384]{0,2,1:T(8,128)(2,1)S(1)} copy(bf16[384,5,384]{2,0,1:T(8,128)(2,1)} %param.15) | data formatting | bytes 2949120 | tf_op args[1]
  9.2 0.0 copy-done.1
  9.2 0.4 copy.38
  9.6 1.3 copy.36
  10.9 1.9 copy.37
  12.7 0.0 copy-start
  12.7 2.5 %maximum_select_fusion = bf16[384,2048]{0,1:T(8,128)(2,1)} fusion(bf16[384,1024]{0,1:T(8,128)(2,1)S(1)} %copy.38, bf16[384,384]{0,1:T(8,128)(2,1)} %copy.37, bf16[384,640]{0,1:T(8,128)(2,1)S(1)} %copy.36, bf16[384,1920]{0,1:T(8,128)(2,1)S(1)} %bitcast.59, pred[]{:T(512)S(6)} %eq.23), kind=kLoop, calls=%fused_computation.61 | loop fusion | flops 5505024 | bytes 4620289 | tf_op jit(solution)/shard_map/jit(_where)/select_n | solution.py:123
  15.3 0.0 all-gather.2.cloned.1.call-update
  15.3 0.0 all-reduce.4.cloned.1.call-start
  15.4 118.1 %all-gather.2.cloned.1.call-done = bf16[1536,2048]{0,1:T(8,128)(2,1)} async-done(((bf16[384,2048]{0,1:T(8,128)(2,1)}), bf16[1536,2048]{0,1:T(8,128)(2,1)}) %all-gather.2.cloned.1.call-update) | async-done | bytes 6291472 | tf_op jit(solution)/shard_map/all_gather | solution.py:132
  133.5 0.0 copy-done
  133.5 0.0 copy-start.3
  133.5 7.6 %conditional.3 = (f32[384,256]{1,0:T(8,128)S(1)}) conditional(s32[]{:T(128)} %convert_element_type.111, () %tuple.24, (bf16[1,1536,256]{2,1,0:T(8,128)(2,1)S(1)}, bf16[1536,2048]{0,1:T(8,128)(2,1)}) %tuple.48), branch_computations={%region_0.1_spmd, %region_1.2_spmd} | conditional | flops 1510342656 | bytes 25952264 | solution.py:41
  133.5 3.1 %slice.53 = bf16[1536,1920]{0,1:T(8,128)(2,1)S(1)} slice(bf16[1536,2048]{0,1:T(8,128)(2,1)} %get-tuple-element.41), slice={[0:1536], [0:1920]} | slice | bytes 11796480 | tf_op jit(solution)/shard_map/slice | solution.py:40
  136.6 0.9 fusion.3
  137.5 0.9 fusion.2
  138.4 0.6 convolution_add_fusion
  139.1 0.9 convolution_bitcast_fusion
  140.0 0.9 fusion.1
  140.9 0.2 copy.45
  141.1 0.0 copy-done.3
  141.1 0.2 fusion.55
  141.3 1.3 collective-permute-start
  142.6 4.6 %collective-permute-done = bf16[384,256]{1,0:T(8,128)(2,1)S(1)} collective-permute-done((bf16[384,256]{1,0:T(8,128)(2,1)S(1)}, bf16[384,256]{1,0:T(8,128)(2,1)S(1)}, u32[]{:S(2)}, u32[]{:S(2)}) %collective-permute-start) | collective-permute-done | bytes 196640 | tf_op jit(solution)/shard_map/ppermute | solution.py:17
  147.3 8.6 %all_gather.7 = bf16[1536,256]{1,0:T(8,128)(2,1)S(1)} all-gather(bf16[384,256]{1,0:T(8,128)(2,1)S(1)} %collective-permute-done), channel_id=1, replica_groups=mesh['segment'=2,'win'=4,'mp'=4] {'mp'}, dimensions={0}, use_global_device_ids=true | all-gather | bytes 983040 | tf_op jit(solution)/shard_map/all_gather | solution.py:143
  155.8 0.1 conditional.4
  155.8 0.1 broadcast.12
  155.9 0.0 copy-start.2
  155.9 1.2 copy.41
  157.1 0.0 copy-start.4
  157.1 0.0 all-reduce.4.cloned.1.call-update
  157.1 0.0 copy-done.2
  157.1 0.6 copy.34
  157.7 17.4 %all-to-all-start = ((bf16[8,1,8]{2,1,0:T(2,128)(2,1)}), bf16[8,1,8]{2,1,0:T(2,128)(2,1)S(1)}, u32[]{:S(2)}, u32[]{:S(2)}) async-start(bf16[8,1,8]{2,1,0:T(2,128)(2,1)} %copy.34), calls=%async_computation | async-start | bytes 8192 | tf_op jit(solution)/shard_map/all_to_all | solution.py:167
  175.2 28.9 %all-reduce.4.cloned.1.call-done = bf16[1536,256]{1,0:T(8,128)(2,1)} async-done(((bf16[1536,256]{1,0:T(8,128)(2,1)}), bf16[1536,256]{1,0:T(8,128)(2,1)}) %all-reduce.4.cloned.1.call-update) | async-done | bytes 786448 | tf_op jit(solution)/shard_map/psum | solution.py:150
  204.1 1.3 add_convert_fusion
  205.4 0.0 copy-done.4
  205.4 0.7 conditional.5
  205.4 0.7 broadcast.14
  206.1 0.0 all-to-all-done
  206.1 17.9 %all-to-all-start.1 = ((bf16[8,8,1024]{2,1,0:T(8,128)(2,1)}), bf16[8,8,1024]{2,1,0:T(8,128)(2,1)S(1)}, u32[]{:S(2)}, u32[]{:S(2)}) async-start(bf16[8,8,1024]{2,1,0:T(8,128)(2,1)} %bitcast.51), calls=%async_computation.1 | async-start | bytes 262144 | tf_op jit(solution)/shard_map/all_to_all | solution.py:160
  224.0 0.1 convert_element_type.107
  224.1 7.4 %all-to-all-done.1 = bf16[8,8,1024]{2,1,0:T(8,128)(2,1)S(1)} async-done(((bf16[8,8,1024]{2,1,0:T(8,128)(2,1)}), bf16[8,8,1024]{2,1,0:T(8,128)(2,1)S(1)}, u32[]{:S(2)}, u32[]{:S(2)}) %all-to-all-start.1) | async-done | bytes 131104 | tf_op jit(solution)/shard_map/all_to_all | solution.py:160
  231.5 0.9 convolution_log-plus-one_fusion
  (2 shorter events, 0.0 us)
Async XLA Ops:
  6.5 2.7 %copy-start.1 = (bf16[384,1024]{1,0:T(8,128)(2,1)S(1)}, bf16[384,1024]{1,0:T(8,128)(2,1)}, u32[]{:S(2)}) copy-start(bf16[384,1024]{1,0:T(8,128)(2,1)} %param.19) | copy-start | bytes 2359300
  6.5 127.0 %all-gather.2.cloned.1.call-start = ((), (), s32[]{:S(2)}) async-start(), calls=%async_computation.2 | async-start | bytes 7864320 | tf_op jit(solution)/shard_map/all_gather | solution.py:132
  12.7 120.8 %copy-start = (bf16[1,1536,256]{2,1,0:T(8,128)(2,1)S(1)}, bf16[1,1536,256]{2,1,0:T(8,128)(2,1)}, u32[]{:S(2)}) copy-start(bf16[1,1536,256]{2,1,0:T(8,128)(2,1)} %param.14) | copy-start | bytes 2359300
  15.3 188.8 %all-reduce.4.cloned.1.call-start = ((), (), s32[]{:S(2)}) async-start(), calls=%async_computation.3 | async-start | bytes 1572864 | tf_op jit(solution)/shard_map/psum | solution.py:150
  133.5 7.6 %copy-start.3 = (f32[384]{0:T(512)S(1)}, f32[384]{0:T(512)}, u32[]{:S(2)}) copy-start(f32[384]{0:T(512)} %param.16) | copy-start | bytes 4612
  141.3 5.9 %collective-permute-start = (bf16[384,256]{1,0:T(8,128)(2,1)S(1)}, bf16[384,256]{1,0:T(8,128)(2,1)S(1)}, u32[]{:S(2)}, u32[]{:S(2)}) collective-permute-start(bf16[384,256]{1,0:T(8,128)(2,1)S(1)} %fusion.55), channel_id=1, source_target_pairs={{0,16},{1,17},{2,18},{3,19},{4,20},{5,21},{6,22},{7,23},{8,24},{9,... | collective-permute-start | bytes 589832 | tf_op jit(solution)/shard_map/ppermute | solution.py:17
  155.9 1.2 copy-start.2
  157.1 48.4 %copy-start.4 = (f32[1024]{0:T(1024)S(1)}, f32[1024]{0:T(1024)}, u32[]{:S(2)}) copy-start(f32[1024]{0:T(1024)} %param.20) | copy-start | bytes 12292
  157.7 48.4 %all-to-all-start = ((bf16[8,1,8]{2,1,0:T(2,128)(2,1)}), bf16[8,1,8]{2,1,0:T(2,128)(2,1)S(1)}, u32[]{:S(2)}, u32[]{:S(2)}) async-start(bf16[8,1,8]{2,1,0:T(2,128)(2,1)} %copy.34), calls=%async_computation | async-start | bytes 8192 | tf_op jit(solution)/shard_map/all_to_all | solution.py:167
  206.1 25.4 %all-to-all-start.1 = ((bf16[8,8,1024]{2,1,0:T(8,128)(2,1)}), bf16[8,8,1024]{2,1,0:T(8,128)(2,1)S(1)}, u32[]{:S(2)}, u32[]{:S(2)}) async-start(bf16[8,8,1024]{2,1,0:T(8,128)(2,1)} %bitcast.51), calls=%async_computation.1 | async-start | bytes 262144 | tf_op jit(solution)/shard_map/all_to_all | solution.py:160
Sparse Core Ops, SparseCore 0:
  15.4 118.0 all-gather.1
  157.2 46.8 all-reduce.3
where the time goes:
time: 240 us; the launch traced here: 239 us
  waiting for transfers between devices  159 us (66%)
  starting transfers between devices  36.7 us (15%)
  between operations  13.5 us (6%)
  local copies, waits for them, and re-layouts  12 us (5%)
  blocking collectives  8.56 us (4%)
  matrix products  5.16 us (2%)
  other arithmetic  4.14 us (2%)
    all_gather x1, waiting for transfers between devices, local(): lax.all_gather(packed, 'win', axis=0, tiled=True)  118 us
    psum x1, waiting for transfers between devices, local(): lax.psum(partial_value.astype(jnp.bfloat16), 'mp').astype(jnp.float32)  28.9 us
    all_to_all x1, starting transfers between devices, local(): lax.all_to_all(entry_rows.astype(jnp.bfloat16), ('segment', 'win'), split...  17.9 us
    all_to_all x1, starting transfers between devices, local(): lax.all_to_all(gene_slots.astype(jnp.bfloat16), ('segment', 'win'), split...  17.4 us
    all_gather x1, blocking collectives, local(): all_chan = lax.all_gather(handed, 'mp', axis=0, tiled=True)  8.56 us
    all_to_all x1, waiting for transfers between devices, local(): lax.all_to_all(entry_rows.astype(jnp.bfloat16), ('segment', 'win'), split...  7.42 us
    unnamed x14, local copies, waits for them, and re-layouts  6.19 us
  transfers between devices with their start and end apart: 5, of which 4 were waited for; matrix products, arithmetic and copies ran while one was open for 1% of the time, Pallas kernels for 0%

commit v1 on v0

v1 whole, which is shorter than its diff:
```python
import functools
import math

import jax
import jax.numpy as jnp
from jax import lax
from jax.experimental import pallas as pl
from jax.experimental.pallas import tpu as pltpu
from jax.sharding import PartitionSpec as P

KEY = 64
VAL = 192
DILATION_STEP = 4
GENE_DEV = 8
SPAN = 2 * KEY + VAL
VMEM_BYTES = 40 * 1024 * 1024
F32 = jnp.float32
BF16 = jnp.bfloat16


def call_kernel(body, out_shape, *operands, flops=0):
    whole = pl.BlockSpec(memory_space=pltpu.VMEM)
    return pl.pallas_call(
        body,
        out_shape=out_shape,
        in_specs=[whole] * len(operands),
        out_specs=whole,
        compiler_params=pltpu.CompilerParams(vmem_limit_bytes=VMEM_BYTES),
        cost_estimate=pl.CostEstimate(flops=flops, bytes_accessed=1 << 20, transcendentals=0),
    )(*operands)


def shifted(x, axis, by):
    size = lax.axis_size(axis)
    return lax.ppermute(x, axis, [(i, (i + by) % size) for i in range(size)])


def conv_kernel(x_ref, w_ref, o_ref):
    bins = o_ref.shape[0]
    x = x_ref[...].astype(F32)
    total = jnp.zeros(o_ref.shape, F32)
    for tap in range(w_ref.shape[0]):
        start = tap * DILATION_STEP
        total += jnp.dot(
            x[start : start + bins].astype(BF16), w_ref[tap], preferred_element_type=F32
        )
    o_ref[...] = total.astype(o_ref.dtype)


def joined_bins(blocks_ref, segments):
    models = blocks_ref.shape[0] // segments
    rows = [
        jnp.concatenate([blocks_ref[s * models + m] for m in range(models)], axis=1)
        for s in range(segments)
    ]
    return jnp.concatenate(rows, axis=0)


def attention_kernel(segments, x_ref, qkv_ref, out_ref, o_ref):
    x = joined_bins(x_ref, segments)
    models = o_ref.shape[0] // segments
    bins, cols = o_ref.shape[1:]
    total = None
    for head in range(qkv_ref.shape[1] // SPAN):
        rows = jnp.dot(
            x, qkv_ref[:, head * SPAN : (head + 1) * SPAN], preferred_element_type=F32
        ).astype(BF16)
        query, key, value = rows[:, :KEY], rows[:, KEY : 2 * KEY], rows[:, 2 * KEY :]
        scores = lax.dot_general(
            query, key, (((1,), (1,)), ((), ())), preferred_element_type=F32
        ) * (1.0 / math.sqrt(KEY))
        weights = jnp.exp(scores)
        probs = (weights / jnp.sum(weights, axis=1, keepdims=True)).astype(BF16)
        att = jnp.dot(probs, value, preferred_element_type=F32).astype(BF16)
        term = lax.dot_general(
            att,
            out_ref[:, head * VAL : (head + 1) * VAL],
            (((1,), (1,)), ((), ())),
            preferred_element_type=F32,
        )
        total = term if total is None else total + term
    total = total.astype(o_ref.dtype)
    for s in range(segments):
        for m in range(models):
            o_ref[s * models + m] = total[s * bins : (s + 1) * bins, m * cols : (m + 1) * cols]


def head_kernel(segments, x_ref, w_ref, b_ref, counts_ref, o_ref):
    x = joined_bins(x_ref, segments)
    logits = jnp.dot(x, w_ref[...], preferred_element_type=F32) + b_ref[...]
    tracks = jax.nn.softplus(logits).astype(BF16)
    sums = jnp.dot(counts_ref[...], tracks, preferred_element_type=F32)
    o_ref[...] = sums.astype(o_ref.dtype)


def gene_counts(ranges, bins):
    position = jnp.arange(bins, dtype=jnp.int32)
    inside = (position >= ranges[0][:, :, None]) & (position < ranges[1][:, :, None])
    slots = jnp.arange(GENE_DEV, dtype=jnp.int32)
    chosen = ranges[2][:, None, :] == slots[None, :, None]
    counts = jnp.sum(
        (chosen[..., None] & inside[:, None]).astype(F32), axis=2
    )
    return counts.reshape(-1, bins).astype(BF16)


def local(
    feats,
    convolution_kernel_weight,
    conv_bias,
    qkv_weight,
    out_weight,
    head_weight,
    head_bias,
    exon_lists,
):
    segment_index = lax.axis_index("segment")
    win_index = lax.axis_index("win")
    model_index = lax.axis_index("mp")
    segments, windows, models = (lax.axis_size(a) for a in ("segment", "win", "mp"))
    chan_count, bin_count = feats.shape[1:]
    row_count, tap_count, out_cols = convolution_kernel_weight.shape
    bins = bin_count // segments
    reach = (tap_count - 1) // 2 * DILATION_STEP
    plane = ("segment", "mp")

    def part_of_segment(x):
        size = x.shape[1] // segments
        return lax.dynamic_slice_in_dim(x, segment_index * size, size, 1)

    qkv_full = lax.all_gather(part_of_segment(qkv_weight), "win", axis=0, tiled=True)
    out_full = lax.all_gather(part_of_segment(out_weight), "win", axis=0, tiled=True)
    head_full = lax.all_gather(part_of_segment(head_weight), "win", axis=0, tiled=True)
    track_cols = head_full.shape[1]
    bias_part = lax.dynamic_slice_in_dim(head_bias, segment_index * track_cols, track_cols, 0)
    counts = gene_counts(exon_lists[:, 0], bin_count)

    taps = jnp.transpose(convolution_kernel_weight, (1, 0, 2))
    padded = jnp.pad(feats[0].T, ((reach, reach), (0, 0)))
    own_bins = lax.dynamic_slice_in_dim(padded, segment_index * bins, bins + 2 * reach, 0)

    def rows_for(window):
        return lax.dynamic_slice_in_dim(own_bins, window * row_count, row_count, 1)

    def conv_of(x, dtype):
        return call_kernel(
            conv_kernel,
            jax.ShapeDtypeStruct((bins, out_cols), dtype),
            x,
            taps,
            flops=2 * bins * out_cols * row_count * tap_count,
        )

    if windows <= 8:
        arrived = [
            shifted(rows_for(lax.rem(win_index + by, windows)), "win", by)
            for by in range(1, windows)
        ]
        conv_pre = conv_of(rows_for(win_index), F32)
        for by, x in enumerate(arrived, 1):
            conv_pre = conv_pre + shifted(conv_of(x, BF16), "win", -by).astype(F32)
    else:
        blocks = own_bins.reshape(own_bins.shape[0], windows, row_count).transpose(1, 0, 2)
        arrived = lax.all_to_all(blocks, "win", 0, 0, tiled=True)
        partial = jnp.stack([conv_of(arrived[w], BF16) for w in range(windows)])
        conv_pre = lax.all_to_all(partial, "win", 0, 0, tiled=True).astype(F32).sum(axis=0)

    own_feats = lax.dynamic_slice(own_bins, (reach, model_index * out_cols), (bins, out_cols))
    conv_out = (own_feats + jax.nn.gelu(conv_pre + conv_bias)).astype(BF16)
    all_chan = lax.all_gather(conv_out, plane, axis=0)

    partial = call_kernel(
        functools.partial(attention_kernel, segments),
        jax.ShapeDtypeStruct(all_chan.shape, BF16),
        all_chan,
        qkv_full,
        out_full,
    )
    summed = lax.all_to_all(partial, plane, 0, 0, tiled=True).astype(F32).sum(axis=0)
    resid = (conv_out.astype(F32) + summed).astype(BF16)
    all_resid = lax.all_gather(resid, plane, axis=0)

    sums = call_kernel(
        functools.partial(head_kernel, segments),
        jax.ShapeDtypeStruct((counts.shape[0], track_cols), BF16),
        all_resid,
        head_full,
        bias_part[None, :],
        counts,
    )
    owners = segments * windows
    got = lax.all_to_all(
        sums.reshape(owners, GENE_DEV, track_cols), ("segment", "win"), 0, 0, tiled=True
    )
    got = got.astype(F32).reshape(segments, windows, GENE_DEV, track_cols).sum(axis=1)
    return jnp.log1p(got.transpose(1, 0, 2).reshape(GENE_DEV, segments * track_cols))


def solution(mesh):
    in_specs = (
        P("win", None, None),
        P("win", None, "mp"),
        P("mp"),
        P("win", "mp"),
        P("win", "mp"),
        P("win", "mp"),
        P("mp"),
        P(None, "win", None, None),
    )
    out_specs = P(("segment", "win"), "mp")
    return jax.shard_map(local, mesh=mesh, in_specs=in_specs, out_specs=out_specs, check_vma=False)
```

time: 240 us -> 158 us (0.66)
  waiting for transfers between devices: 159 us -> 11.2 us
  blocking collectives: 8.56 us -> 90.6 us
  starting transfers between devices: 36.7 us -> 22.9 us
  Pallas kernels: 0 us -> 9.6 us
  matrix products: 5.16 us -> 0 us
  local copies, waits for them, and re-layouts: 12 us -> 7.42 us
  other arithmetic: 4.14 us -> 1.71 us
    all_gather x1, waiting for transfers between devices: 118 us -> 0.01 us  [local(): lax.all_gather(part_of_segment(head_weight), 'win', axis=0, tiled=True)]
    all_gather x1 -> x4, blocking collectives: 8.56 us -> 80.5 us  [the longest x1 41.2 us: local(): lax.all_gather(part_of_segment(qkv_weight), 'win', axis=0, tiled=True)]
    all_to_all x2 -> x1, starting transfers between devices: 35.3 us -> 3.68 us  [local(): lax.all_to_all(partial, plane, 0, 0, tiled=True).astype(F32).sum(axis=0)]
    psum x1 -> x0, waiting for transfers between devices: 28.9 us -> none  [local(): lax.psum(partial_value.astype(jnp.bfloat16), 'mp').astype(jnp.float32)]
    ppermute x1 -> x6, starting transfers between devices: 1.3 us -> 19.3 us  [shifted(): return lax.ppermute(x, axis, [(i, (i + by) % size) for i in range(size)])]
    all_to_all x0 -> x1, blocking collectives: none -> 10.1 us  [local(): lax.all_to_all(sums.reshape(owners, GENE_DEV, track_cols), ('segment', 'w...]
    pallas_call x0 -> x6, Pallas kernels: none -> 9.6 us  [call_kernel(): pl.pallas_call(body, out_shape=out_shape, in_specs=[whole] * len(operands...]
    dot_general x6 -> x0, matrix products: 5.16 us -> none  [the longest x5 4.28 us: contract_rows(): lax.dot_general(left, right, (((0,), (0,)), ((), ())), preferred_element_...]
  transfers between devices with their start and end apart: 5 -> 8, of which waited for: 4 -> 1; matrix products, arithmetic and copies ran while one was open for 1% -> 3% of each run, Pallas kernels for 0% -> 5%
where the time goes in v1:
time: 158 us; the launch traced here: 157 us
  blocking collectives  90.6 us (57%)
  starting transfers between devices  22.9 us (14%)
  between operations  13.6 us (9%)
  waiting for transfers between devices  11.2 us (7%)
  Pallas kernels  9.6 us (6%)
  local copies, waits for them, and re-layouts  7.42 us (5%)
  other arithmetic  1.71 us (1%)
    all_gather x1, blocking collectives, local(): lax.all_gather(part_of_segment(qkv_weight), 'win', axis=0, tiled=True)  41.2 us
    ppermute x6, starting transfers between devices, shifted(): return lax.ppermute(x, axis, [(i, (i + by) % size) for i in range(size)])  19.3 us
    all_gather x1, blocking collectives, local(): lax.all_gather(part_of_segment(out_weight), 'win', axis=0, tiled=True)  18.3 us
    all_to_all x1, waiting for transfers between devices, local(): lax.all_to_all(partial, plane, 0, 0, tiled=True).astype(F32).sum(axis=0)  11.2 us
    all_gather x1, blocking collectives, local(): all_chan = lax.all_gather(conv_out, plane, axis=0)  10.7 us
    all_gather x1, blocking collectives, local(): all_resid = lax.all_gather(resid, plane, axis=0)  10.4 us
    all_to_all x1, blocking collectives, local(): lax.all_to_all(sums.reshape(owners, GENE_DEV, track_cols), ('segment', 'w...  10.1 us
    pallas_call x6, Pallas kernels, call_kernel(): pl.pallas_call(body, out_shape=out_shape, in_specs=[whole] * len(operands...  9.6 us
  transfers between devices with their start and end apart: 8, of which 1 were waited for; matrix products, arithmetic and copies ran while one was open for 3% of the time, Pallas kernels for 5%

profile of v1, /device:TPU:0, one launch (start us, length us, event | category | flops | bytes accessed | tf_op | source)
XLA Modules:
  0.0 157.1 jit_solution(3249323508419368100)
XLA Ops:
  6.5 0.0 copy-start
  6.5 0.0 all-gather.4.cloned.1.call-start
  6.5 1.5 copy.10
  8.0 0.0 copy-start.4
  8.0 0.0 copy-start.6
  8.0 1.0 pad_dynamic-slice_fusion.2
  9.1 3.0 %collective-permute-start = (bf16[144,384]{1,0:T(8,128)(2,1)}, bf16[144,384]{1,0:T(8,128)(2,1)}, u32[]{:S(2)}, u32[]{:S(2)}) collective-permute-start(bf16[144,384]{1,0:T(8,128)(2,1)} %get-tuple-element.5), channel_id=1, source_target_pairs={{0,4},{4,8},{8,12},{12,0},{1,5},{5,9},{9,13},{13,1},{2,6},{6,10},{... | collective-permute-start | bytes 331784 | tf_op jit(solution)/shard_map/ppermute | solution.py:35
  12.1 2.6 %collective-permute-start.2 = (bf16[144,384]{1,0:T(8,128)(2,1)}, bf16[144,384]{1,0:T(8,128)(2,1)}, u32[]{:S(2)}, u32[]{:S(2)}) collective-permute-start(bf16[144,384]{1,0:T(8,128)(2,1)} %get-tuple-element.7), channel_id=1, source_target_pairs={{0,8},{4,12},{8,0},{12,4},{1,9},{5,13},{9,1},{13,5},{2,10},{6,14},... | collective-permute-start | bytes 331784 | tf_op jit(solution)/shard_map/ppermute | solution.py:35
  14.7 1.4 collective-permute-start.4
  16.0 0.0 copy-done.4
  16.0 0.0 copy-done
  16.0 0.8 constant_dynamic-slice_fusion
  16.8 0.0 all-gather.4.cloned.1.call-update
  16.8 0.0 copy-done.6
  16.8 0.2 constant_dynamic-slice_fusion.2
  17.0 41.2 %all_gather.23.qkv_ref = bf16[1536,320]{1,0:T(8,128)(2,1)S(1)} all-gather(bf16[384,320]{1,0:T(8,128)(2,1)S(1)} %constant_dynamic-slice_fusion.2), channel_id=1, replica_groups=mesh['segment'=2,'win'=4,'mp'=4] {'win'}, dimensions={0}, use_global_device_ids=true | all-gather | bytes 1228800 | tf_op jit(solution)/shard_map/all_gather | solution.py:131
  58.2 1.1 constant_dynamic-slice_fusion.1
  59.3 0.0 collective-permute-done.x_ref
  59.3 2.0 %shard_map.83 = bf16[128,384]{1,0:T(8,128)(2,1)} custom-call(bf16[144,384]{1,0:T(8,128)(2,1)} %collective-permute-done.x_ref, bf16[5,384,384]{2,1,0:T(8,128)(2,1)S(1)} %bitcast.23), custom_call_target="tpu_custom_call" | custom-call | flops 188743680 | bytes 1048576 | tf_op jit(solution)/shard_map/pallas_call | solution.py:23
  61.3 4.4 %collective-permute-start.1 = (bf16[128,384]{1,0:T(8,128)(2,1)}, bf16[128,384]{1,0:T(8,128)(2,1)}, u32[]{:S(2)}, u32[]{:S(2)}) collective-permute-start(bf16[128,384]{1,0:T(8,128)(2,1)} %shard_map.83), channel_id=1, source_target_pairs={{0,12},{4,0},{8,4},{12,8},{1,13},{5,1},{9,5},{13,9},{2,14},{6,2},{... | collective-permute-start | bytes 294920 | tf_op jit(solution)/shard_map/ppermute | solution.py:35
  65.6 0.0 collective-permute-done.2.x_ref
  65.6 2.0 %shard_map.84 = bf16[128,384]{1,0:T(8,128)(2,1)} custom-call(bf16[144,384]{1,0:T(8,128)(2,1)} %collective-permute-done.2.x_ref, bf16[5,384,384]{2,1,0:T(8,128)(2,1)S(1)} %bitcast.24), custom_call_target="tpu_custom_call" | custom-call | flops 188743680 | bytes 1048576 | tf_op jit(solution)/shard_map/pallas_call | solution.py:23
  67.7 5.9 %collective-permute-start.3 = (bf16[128,384]{1,0:T(8,128)(2,1)}, bf16[128,384]{1,0:T(8,128)(2,1)}, u32[]{:S(2)}, u32[]{:S(2)}) collective-permute-start(bf16[128,384]{1,0:T(8,128)(2,1)} %shard_map.84), channel_id=1, source_target_pairs={{0,8},{4,12},{8,0},{12,4},{1,9},{5,13},{9,1},{13,5},{2,10},{6,14},... | collective-permute-start | bytes 294920 | tf_op jit(solution)/shard_map/ppermute | solution.py:35
  73.6 0.0 collective-permute-done.4.x_ref
  73.6 2.0 %shard_map.85 = bf16[128,384]{1,0:T(8,128)(2,1)} custom-call(bf16[144,384]{1,0:T(8,128)(2,1)} %collective-permute-done.4.x_ref, bf16[5,384,384]{2,1,0:T(8,128)(2,1)S(1)} %bitcast.25), custom_call_target="tpu_custom_call" | custom-call | flops 188743680 | bytes 1048576 | tf_op jit(solution)/shard_map/pallas_call | solution.py:23
  75.5 2.0 %collective-permute-start.5 = (bf16[128,384]{1,0:T(8,128)(2,1)}, bf16[128,384]{1,0:T(8,128)(2,1)}, u32[]{:S(2)}, u32[]{:S(2)}) collective-permute-start(bf16[128,384]{1,0:T(8,128)(2,1)} %shard_map.85), channel_id=1, source_target_pairs={{0,4},{4,8},{8,12},{12,0},{1,5},{5,9},{9,13},{13,1},{2,6},{6,10},{... | collective-permute-start | bytes 294920 | tf_op jit(solution)/shard_map/ppermute | solution.py:35
  77.6 18.3 %all_gather.24.out_ref = bf16[1536,192]{1,0:T(8,128)(2,1)} all-gather(bf16[384,192]{1,0:T(8,128)(2,1)S(1)} %constant_dynamic-slice_fusion.1), channel_id=1, replica_groups=mesh['segment'=2,'win'=4,'mp'=4] {'win'}, dimensions={0}, use_global_device_ids=true | all-gather | bytes 737280 | tf_op jit(solution)/shard_map/all_gather | solution.py:132
  95.8 0.8 dynamic_slice.39
  96.7 0.5 shard_map.82
  97.1 0.0 copy-start.2
  97.1 0.0 collective-permute-done.1
  97.2 0.0 collective-permute-done.3
  97.2 0.0 collective-permute-done.5
  97.2 0.0 copy-done.5
  97.2 1.2 fusion.8
  98.4 10.7 %all-gather = bf16[1024,384]{1,0:T(8,128)(2,1)S(1)} all-gather(bf16[128,384]{1,0:T(8,128)(2,1)S(1)} %fusion.8), channel_id=2, replica_groups=mesh['segment'=2,'win'=4,'mp'=4] {'segment','mp'}, dimensions={0}, use_global_device_ids=true | all-gather | bytes 884736 | tf_op jit(solution)/shard_map/all_gather | solution.py:170
  109.1 2.2 %shard_map.86 = bf16[8,128,384]{2,1,0:T(8,128)(2,1)} custom-call(bf16[8,128,384]{2,1,0:T(8,128)(2,1)S(1)} %bitcast.27, bf16[1536,320]{1,0:T(8,128)(2,1)S(1)} %all_gather.23.qkv_ref, bf16[1536,192]{1,0:T(8,128)(2,1)S(1)} %copy-done.2), custom_call_target="tpu_custom_call" | custom-call | bytes 1048576 | tf_op jit(solution)/shard_map/pallas_call | solution.py:23
  111.3 3.7 %all-to-all-start = ((bf16[8,128,384]{2,1,0:T(8,128)(2,1)}), bf16[8,128,384]{2,1,0:T(8,128)(2,1)S(1)}, u32[]{:S(2)}, u32[]{:S(2)}) async-start(bf16[8,128,384]{2,1,0:T(8,128)(2,1)} %shard_map.86), calls=%async_computation | async-start | bytes 1572864 | tf_op jit(solution)/shard_map/all_to_all | solution.py:179
  115.0 0.0 copy-done.7
  115.0 0.1 fusion.9
  115.1 0.2 convert_reduce_fusion.1
  115.4 11.2 %all-to-all-done = bf16[8,128,384]{2,1,0:T(8,128)(2,1)S(1)} async-done(((bf16[8,128,384]{2,1,0:T(8,128)(2,1)}), bf16[8,128,384]{2,1,0:T(8,128)(2,1)S(1)}, u32[]{:S(2)}, u32[]{:S(2)}) %all-to-all-start) | async-done | bytes 786464 | tf_op jit(solution)/shard_map/all_to_all | solution.py:179
  126.6 0.1 convert_reduce_fusion
  126.7 10.4 %all-gather.1 = bf16[1024,384]{1,0:T(8,128)(2,1)S(1)} all-gather(bf16[128,384]{1,0:T(8,128)(2,1)S(1)} %add_convert_fusion), channel_id=3, replica_groups=mesh['segment'=2,'win'=4,'mp'=4] {'segment','mp'}, dimensions={0}, use_global_device_ids=true | all-gather | bytes 884736 | tf_op jit(solution)/shard_map/all_gather | solution.py:181
  137.1 1.4 copy-done.3
  138.5 1.0 shard_map.87
  139.4 10.1 %all_to_all.10 = bf16[8,8,512]{2,1,0:T(8,128)(2,1)S(1)} all-to-all(bf16[8,8,512]{2,1,0:T(8,128)(2,1)S(1)} %bitcast.29), channel_id=1, replica_groups=mesh['segment'=2,'win'=4,'mp'=4] {'segment','win'}, dimensions={0} | all-to-all | bytes 131072 | tf_op jit(solution)/shard_map/all_to_all | solution.py:192
  149.6 0.6 log1p.9
  (11 shorter events, 0.1 us)
Async XLA Ops:
  6.5 9.5 %copy-start = (bf16[384,1024]{1,0:T(8,128)(2,1)S(1)}, bf16[384,1024]{1,0:T(8,128)(2,1)}, u32[]{:S(2)}) copy-start(bf16[384,1024]{1,0:T(8,128)(2,1)} %param.13) | copy-start | bytes 2359300
  6.5 130.5 %all-gather.4.cloned.1.call-start = ((), (), s32[]{:S(2)}) async-start(), calls=%async_computation.2 | async-start | bytes 1966080 | tf_op jit(solution)/shard_map/all_gather | solution.py:133
  8.0 8.0 %copy-start.4 = (bf16[1,1536,256]{1,2,0:T(8,128)(2,1)}, bf16[1,1536,256]{1,2,0:T(8,128)(2,1)S(1)}, u32[]{:S(2)}) copy-start(bf16[1,1536,256]{1,2,0:T(8,128)(2,1)S(1)} %copy.10) | copy-start | bytes 2359300
  8.0 8.8 %copy-start.6 = (bf16[384,640]{1,0:T(8,128)(2,1)S(1)}, bf16[384,640]{1,0:T(8,128)(2,1)}, u32[]{:S(2)}) copy-start(bf16[384,640]{1,0:T(8,128)(2,1)} %param.11) | copy-start | bytes 1474564
  9.1 50.2 %collective-permute-start = (bf16[144,384]{1,0:T(8,128)(2,1)}, bf16[144,384]{1,0:T(8,128)(2,1)}, u32[]{:S(2)}, u32[]{:S(2)}) collective-permute-start(bf16[144,384]{1,0:T(8,128)(2,1)} %get-tuple-element.5), channel_id=1, source_target_pairs={{0,4},{4,8},{8,12},{12,0},{1,5},{5,9},{9,13},{13,1},{2,6},{6,10},{... | collective-permute-start | bytes 331784 | tf_op jit(solution)/shard_map/ppermute | solution.py:35
  12.1 53.6 %collective-permute-start.2 = (bf16[144,384]{1,0:T(8,128)(2,1)}, bf16[144,384]{1,0:T(8,128)(2,1)}, u32[]{:S(2)}, u32[]{:S(2)}) collective-permute-start(bf16[144,384]{1,0:T(8,128)(2,1)} %get-tuple-element.7), channel_id=1, source_target_pairs={{0,8},{4,12},{8,0},{12,4},{1,9},{5,13},{9,1},{13,5},{2,10},{6,14},... | collective-permute-start | bytes 331784 | tf_op jit(solution)/shard_map/ppermute | solution.py:35
  14.7 58.9 %collective-permute-start.4 = (bf16[144,384]{1,0:T(8,128)(2,1)}, bf16[144,384]{1,0:T(8,128)(2,1)}, u32[]{:S(2)}, u32[]{:S(2)}) collective-permute-start(bf16[144,384]{1,0:T(8,128)(2,1)} %get-tuple-element.6), channel_id=1, source_target_pairs={{0,12},{4,0},{8,4},{12,8},{1,13},{5,1},{9,5},{13,9},{2,14},{6,2},{... | collective-permute-start | bytes 331784 | tf_op jit(solution)/shard_map/ppermute | solution.py:35
  16.8 42.5 %copy-start.1 = (bf16[384,5,384]{2,0,1:T(8,128)(2,1)S(1)}, bf16[384,5,384]{2,0,1:T(8,128)(2,1)}, u32[]{:S(2)}) copy-start(bf16[384,5,384]{2,0,1:T(8,128)(2,1)} %param.9) | copy-start | bytes 4423684
  61.3 35.9 %collective-permute-start.1 = (bf16[128,384]{1,0:T(8,128)(2,1)}, bf16[128,384]{1,0:T(8,128)(2,1)}, u32[]{:S(2)}, u32[]{:S(2)}) collective-permute-start(bf16[128,384]{1,0:T(8,128)(2,1)} %shard_map.83), channel_id=1, source_target_pairs={{0,12},{4,0},{8,4},{12,8},{1,13},{5,1},{9,5},{13,9},{2,14},{6,2},{... | collective-permute-start | bytes 294920 | tf_op jit(solution)/shard_map/ppermute | solution.py:35
  67.7 29.5 %collective-permute-start.3 = (bf16[128,384]{1,0:T(8,128)(2,1)}, bf16[128,384]{1,0:T(8,128)(2,1)}, u32[]{:S(2)}, u32[]{:S(2)}) collective-permute-start(bf16[128,384]{1,0:T(8,128)(2,1)} %shard_map.84), channel_id=1, source_target_pairs={{0,8},{4,12},{8,0},{12,4},{1,9},{5,13},{9,1},{13,5},{2,10},{6,14},... | collective-permute-start | bytes 294920 | tf_op jit(solution)/shard_map/ppermute | solution.py:35
  75.5 21.6 %collective-permute-start.5 = (bf16[128,384]{1,0:T(8,128)(2,1)}, bf16[128,384]{1,0:T(8,128)(2,1)}, u32[]{:S(2)}, u32[]{:S(2)}) collective-permute-start(bf16[128,384]{1,0:T(8,128)(2,1)} %shard_map.85), channel_id=1, source_target_pairs={{0,4},{4,8},{8,12},{12,0},{1,5},{5,9},{9,13},{13,1},{2,6},{6,10},{... | collective-permute-start | bytes 294920 | tf_op jit(solution)/shard_map/ppermute | solution.py:35
  95.8 1.3 copy-start.5
  97.1 12.0 %copy-start.2 = (bf16[1536,192]{1,0:T(8,128)(2,1)S(1)}, bf16[1536,192]{1,0:T(8,128)(2,1)}, u32[]{:S(2)}) copy-start(bf16[1536,192]{1,0:T(8,128)(2,1)} %all_gather.24.out_ref) | copy-start | bytes 1769476
  111.3 3.7 %copy-start.7 = (s32[3,1,8,8]{3,2,1,0:T(8,128)S(1)}, s32[3,1,8,8]{3,2,1,0:T(8,128)}, u32[]{:S(2)}) copy-start(s32[3,1,8,8]{3,2,1,0:T(8,128)} %param.15) | copy-start | bytes 2308
  111.3 15.3 %all-to-all-start = ((bf16[8,128,384]{2,1,0:T(8,128)(2,1)}), bf16[8,128,384]{2,1,0:T(8,128)(2,1)S(1)}, u32[]{:S(2)}, u32[]{:S(2)}) async-start(bf16[8,128,384]{2,1,0:T(8,128)(2,1)} %shard_map.86), calls=%async_computation | async-start | bytes 1572864 | tf_op jit(solution)/shard_map/all_to_all | solution.py:179
  137.1 1.4 copy-start.3
Sparse Core Ops, SparseCore 0:
  17.0 52.1 all-gather.3

commit v2 on v1

--- a/solution.py
+++ b/solution.py
@@ -20,10 +20,11 @@
 
 def call_kernel(body, out_shape, *operands, flops=0):
     whole = pl.BlockSpec(memory_space=pltpu.VMEM)
+    scalars = pl.BlockSpec(memory_space=pltpu.SMEM)
     return pl.pallas_call(
         body,
         out_shape=out_shape,
-        in_specs=[whole] * len(operands),
+        in_specs=[scalars if x.dtype == jnp.int32 else whole for x in operands],
         out_specs=whole,
         compiler_params=pltpu.CompilerParams(vmem_limit_bytes=VMEM_BYTES),
         cost_estimate=pl.CostEstimate(flops=flops, bytes_accessed=1 << 20, transcendentals=0),
@@ -47,47 +48,63 @@
     o_ref[...] = total.astype(o_ref.dtype)
 
 
-def joined_bins(blocks_ref, segments):
-    models = blocks_ref.shape[0] // segments
-    rows = [
-        jnp.concatenate([blocks_ref[s * models + m] for m in range(models)], axis=1)
-        for s in range(segments)
-    ]
-    return jnp.concatenate(rows, axis=0)
-
-
-def attention_kernel(segments, x_ref, qkv_ref, out_ref, o_ref):
-    x = joined_bins(x_ref, segments)
+def block_of(win_ref, by, windows):
+    return lax.rem(win_ref[0] + windows - by, windows)
+
+
+def contract_blocks(x_ref, segments, win_ref, pieces, cols):
+    models = x_ref.shape[0] // segments
+    total = None
+    for by, piece in enumerate(pieces):
+        if len(pieces) == 1:
+            rows = [
+                jnp.concatenate([x_ref[s * models + m] for m in range(models)], axis=1)
+                for s in range(segments)
+            ]
+        else:
+            block = block_of(win_ref, by, len(pieces))
+            rows = [x_ref[s * models + block] for s in range(segments)]
+        term = jnp.dot(jnp.concatenate(rows, axis=0), piece[:, cols], preferred_element_type=F32)
+        total = term if total is None else total + term
+    return total
+
+
+def attention_kernel(segments, heads, win_ref, x_ref, *refs):
+    *pieces, o_ref = refs
     models = o_ref.shape[0] // segments
-    bins, cols = o_ref.shape[1:]
-    total = None
-    for head in range(qkv_ref.shape[1] // SPAN):
-        rows = jnp.dot(
-            x, qkv_ref[:, head * SPAN : (head + 1) * SPAN], preferred_element_type=F32
-        ).astype(BF16)
-        query, key, value = rows[:, :KEY], rows[:, KEY : 2 * KEY], rows[:, 2 * KEY :]
+    bins = o_ref.shape[1]
+    width = o_ref.shape[2]
+    rows = contract_blocks(x_ref, segments, win_ref, pieces, slice(0, heads * SPAN)).astype(BF16)
+    outputs = []
+    for head in range(heads):
+        own = rows[:, head * SPAN : (head + 1) * SPAN]
+        query, key, value = own[:, :KEY], own[:, KEY : 2 * KEY], own[:, 2 * KEY :]
         scores = lax.dot_general(
             query, key, (((1,), (1,)), ((), ())), preferred_element_type=F32
         ) * (1.0 / math.sqrt(KEY))
         weights = jnp.exp(scores)
         probs = (weights / jnp.sum(weights, axis=1, keepdims=True)).astype(BF16)
-        att = jnp.dot(probs, value, preferred_element_type=F32).astype(BF16)
+        outputs.append(jnp.dot(probs, value, preferred_element_type=F32).astype(BF16))
+    att = jnp.concatenate(outputs, axis=1)
+    for by, piece in enumerate(pieces):
         term = lax.dot_general(
             att,
-            out_ref[:, head * VAL : (head + 1) * VAL],
+            piece[:, heads * SPAN :],
             (((1,), (1,)), ((), ())),
             preferred_element_type=F32,
-        )
-        total = term if total is None else total + term
-    total = total.astype(o_ref.dtype)
-    for s in range(segments):
-        for m in range(models):
-            o_ref[s * models + m] = total[s * bins : (s + 1) * bins, m * cols : (m + 1) * cols]
-
-
-def head_kernel(segments, x_ref, w_ref, b_ref, counts_ref, o_ref):
-    x = joined_bins(x_ref, segments)
-    logits = jnp.dot(x, w_ref[...], preferred_element_type=F32) + b_ref[...]
+        ).astype(o_ref.dtype)
+        for s in range(segments):
+            own = term[s * bins : (s + 1) * bins]
+            if len(pieces) > 1:
+                o_ref[s * models + block_of(win_ref, by, len(pieces))] = own
+            else:
+                for m in range(models):
+                    o_ref[s * models + m] = own[:, m * width : (m + 1) * width]
+
+
+def head_kernel(segments, win_ref, x_ref, b_ref, counts_ref, *refs):
+    *pieces, o_ref = refs
+    logits = contract_blocks(x_ref, segments, win_ref, pieces, slice(None)) + b_ref[...]
     tracks = jax.nn.softplus(logits).astype(BF16)
     sums = jnp.dot(counts_ref[...], tracks, preferred_element_type=F32)
     o_ref[...] = sums.astype(o_ref.dtype)
@@ -128,10 +145,21 @@
         size = x.shape[1] // segments
         return lax.dynamic_slice_in_dim(x, segment_index * size, size, 1)
 
-    qkv_full = lax.all_gather(part_of_segment(qkv_weight), "win", axis=0, tiled=True)
-    out_full = lax.all_gather(part_of_segment(out_weight), "win", axis=0, tiled=True)
-    head_full = lax.all_gather(part_of_segment(head_weight), "win", axis=0, tiled=True)
-    track_cols = head_full.shape[1]
+    attention_own = jnp.concatenate(
+        [part_of_segment(qkv_weight), part_of_segment(out_weight)], axis=1
+    )
+    head_own = part_of_segment(head_weight)
+    heads = qkv_weight.shape[1] // segments // SPAN
+    stepwise = windows <= 8 and row_count == out_cols
+
+    def gathered(own, after):
+        if not stepwise:
+            return [lax.all_gather(own, "win", axis=0, tiled=True)]
+        sent, _ = lax.optimization_barrier((own, after))
+        return [own] + [shifted(sent, "win", by) for by in range(1, windows)]
+
+    win_ref = win_index.astype(jnp.int32)[None]
+    track_cols = head_own.shape[1]
     bias_part = lax.dynamic_slice_in_dim(head_bias, segment_index * track_cols, track_cols, 0)
     counts = gene_counts(exon_lists[:, 0], bin_count)
 
@@ -151,30 +179,33 @@
             flops=2 * bins * out_cols * row_count * tap_count,
         )
 
-    if windows <= 8:
+    if stepwise:
         arrived = [
             shifted(rows_for(lax.rem(win_index + by, windows)), "win", by)
             for by in range(1, windows)
         ]
+        attention_pieces = gathered(attention_own, arrived)
         conv_pre = conv_of(rows_for(win_index), F32)
         for by, x in enumerate(arrived, 1):
             conv_pre = conv_pre + shifted(conv_of(x, BF16), "win", -by).astype(F32)
     else:
         blocks = own_bins.reshape(own_bins.shape[0], windows, row_count).transpose(1, 0, 2)
         arrived = lax.all_to_all(blocks, "win", 0, 0, tiled=True)
+        attention_pieces = gathered(attention_own, None)
         partial = jnp.stack([conv_of(arrived[w], BF16) for w in range(windows)])
         conv_pre = lax.all_to_all(partial, "win", 0, 0, tiled=True).astype(F32).sum(axis=0)
 
     own_feats = lax.dynamic_slice(own_bins, (reach, model_index * out_cols), (bins, out_cols))
     conv_out = (own_feats + jax.nn.gelu(conv_pre + conv_bias)).astype(BF16)
+    head_pieces = gathered(head_own, conv_out)
     all_chan = lax.all_gather(conv_out, plane, axis=0)
 
     partial = call_kernel(
-        functools.partial(attention_kernel, segments),
+        functools.partial(attention_kernel, segments, heads),
         jax.ShapeDtypeStruct(all_chan.shape, BF16),
+        win_ref,
         all_chan,
-        qkv_full,
-        out_full,
+        *attention_pieces,
     )
     summed = lax.all_to_all(partial, plane, 0, 0, tiled=True).astype(F32).sum(axis=0)
     resid = (conv_out.astype(F32) + summed).astype(BF16)
@@ -183,10 +214,11 @@
     sums = call_kernel(
         functools.partial(head_kernel, segments),
         jax.ShapeDtypeStruct((counts.shape[0], track_cols), BF16),
+        win_ref,
         all_resid,
-        head_full,
         bias_part[None, :],
         counts,
+        *head_pieces,
     )
     owners = segments * windows
     got = lax.all_to_all(

time: 158 us -> 117 us (0.74)
  blocking collectives: 90.6 us -> 37.8 us
  waiting for transfers between devices: 11.2 us -> 33.9 us
  between operations: 13.6 us -> 0.18 us
  starting transfers between devices: 22.9 us -> 34 us
  Pallas kernels: 9.6 us -> 5.4 us
  local copies, waits for them, and re-layouts: 7.42 us -> 4.65 us
    all_gather x2 -> x0, blocking collectives: 59.4 us -> none  [the longest x1 41.2 us: local(): lax.all_gather(part_of_segment(qkv_weight), 'win', axis=0, tiled=True)]
    ppermute x6 -> x12, waiting for transfers between devices: 0.02 us -> 33.1 us  [shifted(): return lax.ppermute(x, axis, [(i, (i + by) % size) for i in range(size)])]
    ppermute x6 -> x12, starting transfers between devices: 19.3 us -> 30.4 us  [shifted(): return lax.ppermute(x, axis, [(i, (i + by) % size) for i in range(size)])]
    all_to_all x1, waiting for transfers between devices: 11.2 us -> 0.79 us  [local(): lax.all_to_all(partial, plane, 0, 0, tiled=True).astype(F32).sum(axis=0)]
    all_to_all x1, blocking collectives: 10.1 us -> 17 us  [local(): lax.all_to_all(sums.reshape(owners, GENE_DEV, track_cols), ('segment', 'w...]
    pallas_call x6, Pallas kernels: 9.6 us -> 5.4 us  [call_kernel(): pl.pallas_call(body, out_shape=out_shape, in_specs=[scalars if x.dtype ==...]
  transfers between devices with their start and end apart: 8 -> 13, of which waited for: 1 -> 6; matrix products, arithmetic and copies ran while one was open for 3% -> 2% of each run, Pallas kernels for 5% -> 2%
where the time goes in v2:
time: 117 us
  blocking collectives  37.8 us (32%)
  starting transfers between devices  34 us (29%)
  waiting for transfers between devices  33.9 us (29%)
  Pallas kernels  5.4 us (5%)
  local copies, waits for them, and re-layouts  4.65 us (4%)
    ppermute x12, waiting for transfers between devices, shifted(): return lax.ppermute(x, axis, [(i, (i + by) % size) for i in range(size)])  33.1 us
    ppermute x12, starting transfers between devices, shifted(): return lax.ppermute(x, axis, [(i, (i + by) % size) for i in range(size)])  30.4 us
    all_to_all x1, blocking collectives, local(): lax.all_to_all(sums.reshape(owners, GENE_DEV, track_cols), ('segment', 'w...  17 us
    all_gather x1, blocking collectives, local(): all_chan = lax.all_gather(conv_out, plane, axis=0)  10.4 us
    all_gather x1, blocking collectives, local(): all_resid = lax.all_gather(resid, plane, axis=0)  10.4 us
    pallas_call x6, Pallas kernels, call_kernel(): pl.pallas_call(body, out_shape=out_shape, in_specs=[scalars if x.dtype ==...  5.4 us
    all_to_all x1, starting transfers between devices, local(): lax.all_to_all(partial, plane, 0, 0, tiled=True).astype(F32).sum(axis=0)  3.55 us
  transfers between devices with their start and end apart: 13, of which 6 were waited for; matrix products, arithmetic and copies ran while one was open for 2% of the time, Pallas kernels for 2%

profile of v2, /device:TPU:0, one launch (start us, length us, event | category | flops | bytes accessed | tf_op | source)
XLA Modules:
  0.0 116.7 jit_solution(2524282982894247944)
XLA Ops:
  0.0 1.6 %copy.10 = bf16[1,1536,256]{1,2,0:T(8,128)(2,1)S(1)} copy(bf16[1,1536,256]{2,1,0:T(8,128)(2,1)} %param.8) | data formatting | bytes 1572864 | tf_op args[0]
  1.6 1.0 pad_dynamic-slice_fusion.2
  2.6 0.0 copy-done.2
  2.6 3.1 %collective-permute-start = (bf16[144,384]{1,0:T(8,128)(2,1)}, bf16[144,384]{1,0:T(8,128)(2,1)S(1)}, u32[]{:S(2)}, u32[]{:S(2)}) collective-permute-start(bf16[144,384]{1,0:T(8,128)(2,1)} %get-tuple-element.9), channel_id=1, source_target_pairs={{0,4},{4,8},{8,12},{12,0},{1,5},{5,9},{9,13},{13,1},{2,6},{6,10},{... | collective-permute-start | bytes 331784 | tf_op jit(solution)/shard_map/ppermute | solution.py:36
  5.7 2.6 %collective-permute-start.2 = (bf16[144,384]{1,0:T(8,128)(2,1)}, bf16[144,384]{1,0:T(8,128)(2,1)S(1)}, u32[]{:S(2)}, u32[]{:S(2)}) collective-permute-start(bf16[144,384]{1,0:T(8,128)(2,1)} %get-tuple-element.11), channel_id=1, source_target_pairs={{0,8},{4,12},{8,0},{12,4},{1,9},{5,13},{9,1},{13,5},{2,10},{6,14},... | collective-permute-start | bytes 331784 | tf_op jit(solution)/shard_map/ppermute | solution.py:36
  8.3 1.3 %collective-permute-start.4 = (bf16[144,384]{1,0:T(8,128)(2,1)}, bf16[144,384]{1,0:T(8,128)(2,1)S(1)}, u32[]{:S(2)}, u32[]{:S(2)}) collective-permute-start(bf16[144,384]{1,0:T(8,128)(2,1)} %get-tuple-element.10), channel_id=1, source_target_pairs={{0,12},{4,0},{8,4},{12,8},{1,13},{5,1},{9,5},{13,9},{2,14},{6,2},{... | collective-permute-start | bytes 331784 | tf_op jit(solution)/shard_map/ppermute | solution.py:36
  9.6 1.2 constant_dynamic-slice_fusion.2
  10.8 0.5 shard_map.82
  11.3 0.1 dynamic_slice.38
  11.4 0.1 constant_dynamic-slice_fusion.1
  11.5 0.4 collective-permute-done.x_ref
  11.9 0.5 shard_map.83
  12.4 1.4 %collective-permute-start.1 = (bf16[128,384]{1,0:T(8,128)(2,1)S(1)}, bf16[128,384]{1,0:T(8,128)(2,1)S(1)}, u32[]{:S(2)}, u32[]{:S(2)}) collective-permute-start(bf16[128,384]{1,0:T(8,128)(2,1)S(1)} %shard_map.83), channel_id=1, source_target_pairs={{0,12},{4,0},{8,4},{12,8},{1,13},{5,1},{9,5},{13,9},{2,14},{6,2},{... | collective-permute-start | bytes 294920 | tf_op jit(solution)/shard_map/ppermute | solution.py:36
  13.8 2.0 %collective-permute-done.2.x_ref = bf16[144,384]{1,0:T(8,128)(2,1)S(1)} collective-permute-done((bf16[144,384]{1,0:T(8,128)(2,1)}, bf16[144,384]{1,0:T(8,128)(2,1)S(1)}, u32[]{:S(2)}, u32[]{:S(2)}) %collective-permute-start.2) | collective-permute-done | bytes 110624 | tf_op jit(solution)/shard_map/ppermute | solution.py:36
  15.9 0.5 shard_map.84
  16.4 0.0 copy-start.6
  16.4 4.4 %collective-permute-start.3 = (bf16[128,384]{1,0:T(8,128)(2,1)S(1)}, bf16[128,384]{1,0:T(8,128)(2,1)S(1)}, u32[]{:S(2)}, u32[]{:S(2)}) collective-permute-start(bf16[128,384]{1,0:T(8,128)(2,1)S(1)} %shard_map.84), channel_id=1, source_target_pairs={{0,8},{4,12},{8,0},{12,4},{1,9},{5,13},{9,1},{13,5},{2,10},{6,14},... | collective-permute-start | bytes 294920 | tf_op jit(solution)/shard_map/ppermute | solution.py:36
  20.8 0.0 collective-permute-done.4.x_ref
  20.8 0.5 shard_map.85
  21.3 3.3 %collective-permute-start.5 = (bf16[128,384]{1,0:T(8,128)(2,1)S(1)}, bf16[128,384]{1,0:T(8,128)(2,1)S(1)}, u32[]{:S(2)}, u32[]{:S(2)}) collective-permute-start(bf16[128,384]{1,0:T(8,128)(2,1)S(1)} %shard_map.85), channel_id=1, source_target_pairs={{0,4},{4,8},{8,12},{12,0},{1,5},{5,9},{9,13},{13,1},{2,6},{6,10},{... | collective-permute-start | bytes 294920 | tf_op jit(solution)/shard_map/ppermute | solution.py:36
  24.5 0.1 pad_maximum_fusion.refs_0_
  24.7 0.1 collective-permute-start.6
  24.7 1.2 %collective-permute-start.7 = (bf16[384,512]{1,0:T(8,128)(2,1)S(1)}, bf16[384,512]{1,0:T(8,128)(2,1)S(1)}, u32[]{:S(2)}, u32[]{:S(2)}) collective-permute-start(bf16[384,512]{1,0:T(8,128)(2,1)S(1)} %pad_maximum_fusion.refs_0_), channel_id=1, source_target_pairs={{0,8},{4,12},{8,0},{12,4},{1,9},{5,13},{9,1},{13,5},{2,10},{6,14},... | collective-permute-start | bytes 1179656 | tf_op jit(solution)/shard_map/ppermute | solution.py:36
  25.9 0.0 collective-permute-done.1
  25.9 2.6 %collective-permute-start.8 = (bf16[384,512]{1,0:T(8,128)(2,1)S(1)}, bf16[384,512]{1,0:T(8,128)(2,1)S(1)}, u32[]{:S(2)}, u32[]{:S(2)}) collective-permute-start(bf16[384,512]{1,0:T(8,128)(2,1)S(1)} %pad_maximum_fusion.refs_0_), channel_id=1, source_target_pairs={{0,12},{4,0},{8,4},{12,8},{1,13},{5,1},{9,5},{13,9},{2,14},{6,2},{... | collective-permute-start | bytes 1179656 | tf_op jit(solution)/shard_map/ppermute | solution.py:36
  28.5 15.5 %collective-permute-done.3 = bf16[128,384]{1,0:T(8,128)(2,1)S(1)} collective-permute-done((bf16[128,384]{1,0:T(8,128)(2,1)S(1)}, bf16[128,384]{1,0:T(8,128)(2,1)S(1)}, u32[]{:S(2)}, u32[]{:S(2)}) %collective-permute-start.3) | collective-permute-done | bytes 98336 | tf_op jit(solution)/shard_map/ppermute | solution.py:36
  44.0 0.0 collective-permute-done.5
  44.0 0.2 fusion.8
  44.2 10.4 %all-gather = bf16[1024,384]{1,0:T(8,128)(2,1)S(1)} all-gather(bf16[128,384]{1,0:T(8,128)(2,1)S(1)} %fusion.8), channel_id=2, replica_groups=mesh['segment'=2,'win'=4,'mp'=4] {'segment','mp'}, dimensions={0}, use_global_device_ids=true | all-gather | bytes 884736 | tf_op jit(solution)/shard_map/all_gather | solution.py:201
  54.6 0.0 collective-permute-done.6.refs_1_
  54.6 0.0 collective-permute-done.7.refs_2_
  54.6 0.0 collective-permute-done.8.refs_3_
  54.6 2.5 %shard_map.86 = bf16[8,128,384]{2,1,0:T(8,128)(2,1)} custom-call(s32[1]{0:T(128)} %bitcast.win_ref, bf16[8,128,384]{2,1,0:T(8,128)(2,1)S(1)} %bitcast.29, bf16[384,512]{1,0:T(8,128)(2,1)S(1)} %pad_maximum_fusion.refs_0_, bf16[384,512]{1,0:T(8,128)(2,1)S(1)} %collective-permute-done.6.refs_1_, bf16[384,512]{1,0:T(8,128)(2,1)S(1)} %collective-permute-done.7.refs_2_, ...), custom_call_target="tpu_custom_call" | custom-call | bytes 1048576 | tf_op jit(solution)/shard_map/pallas_call | solution.py:24
  57.1 3.5 %all-to-all-start = ((bf16[8,128,384]{2,1,0:T(8,128)(2,1)}), bf16[8,128,384]{2,1,0:T(8,128)(2,1)S(1)}, u32[]{:S(2)}, u32[]{:S(2)}) async-start(bf16[8,128,384]{2,1,0:T(8,128)(2,1)} %shard_map.86), calls=%async_computation | async-start | bytes 1572864 | tf_op jit(solution)/shard_map/all_to_all | solution.py:210
  60.7 0.1 fusion.9
  60.8 0.2 convert_reduce_fusion.1
  61.1 7.0 %collective-permute-start.10 = (bf16[384,512]{1,0:T(8,128)(2,1)S(1)}, bf16[384,512]{1,0:T(8,128)(2,1)S(1)}, u32[]{:S(2)}, u32[]{:S(2)}) collective-permute-start(bf16[384,512]{1,0:T(8,128)(2,1)S(1)} %constant_dynamic-slice_fusion.refs_0_), channel_id=1, source_target_pairs={{0,8},{4,12},{8,0},{12,4},{1,9},{5,13},{9,1},{13,5},{2,10},{6,14},... | collective-permute-start | bytes 1179656 | tf_op jit(solution)/shard_map/ppermute | solution.py:36
  68.1 3.4 %collective-permute-start.11 = (bf16[384,512]{1,0:T(8,128)(2,1)S(1)}, bf16[384,512]{1,0:T(8,128)(2,1)S(1)}, u32[]{:S(2)}, u32[]{:S(2)}) collective-permute-start(bf16[384,512]{1,0:T(8,128)(2,1)S(1)} %constant_dynamic-slice_fusion.refs_0_), channel_id=1, source_target_pairs={{0,12},{4,0},{8,4},{12,8},{1,13},{5,1},{9,5},{13,9},{2,14},{6,2},{... | collective-permute-start | bytes 1179656 | tf_op jit(solution)/shard_map/ppermute | solution.py:36
  71.4 0.0 collective-permute-start.9
  71.4 0.8 all-to-all-done
  72.2 0.1 convert_reduce_fusion
  72.4 10.4 %all-gather.1 = bf16[1024,384]{1,0:T(8,128)(2,1)S(1)} all-gather(bf16[128,384]{1,0:T(8,128)(2,1)S(1)} %add_convert_fusion), channel_id=3, replica_groups=mesh['segment'=2,'win'=4,'mp'=4] {'segment','mp'}, dimensions={0}, use_global_device_ids=true | all-gather | bytes 884736 | tf_op jit(solution)/shard_map/all_gather | solution.py:212
  82.8 3.7 %collective-permute-done.10.refs_2_ = bf16[384,512]{1,0:T(8,128)(2,1)S(1)} collective-permute-done((bf16[384,512]{1,0:T(8,128)(2,1)S(1)}, bf16[384,512]{1,0:T(8,128)(2,1)S(1)}, u32[]{:S(2)}, u32[]{:S(2)}) %collective-permute-start.10) | collective-permute-done | bytes 393248 | tf_op jit(solution)/shard_map/ppermute | solution.py:36
  86.5 0.0 collective-permute-done.11.refs_3_
  86.5 11.5 %collective-permute-done.9.refs_1_ = bf16[384,512]{1,0:T(8,128)(2,1)S(1)} collective-permute-done((bf16[384,512]{1,0:T(8,128)(2,1)S(1)}, bf16[384,512]{1,0:T(8,128)(2,1)S(1)}, u32[]{:S(2)}, u32[]{:S(2)}) %collective-permute-start.9) | collective-permute-done | bytes 393248 | tf_op jit(solution)/shard_map/ppermute | solution.py:36
  97.9 1.1 shard_map.87
  99.0 17.0 %all_to_all.10 = bf16[8,8,512]{2,1,0:T(8,128)(2,1)S(1)} all-to-all(bf16[8,8,512]{2,1,0:T(8,128)(2,1)S(1)} %bitcast.30), channel_id=1, replica_groups=mesh['segment'=2,'win'=4,'mp'=4] {'segment','win'}, dimensions={0} | all-to-all | bytes 131072 | tf_op jit(solution)/shard_map/all_to_all | solution.py:224
  116.1 0.6 log1p.9
  (19 shorter events, 0.1 us)
Async XLA Ops:
  0.0 60.7 %copy-start = (bf16[384,1024]{1,0:T(8,128)(2,1)S(1)}, bf16[384,1024]{1,0:T(8,128)(2,1)}, u32[]{:S(2)}) copy-start(bf16[384,1024]{1,0:T(8,128)(2,1)} %param.13) | copy-start | bytes 2359300
  0.0 9.6 %copy-start.5 = (s32[3,1,8,8]{3,2,1,0:T(8,128)S(1)}, s32[3,1,8,8]{3,2,1,0:T(8,128)}, u32[]{:S(2)}) copy-start(s32[3,1,8,8]{3,2,1,0:T(8,128)} %param.15) | copy-start | bytes 2308
  0.0 10.8 %copy-start.1 = (bf16[384,5,384]{2,0,1:T(8,128)(2,1)S(1)}, bf16[384,5,384]{2,0,1:T(8,128)(2,1)}, u32[]{:S(2)}) copy-start(bf16[384,5,384]{2,0,1:T(8,128)(2,1)} %param.9) | copy-start | bytes 4423684
  1.6 1.1 copy-start.2
  2.6 8.7 %copy-start.7 = (f32[1024]{0:T(1024)S(1)}, f32[1024]{0:T(1024)}, u32[]{:S(2)}) copy-start(f32[1024]{0:T(1024)} %param.14) | copy-start | bytes 12292
  2.6 8.8 %copy-start.4 = (bf16[384,384]{1,0:T(8,128)(2,1)S(1)}, bf16[384,384]{1,0:T(8,128)(2,1)}, u32[]{:S(2)}) copy-start(bf16[384,384]{1,0:T(8,128)(2,1)} %param.12) | copy-start | bytes 884740
  2.6 9.3 %collective-permute-start = (bf16[144,384]{1,0:T(8,128)(2,1)}, bf16[144,384]{1,0:T(8,128)(2,1)S(1)}, u32[]{:S(2)}, u32[]{:S(2)}) collective-permute-start(bf16[144,384]{1,0:T(8,128)(2,1)} %get-tuple-element.9), channel_id=1, source_target_pairs={{0,4},{4,8},{8,12},{12,0},{1,5},{5,9},{9,13},{13,1},{2,6},{6,10},{... | collective-permute-start | bytes 331784 | tf_op jit(solution)/shard_map/ppermute | solution.py:36
  5.7 10.2 %collective-permute-start.2 = (bf16[144,384]{1,0:T(8,128)(2,1)}, bf16[144,384]{1,0:T(8,128)(2,1)S(1)}, u32[]{:S(2)}, u32[]{:S(2)}) collective-permute-start(bf16[144,384]{1,0:T(8,128)(2,1)} %get-tuple-element.11), channel_id=1, source_target_pairs={{0,8},{4,12},{8,0},{12,4},{1,9},{5,13},{9,1},{13,5},{2,10},{6,14},... | collective-permute-start | bytes 331784 | tf_op jit(solution)/shard_map/ppermute | solution.py:36
  8.3 12.5 %collective-permute-start.4 = (bf16[144,384]{1,0:T(8,128)(2,1)}, bf16[144,384]{1,0:T(8,128)(2,1)S(1)}, u32[]{:S(2)}, u32[]{:S(2)}) collective-permute-start(bf16[144,384]{1,0:T(8,128)(2,1)} %get-tuple-element.10), channel_id=1, source_target_pairs={{0,12},{4,0},{8,4},{12,8},{1,13},{5,1},{9,5},{13,9},{2,14},{6,2},{... | collective-permute-start | bytes 331784 | tf_op jit(solution)/shard_map/ppermute | solution.py:36
  12.4 13.5 %collective-permute-start.1 = (bf16[128,384]{1,0:T(8,128)(2,1)S(1)}, bf16[128,384]{1,0:T(8,128)(2,1)S(1)}, u32[]{:S(2)}, u32[]{:S(2)}) collective-permute-start(bf16[128,384]{1,0:T(8,128)(2,1)S(1)} %shard_map.83), channel_id=1, source_target_pairs={{0,12},{4,0},{8,4},{12,8},{1,13},{5,1},{9,5},{13,9},{2,14},{6,2},{... | collective-permute-start | bytes 294920 | tf_op jit(solution)/shard_map/ppermute | solution.py:36
  16.3 27.7 %copy-start.3 = (bf16[1,1536,256]{1,2,0:T(8,128)(2,1)S(1)}, bf16[1,1536,256]{1,2,0:T(8,128)(2,1)}, u32[]{:S(2)}) copy-start(bf16[1,1536,256]{1,2,0:T(8,128)(2,1)} %copy-done.2) | copy-start | bytes 2359300
  16.4 27.7 %copy-start.6 = (f32[384]{0:T(512)S(1)}, f32[384]{0:T(512)}, u32[]{:S(2)}) copy-start(f32[384]{0:T(512)} %param.10) | copy-start | bytes 4612
  16.4 27.6 %collective-permute-start.3 = (bf16[128,384]{1,0:T(8,128)(2,1)S(1)}, bf16[128,384]{1,0:T(8,128)(2,1)S(1)}, u32[]{:S(2)}, u32[]{:S(2)}) collective-permute-start(bf16[128,384]{1,0:T(8,128)(2,1)S(1)} %shard_map.84), channel_id=1, source_target_pairs={{0,8},{4,12},{8,0},{12,4},{1,9},{5,13},{9,1},{13,5},{2,10},{6,14},... | collective-permute-start | bytes 294920 | tf_op jit(solution)/shard_map/ppermute | solution.py:36
  21.3 22.7 %collective-permute-start.5 = (bf16[128,384]{1,0:T(8,128)(2,1)S(1)}, bf16[128,384]{1,0:T(8,128)(2,1)S(1)}, u32[]{:S(2)}, u32[]{:S(2)}) collective-permute-start(bf16[128,384]{1,0:T(8,128)(2,1)S(1)} %shard_map.85), channel_id=1, source_target_pairs={{0,4},{4,8},{8,12},{12,0},{1,5},{5,9},{9,13},{13,1},{2,6},{6,10},{... | collective-permute-start | bytes 294920 | tf_op jit(solution)/shard_map/ppermute | solution.py:36
  24.7 30.0 %collective-permute-start.6 = (bf16[384,512]{1,0:T(8,128)(2,1)S(1)}, bf16[384,512]{1,0:T(8,128)(2,1)S(1)}, u32[]{:S(2)}, u32[]{:S(2)}) collective-permute-start(bf16[384,512]{1,0:T(8,128)(2,1)S(1)} %pad_maximum_fusion.refs_0_), channel_id=1, source_target_pairs={{0,4},{4,8},{8,12},{12,0},{1,5},{5,9},{9,13},{13,1},{2,6},{6,10},{... | collective-permute-start | bytes 1179656 | tf_op jit(solution)/shard_map/ppermute | solution.py:36
  24.7 29.9 %collective-permute-start.7 = (bf16[384,512]{1,0:T(8,128)(2,1)S(1)}, bf16[384,512]{1,0:T(8,128)(2,1)S(1)}, u32[]{:S(2)}, u32[]{:S(2)}) collective-permute-start(bf16[384,512]{1,0:T(8,128)(2,1)S(1)} %pad_maximum_fusion.refs_0_), channel_id=1, source_target_pairs={{0,8},{4,12},{8,0},{12,4},{1,9},{5,13},{9,1},{13,5},{2,10},{6,14},... | collective-permute-start | bytes 1179656 | tf_op jit(solution)/shard_map/ppermute | solution.py:36
  25.9 28.7 %collective-permute-start.8 = (bf16[384,512]{1,0:T(8,128)(2,1)S(1)}, bf16[384,512]{1,0:T(8,128)(2,1)S(1)}, u32[]{:S(2)}, u32[]{:S(2)}) collective-permute-start(bf16[384,512]{1,0:T(8,128)(2,1)S(1)} %pad_maximum_fusion.refs_0_), channel_id=1, source_target_pairs={{0,12},{4,0},{8,4},{12,8},{1,13},{5,1},{9,5},{13,9},{2,14},{6,2},{... | collective-permute-start | bytes 1179656 | tf_op jit(solution)/shard_map/ppermute | solution.py:36
  57.1 15.1 %all-to-all-start = ((bf16[8,128,384]{2,1,0:T(8,128)(2,1)}), bf16[8,128,384]{2,1,0:T(8,128)(2,1)S(1)}, u32[]{:S(2)}, u32[]{:S(2)}) async-start(bf16[8,128,384]{2,1,0:T(8,128)(2,1)} %shard_map.86), calls=%async_computation | async-start | bytes 1572864 | tf_op jit(solution)/shard_map/all_to_all | solution.py:210
  61.1 25.4 %collective-permute-start.10 = (bf16[384,512]{1,0:T(8,128)(2,1)S(1)}, bf16[384,512]{1,0:T(8,128)(2,1)S(1)}, u32[]{:S(2)}, u32[]{:S(2)}) collective-permute-start(bf16[384,512]{1,0:T(8,128)(2,1)S(1)} %constant_dynamic-slice_fusion.refs_0_), channel_id=1, source_target_pairs={{0,8},{4,12},{8,0},{12,4},{1,9},{5,13},{9,1},{13,5},{2,10},{6,14},... | collective-permute-start | bytes 1179656 | tf_op jit(solution)/shard_map/ppermute | solution.py:36
  68.1 18.4 %collective-permute-start.11 = (bf16[384,512]{1,0:T(8,128)(2,1)S(1)}, bf16[384,512]{1,0:T(8,128)(2,1)S(1)}, u32[]{:S(2)}, u32[]{:S(2)}) collective-permute-start(bf16[384,512]{1,0:T(8,128)(2,1)S(1)} %constant_dynamic-slice_fusion.refs_0_), channel_id=1, source_target_pairs={{0,12},{4,0},{8,4},{12,8},{1,13},{5,1},{9,5},{13,9},{2,14},{6,2},{... | collective-permute-start | bytes 1179656 | tf_op jit(solution)/shard_map/ppermute | solution.py:36
  71.4 26.5 %collective-permute-start.9 = (bf16[384,512]{1,0:T(8,128)(2,1)S(1)}, bf16[384,512]{1,0:T(8,128)(2,1)S(1)}, u32[]{:S(2)}, u32[]{:S(2)}) collective-permute-start(bf16[384,512]{1,0:T(8,128)(2,1)S(1)} %constant_dynamic-slice_fusion.refs_0_), channel_id=1, source_target_pairs={{0,4},{4,8},{8,12},{12,0},{1,5},{5,9},{9,13},{13,1},{2,6},{6,10},{... | collective-permute-start | bytes 1179656 | tf_op jit(solution)/shard_map/ppermute | solution.py:36

commit v3 on v2

--- a/solution.py
+++ b/solution.py
@@ -156,7 +156,12 @@
         if not stepwise:
             return [lax.all_gather(own, "win", axis=0, tiled=True)]
         sent, _ = lax.optimization_barrier((own, after))
-        return [own] + [shifted(sent, "win", by) for by in range(1, windows)]
+        if windows != 4:
+            return [own] + [shifted(sent, "win", by) for by in range(1, windows)]
+        below, above = shifted(sent, "win", 1), shifted(sent, "win", -1)
+        handed = jnp.where(win_index == 1, above, jnp.where(win_index == 2, below, sent))
+        across = lax.ppermute(handed, "win", [(0, 2), (1, 0), (2, 3), (3, 1)])
+        return [own, below, across, above]
 
     win_ref = win_index.astype(jnp.int32)[None]
     track_cols = head_own.shape[1]

time: 117 us -> 103 us (0.88)
  blocking collectives: 37.8 us -> 30.2 us
  waiting for transfers between devices: 33.9 us -> 28.3 us
  starting transfers between devices: 34 us -> 32.4 us
    ppermute x12 -> x10, waiting for transfers between devices: 33.1 us -> 20.4 us  [shifted(): return lax.ppermute(x, axis, [(i, (i + by) % size) for i in range(size)])]
    ppermute x12 -> x10, starting transfers between devices: 30.4 us -> 17.8 us  [shifted(): return lax.ppermute(x, axis, [(i, (i + by) % size) for i in range(size)])]
    ppermute x0 -> x2, starting transfers between devices: none -> 11 us  [gathered(): across = lax.ppermute(handed, 'win', [(0, 2), (1, 0), (2, 3), (3, 1)])]
    all_to_all x1, blocking collectives: 17 us -> 9.47 us  [local(): lax.all_to_all(sums.reshape(owners, GENE_DEV, track_cols), ('segment', 'w...]
    all_to_all x1, waiting for transfers between devices: 0.79 us -> 7.91 us  [local(): lax.all_to_all(partial, plane, 0, 0, tiled=True).astype(F32).sum(axis=0)]
  transfers between devices with their start and end apart: 13 -> 13, of which waited for: 6 -> 6; matrix products, arithmetic and copies ran while one was open for 2% -> 3% of each run, Pallas kernels for 2% -> 4%
where the time goes in v3:
time: 103 us
  starting transfers between devices  32.4 us (31%)
  blocking collectives  30.2 us (29%)
  waiting for transfers between devices  28.3 us (27%)
  Pallas kernels  5.38 us (5%)
  local copies, waits for them, and re-layouts  4.67 us (5%)
  other arithmetic  1.64 us (2%)
    ppermute x10, waiting for transfers between devices, shifted(): return lax.ppermute(x, axis, [(i, (i + by) % size) for i in range(size)])  20.4 us
    ppermute x10, starting transfers between devices, shifted(): return lax.ppermute(x, axis, [(i, (i + by) % size) for i in range(size)])  17.8 us
    ppermute x2, starting transfers between devices, gathered(): across = lax.ppermute(handed, 'win', [(0, 2), (1, 0), (2, 3), (3, 1)])  11 us
    all_gather x1, blocking collectives, local(): all_chan = lax.all_gather(conv_out, plane, axis=0)  10.4 us
    all_gather x1, blocking collectives, local(): all_resid = lax.all_gather(resid, plane, axis=0)  10.4 us
    all_to_all x1, blocking collectives, local(): lax.all_to_all(sums.reshape(owners, GENE_DEV, track_cols), ('segment', 'w...  9.47 us
    all_to_all x1, waiting for transfers between devices, local(): lax.all_to_all(partial, plane, 0, 0, tiled=True).astype(F32).sum(axis=0)  7.91 us
    pallas_call x6, Pallas kernels, call_kernel(): pl.pallas_call(body, out_shape=out_shape, in_specs=[scalars if x.dtype ==...  5.38 us
  transfers between devices with their start and end apart: 13, of which 6 were waited for; matrix products, arithmetic and copies ran while one was open for 3% of the time, Pallas kernels for 4%

profile of v3, /device:TPU:0, one launch (start us, length us, event | category | flops | bytes accessed | tf_op | source)
XLA Modules:
  0.0 103.0 jit_solution(14416524471366554320)
XLA Ops:
  0.0 1.6 %copy.10 = bf16[1,1536,256]{1,2,0:T(8,128)(2,1)S(1)} copy(bf16[1,1536,256]{2,1,0:T(8,128)(2,1)} %param.8) | data formatting | bytes 1572864 | tf_op args[0]
  1.6 0.0 copy-start.4
  1.6 1.0 %pad_dynamic-slice_fusion.2 = (bf16[144,384]{1,0:T(8,128)(2,1)}, bf16[144,384]{1,0:T(8,128)(2,1)}, bf16[144,384]{1,0:T(8,128)(2,1)}, bf16[144,384]{1,0:T(8,128)(2,1)S(1)}) fusion(s32[]{:T(128)S(6)} %select_n.63, s32[]{:T(128)S(6)} %select_n.69, bf16[256,1536]{1,0:T(8,128)(2,1)S(1)} %bitcast.33, s32[]{:T(128)S(6)} %select_n.73, s32[]{:T(128)S(6)} %select_n.71, ...), kind=kLoop, calls=%fused_computation.3 | loop fusion | bytes 1228820 | tf_op jit(solution)/shard_map/dynamic_slice | solution.py:176
  2.7 5.0 %collective-permute-start.4 = (bf16[144,384]{1,0:T(8,128)(2,1)}, bf16[144,384]{1,0:T(8,128)(2,1)S(1)}, u32[]{:S(2)}, u32[]{:S(2)}) collective-permute-start(bf16[144,384]{1,0:T(8,128)(2,1)} %get-tuple-element.10), channel_id=1, source_target_pairs={{0,12},{4,0},{8,4},{12,8},{1,13},{5,1},{9,5},{13,9},{2,14},{6,2},{... | collective-permute-start | bytes 331784 | tf_op jit(solution)/shard_map/ppermute | solution.py:36
  7.7 1.0 collective-permute-start
  8.7 0.5 shard_map.82
  9.2 0.0 copy-start.5
  9.2 0.1 constant_dynamic-slice_fusion.1
  9.3 1.2 %constant_dynamic-slice_fusion.2 = bf16[384,320]{1,0:T(8,128)(2,1)S(1)} fusion(bf16[384,640]{1,0:T(8,128)(2,1)} %param.11, s32[]{:T(128)S(6)} %select_n.74), kind=kLoop, calls=%fused_computation.32 | loop fusion | bytes 491524 | tf_op jit(solution)/shard_map/dynamic_slice | solution.py:146
  10.5 0.1 pad_maximum_fusion.refs_0_
  10.6 0.8 collective-permute-done.4.x_ref
  11.5 6.1 %collective-permute-done.2.x_ref = bf16[144,384]{1,0:T(8,128)(2,1)S(1)} collective-permute-done((bf16[144,384]{1,0:T(8,128)(2,1)}, bf16[144,384]{1,0:T(8,128)(2,1)S(1)}, u32[]{:S(2)}, u32[]{:S(2)}) %collective-permute-start.2) | collective-permute-done | bytes 110624 | tf_op jit(solution)/shard_map/ppermute | solution.py:36
  17.6 0.0 collective-permute-done.x_ref
  17.6 0.6 collective-permute-start.6
  18.2 3.2 %collective-permute-start.7 = (bf16[384,512]{1,0:T(8,128)(2,1)S(1)}, bf16[384,512]{1,0:T(8,128)(2,1)S(1)}, u32[]{:S(2)}, u32[]{:S(2)}) collective-permute-start(bf16[384,512]{1,0:T(8,128)(2,1)S(1)} %pad_maximum_fusion.refs_0_), channel_id=1, source_target_pairs={{0,12},{4,0},{8,4},{12,8},{1,13},{5,1},{9,5},{13,9},{2,14},{6,2},{... | collective-permute-start | bytes 1179656 | tf_op jit(solution)/shard_map/ppermute | solution.py:36
  21.5 0.5 shard_map.85
  21.9 0.1 collective-permute-start.5
  22.0 0.5 shard_map.84
  22.5 0.0 copy-start.6
  22.5 0.7 collective-permute-start.3
  23.2 0.5 shard_map.83
  23.6 3.3 %collective-permute-start.1 = (bf16[128,384]{1,0:T(8,128)(2,1)S(1)}, bf16[128,384]{1,0:T(8,128)(2,1)S(1)}, u32[]{:S(2)}, u32[]{:S(2)}) collective-permute-start(bf16[128,384]{1,0:T(8,128)(2,1)S(1)} %shard_map.83), channel_id=1, source_target_pairs={{0,12},{4,0},{8,4},{12,8},{1,13},{5,1},{9,5},{13,9},{2,14},{6,2},{... | collective-permute-start | bytes 294920 | tf_op jit(solution)/shard_map/ppermute | solution.py:36
  26.9 4.6 %collective-permute-done.6.refs_1_ = bf16[384,512]{1,0:T(8,128)(2,1)S(1)} collective-permute-done((bf16[384,512]{1,0:T(8,128)(2,1)S(1)}, bf16[384,512]{1,0:T(8,128)(2,1)S(1)}, u32[]{:S(2)}, u32[]{:S(2)}) %collective-permute-start.6) | collective-permute-done | bytes 393248 | tf_op jit(solution)/shard_map/ppermute | solution.py:36
  31.5 7.8 %collective-permute-done.7.refs_3_ = bf16[384,512]{1,0:T(8,128)(2,1)S(1)} collective-permute-done((bf16[384,512]{1,0:T(8,128)(2,1)S(1)}, bf16[384,512]{1,0:T(8,128)(2,1)S(1)}, u32[]{:S(2)}, u32[]{:S(2)}) %collective-permute-start.7) | collective-permute-done | bytes 393248 | tf_op jit(solution)/shard_map/ppermute | solution.py:36
  39.3 0.1 select_select_fusion.1
  39.4 9.6 %collective-permute-start.8 = (bf16[384,512]{1,0:T(8,128)(2,1)S(1)}, bf16[384,512]{1,0:T(8,128)(2,1)S(1)}, u32[]{:S(2)}, u32[]{:S(2)}) collective-permute-start(bf16[384,512]{1,0:T(8,128)(2,1)S(1)} %select_select_fusion.1), channel_id=1, source_target_pairs={{0,8},{4,0},{8,12},{12,4},{1,9},{5,1},{9,13},{13,5},{2,10},{6,2},{... | collective-permute-start | bytes 1179656 | tf_op jit(solution)/shard_map/ppermute | solution.py:163
  49.0 0.0 collective-permute-done.5
  49.0 0.0 collective-permute-done.3
  49.0 0.0 collective-permute-done.1
  49.0 0.2 fusion.8
  49.2 2.4 %collective-permute-start.9 = (bf16[384,512]{1,0:T(8,128)(2,1)S(1)}, bf16[384,512]{1,0:T(8,128)(2,1)S(1)}, u32[]{:S(2)}, u32[]{:S(2)}) collective-permute-start(bf16[384,512]{1,0:T(8,128)(2,1)S(1)} %constant_dynamic-slice_fusion.refs_0_), channel_id=1, source_target_pairs={{0,4},{4,8},{8,12},{12,0},{1,5},{5,9},{9,13},{13,1},{2,6},{6,10},{... | collective-permute-start | bytes 1179656 | tf_op jit(solution)/shard_map/ppermute | solution.py:36
  51.6 1.5 %collective-permute-start.10 = (bf16[384,512]{1,0:T(8,128)(2,1)S(1)}, bf16[384,512]{1,0:T(8,128)(2,1)S(1)}, u32[]{:S(2)}, u32[]{:S(2)}) collective-permute-start(bf16[384,512]{1,0:T(8,128)(2,1)S(1)} %constant_dynamic-slice_fusion.refs_0_), channel_id=1, source_target_pairs={{0,12},{4,0},{8,4},{12,8},{1,13},{5,1},{9,5},{13,9},{2,14},{6,2},{... | collective-permute-start | bytes 1179656 | tf_op jit(solution)/shard_map/ppermute | solution.py:36
  53.1 10.4 %all-gather = bf16[1024,384]{1,0:T(8,128)(2,1)S(1)} all-gather(bf16[128,384]{1,0:T(8,128)(2,1)S(1)} %fusion.8), channel_id=2, replica_groups=mesh['segment'=2,'win'=4,'mp'=4] {'segment','mp'}, dimensions={0}, use_global_device_ids=true | all-gather | bytes 884736 | tf_op jit(solution)/shard_map/all_gather | solution.py:206
  63.5 0.0 collective-permute-done.8.refs_2_
  63.5 2.5 %shard_map.86 = bf16[8,128,384]{2,1,0:T(8,128)(2,1)} custom-call(s32[1]{0:T(128)} %bitcast.win_ref, bf16[8,128,384]{2,1,0:T(8,128)(2,1)S(1)} %bitcast.29, bf16[384,512]{1,0:T(8,128)(2,1)S(1)} %pad_maximum_fusion.refs_0_, bf16[384,512]{1,0:T(8,128)(2,1)S(1)} %collective-permute-done.6.refs_1_, bf16[384,512]{1,0:T(8,128)(2,1)S(1)} %collective-permute-done.8.refs_2_, ...), custom_call_target="tpu_custom_call" | custom-call | bytes 1048576 | tf_op jit(solution)/shard_map/pallas_call | solution.py:24
  66.0 3.7 %all-to-all-start = ((bf16[8,128,384]{2,1,0:T(8,128)(2,1)}), bf16[8,128,384]{2,1,0:T(8,128)(2,1)S(1)}, u32[]{:S(2)}, u32[]{:S(2)}) async-start(bf16[8,128,384]{2,1,0:T(8,128)(2,1)} %shard_map.86), calls=%async_computation | async-start | bytes 1572864 | tf_op jit(solution)/shard_map/all_to_all | solution.py:215
  69.7 0.1 dynamic_slice.38
  69.8 0.1 fusion.9
  69.9 0.2 convert_reduce_fusion.1
  70.1 1.0 %collective-permute-done.10.refs_3_ = bf16[384,512]{1,0:T(8,128)(2,1)S(1)} collective-permute-done((bf16[384,512]{1,0:T(8,128)(2,1)S(1)}, bf16[384,512]{1,0:T(8,128)(2,1)S(1)}, u32[]{:S(2)}, u32[]{:S(2)}) %collective-permute-start.10) | collective-permute-done | bytes 393248 | tf_op jit(solution)/shard_map/ppermute | solution.py:36
  71.2 0.8 select_select_fusion
  72.0 1.4 %collective-permute-start.11 = (bf16[384,512]{1,0:T(8,128)(2,1)}, bf16[384,512]{1,0:T(8,128)(2,1)S(1)}, u32[]{:S(2)}, u32[]{:S(2)}) collective-permute-start(bf16[384,512]{1,0:T(8,128)(2,1)} %select_select_fusion), channel_id=1, source_target_pairs={{0,8},{4,0},{8,12},{12,4},{1,9},{5,1},{9,13},{13,5},{2,10},{6,2},{... | collective-permute-start | bytes 1179656 | tf_op jit(solution)/shard_map/ppermute | solution.py:163
  73.3 7.9 %all-to-all-done = bf16[8,128,384]{2,1,0:T(8,128)(2,1)S(1)} async-done(((bf16[8,128,384]{2,1,0:T(8,128)(2,1)}), bf16[8,128,384]{2,1,0:T(8,128)(2,1)S(1)}, u32[]{:S(2)}, u32[]{:S(2)}) %all-to-all-start) | async-done | bytes 786464 | tf_op jit(solution)/shard_map/all_to_all | solution.py:215
  81.2 0.1 convert_reduce_fusion
  81.4 10.4 %all-gather.1 = bf16[1024,384]{1,0:T(8,128)(2,1)S(1)} all-gather(bf16[128,384]{1,0:T(8,128)(2,1)S(1)} %add_convert_fusion), channel_id=3, replica_groups=mesh['segment'=2,'win'=4,'mp'=4] {'segment','mp'}, dimensions={0}, use_global_device_ids=true | all-gather | bytes 884736 | tf_op jit(solution)/shard_map/all_gather | solution.py:217
  91.7 1.1 %shard_map.87 = bf16[64,512]{1,0:T(8,128)(2,1)S(1)} custom-call(s32[1]{0:T(128)} %bitcast.win_ref, bf16[8,128,384]{2,1,0:T(8,128)(2,1)S(1)} %bitcast.28, f32[1,512]{1,0:T(1,128)S(1)} %bitcast.32, bf16[64,256]{1,0:T(8,128)(2,1)S(1)} %bitcast.31, bf16[384,512]{1,0:T(8,128)(2,1)S(1)} %constant_dynamic-slice_fusion.refs_0_, ...), custom_call_target="tpu_custom_call" | custom-call | bytes 1048576 | tf_op jit(solution)/shard_map/pallas_call | solution.py:24
  92.9 9.5 %all_to_all.10 = bf16[8,8,512]{2,1,0:T(8,128)(2,1)S(1)} all-to-all(bf16[8,8,512]{2,1,0:T(8,128)(2,1)S(1)} %bitcast.30), channel_id=1, replica_groups=mesh['segment'=2,'win'=4,'mp'=4] {'segment','win'}, dimensions={0} | all-to-all | bytes 131072 | tf_op jit(solution)/shard_map/all_to_all | solution.py:229
  102.3 0.6 log1p.9
  (21 shorter events, 0.1 us)
Async XLA Ops:
  0.0 21.4 %copy-start = (bf16[384,1024]{1,0:T(8,128)(2,1)S(1)}, bf16[384,1024]{1,0:T(8,128)(2,1)}, u32[]{:S(2)}) copy-start(bf16[384,1024]{1,0:T(8,128)(2,1)} %param.13) | copy-start | bytes 2359300
  0.0 8.7 %copy-start.1 = (bf16[384,5,384]{2,0,1:T(8,128)(2,1)S(1)}, bf16[384,5,384]{2,0,1:T(8,128)(2,1)}, u32[]{:S(2)}) copy-start(bf16[384,5,384]{2,0,1:T(8,128)(2,1)} %param.9) | copy-start | bytes 4423684
  1.6 1.1 %copy-start.2 = (bf16[1,1536,256]{1,2,0:T(8,128)(2,1)}, bf16[1,1536,256]{1,2,0:T(8,128)(2,1)S(1)}, u32[]{:S(2)}) copy-start(bf16[1,1536,256]{1,2,0:T(8,128)(2,1)S(1)} %copy.10) | copy-start | bytes 2359300
  1.6 7.6 %copy-start.4 = (bf16[384,384]{1,0:T(8,128)(2,1)S(1)}, bf16[384,384]{1,0:T(8,128)(2,1)}, u32[]{:S(2)}) copy-start(bf16[384,384]{1,0:T(8,128)(2,1)} %param.12) | copy-start | bytes 884740
  2.7 8.8 %collective-permute-start.4 = (bf16[144,384]{1,0:T(8,128)(2,1)}, bf16[144,384]{1,0:T(8,128)(2,1)S(1)}, u32[]{:S(2)}, u32[]{:S(2)}) collective-permute-start(bf16[144,384]{1,0:T(8,128)(2,1)} %get-tuple-element.10), channel_id=1, source_target_pairs={{0,12},{4,0},{8,4},{12,8},{1,13},{5,1},{9,5},{13,9},{2,14},{6,2},{... | collective-permute-start | bytes 331784 | tf_op jit(solution)/shard_map/ppermute | solution.py:36
  7.7 9.9 %collective-permute-start.2 = (bf16[144,384]{1,0:T(8,128)(2,1)}, bf16[144,384]{1,0:T(8,128)(2,1)S(1)}, u32[]{:S(2)}, u32[]{:S(2)}) collective-permute-start(bf16[144,384]{1,0:T(8,128)(2,1)} %get-tuple-element.11), channel_id=1, source_target_pairs={{0,8},{4,12},{8,0},{12,4},{1,9},{5,13},{9,1},{13,5},{2,10},{6,14},... | collective-permute-start | bytes 331784 | tf_op jit(solution)/shard_map/ppermute | solution.py:36
  7.7 9.9 %collective-permute-start = (bf16[144,384]{1,0:T(8,128)(2,1)}, bf16[144,384]{1,0:T(8,128)(2,1)S(1)}, u32[]{:S(2)}, u32[]{:S(2)}) collective-permute-start(bf16[144,384]{1,0:T(8,128)(2,1)} %get-tuple-element.9), channel_id=1, source_target_pairs={{0,4},{4,8},{8,12},{12,0},{1,5},{5,9},{9,13},{13,1},{2,6},{6,10},{... | collective-permute-start | bytes 331784 | tf_op jit(solution)/shard_map/ppermute | solution.py:36
  9.2 12.3 %copy-start.5 = (s32[3,1,8,8]{3,2,1,0:T(8,128)S(1)}, s32[3,1,8,8]{3,2,1,0:T(8,128)}, u32[]{:S(2)}) copy-start(s32[3,1,8,8]{3,2,1,0:T(8,128)} %param.15) | copy-start | bytes 2308
  17.6 13.9 %collective-permute-start.6 = (bf16[384,512]{1,0:T(8,128)(2,1)S(1)}, bf16[384,512]{1,0:T(8,128)(2,1)S(1)}, u32[]{:S(2)}, u32[]{:S(2)}) collective-permute-start(bf16[384,512]{1,0:T(8,128)(2,1)S(1)} %pad_maximum_fusion.refs_0_), channel_id=1, source_target_pairs={{0,4},{4,8},{8,12},{12,0},{1,5},{5,9},{9,13},{13,1},{2,6},{6,10},{... | collective-permute-start | bytes 1179656 | tf_op jit(solution)/shard_map/ppermute | solution.py:36
  18.2 21.1 %collective-permute-start.7 = (bf16[384,512]{1,0:T(8,128)(2,1)S(1)}, bf16[384,512]{1,0:T(8,128)(2,1)S(1)}, u32[]{:S(2)}, u32[]{:S(2)}) collective-permute-start(bf16[384,512]{1,0:T(8,128)(2,1)S(1)} %pad_maximum_fusion.refs_0_), channel_id=1, source_target_pairs={{0,12},{4,0},{8,4},{12,8},{1,13},{5,1},{9,5},{13,9},{2,14},{6,2},{... | collective-permute-start | bytes 1179656 | tf_op jit(solution)/shard_map/ppermute | solution.py:36
  21.9 27.1 %collective-permute-start.5 = (bf16[128,384]{1,0:T(8,128)(2,1)S(1)}, bf16[128,384]{1,0:T(8,128)(2,1)S(1)}, u32[]{:S(2)}, u32[]{:S(2)}) collective-permute-start(bf16[128,384]{1,0:T(8,128)(2,1)S(1)} %shard_map.85), channel_id=1, source_target_pairs={{0,4},{4,8},{8,12},{12,0},{1,5},{5,9},{9,13},{13,1},{2,6},{6,10},{... | collective-permute-start | bytes 294920 | tf_op jit(solution)/shard_map/ppermute | solution.py:36
  22.5 26.6 %copy-start.3 = (bf16[1,1536,256]{1,2,0:T(8,128)(2,1)S(1)}, bf16[1,1536,256]{1,2,0:T(8,128)(2,1)}, u32[]{:S(2)}) copy-start(bf16[1,1536,256]{1,2,0:T(8,128)(2,1)} %copy-done.2) | copy-start | bytes 2359300
  22.5 26.6 %copy-start.6 = (f32[384]{0:T(512)S(1)}, f32[384]{0:T(512)}, u32[]{:S(2)}) copy-start(f32[384]{0:T(512)} %param.10) | copy-start | bytes 4612
  22.5 26.5 %collective-permute-start.3 = (bf16[128,384]{1,0:T(8,128)(2,1)S(1)}, bf16[128,384]{1,0:T(8,128)(2,1)S(1)}, u32[]{:S(2)}, u32[]{:S(2)}) collective-permute-start(bf16[128,384]{1,0:T(8,128)(2,1)S(1)} %shard_map.84), channel_id=1, source_target_pairs={{0,8},{4,12},{8,0},{12,4},{1,9},{5,13},{9,1},{13,5},{2,10},{6,14},... | collective-permute-start | bytes 294920 | tf_op jit(solution)/shard_map/ppermute | solution.py:36
  23.6 25.4 %collective-permute-start.1 = (bf16[128,384]{1,0:T(8,128)(2,1)S(1)}, bf16[128,384]{1,0:T(8,128)(2,1)S(1)}, u32[]{:S(2)}, u32[]{:S(2)}) collective-permute-start(bf16[128,384]{1,0:T(8,128)(2,1)S(1)} %shard_map.83), channel_id=1, source_target_pairs={{0,12},{4,0},{8,4},{12,8},{1,13},{5,1},{9,5},{13,9},{2,14},{6,2},{... | collective-permute-start | bytes 294920 | tf_op jit(solution)/shard_map/ppermute | solution.py:36
  39.4 24.1 %collective-permute-start.8 = (bf16[384,512]{1,0:T(8,128)(2,1)S(1)}, bf16[384,512]{1,0:T(8,128)(2,1)S(1)}, u32[]{:S(2)}, u32[]{:S(2)}) collective-permute-start(bf16[384,512]{1,0:T(8,128)(2,1)S(1)} %select_select_fusion.1), channel_id=1, source_target_pairs={{0,8},{4,0},{8,12},{12,4},{1,9},{5,1},{9,13},{13,5},{2,10},{6,2},{... | collective-permute-start | bytes 1179656 | tf_op jit(solution)/shard_map/ppermute | solution.py:163
  49.2 20.9 %collective-permute-start.9 = (bf16[384,512]{1,0:T(8,128)(2,1)S(1)}, bf16[384,512]{1,0:T(8,128)(2,1)S(1)}, u32[]{:S(2)}, u32[]{:S(2)}) collective-permute-start(bf16[384,512]{1,0:T(8,128)(2,1)S(1)} %constant_dynamic-slice_fusion.refs_0_), channel_id=1, source_target_pairs={{0,4},{4,8},{8,12},{12,0},{1,5},{5,9},{9,13},{13,1},{2,6},{6,10},{... | collective-permute-start | bytes 1179656 | tf_op jit(solution)/shard_map/ppermute | solution.py:36
  51.6 19.6 %collective-permute-start.10 = (bf16[384,512]{1,0:T(8,128)(2,1)S(1)}, bf16[384,512]{1,0:T(8,128)(2,1)S(1)}, u32[]{:S(2)}, u32[]{:S(2)}) collective-permute-start(bf16[384,512]{1,0:T(8,128)(2,1)S(1)} %constant_dynamic-slice_fusion.refs_0_), channel_id=1, source_target_pairs={{0,12},{4,0},{8,4},{12,8},{1,13},{5,1},{9,5},{13,9},{2,14},{6,2},{... | collective-permute-start | bytes 1179656 | tf_op jit(solution)/shard_map/ppermute | solution.py:36
  66.0 3.7 %copy-start.7 = (f32[1024]{0:T(1024)S(1)}, f32[1024]{0:T(1024)}, u32[]{:S(2)}) copy-start(f32[1024]{0:T(1024)} %param.14) | copy-start | bytes 12292
  66.0 15.3 %all-to-all-start = ((bf16[8,128,384]{2,1,0:T(8,128)(2,1)}), bf16[8,128,384]{2,1,0:T(8,128)(2,1)S(1)}, u32[]{:S(2)}, u32[]{:S(2)}) async-start(bf16[8,128,384]{2,1,0:T(8,128)(2,1)} %shard_map.86), calls=%async_computation | async-start | bytes 1572864 | tf_op jit(solution)/shard_map/all_to_all | solution.py:215
  72.0 19.8 %collective-permute-start.11 = (bf16[384,512]{1,0:T(8,128)(2,1)}, bf16[384,512]{1,0:T(8,128)(2,1)S(1)}, u32[]{:S(2)}, u32[]{:S(2)}) collective-permute-start(bf16[384,512]{1,0:T(8,128)(2,1)} %select_select_fusion), channel_id=1, source_target_pairs={{0,8},{4,0},{8,12},{12,4},{1,9},{5,1},{9,13},{13,5},{2,10},{6,2},{... | collective-permute-start | bytes 1179656 | tf_op jit(solution)/shard_map/ppermute | solution.py:163

commit v4 on v3

--- a/solution.py
+++ b/solution.py
@@ -18,14 +18,15 @@
 BF16 = jnp.bfloat16
 
 
-def call_kernel(body, out_shape, *operands, flops=0):
+def call_kernel(body, out_shape, *operands, scratch=(), flops=0):
     whole = pl.BlockSpec(memory_space=pltpu.VMEM)
     scalars = pl.BlockSpec(memory_space=pltpu.SMEM)
     return pl.pallas_call(
         body,
         out_shape=out_shape,
         in_specs=[scalars if x.dtype == jnp.int32 else whole for x in operands],
-        out_specs=whole,
+        out_specs=jax.tree.map(lambda _: whole, out_shape),
+        scratch_shapes=list(scratch),
         compiler_params=pltpu.CompilerParams(vmem_limit_bytes=VMEM_BYTES),
         cost_estimate=pl.CostEstimate(flops=flops, bytes_accessed=1 << 20, transcendentals=0),
     )(*operands)
@@ -36,9 +37,62 @@
     return lax.ppermute(x, axis, [(i, (i + by) % size) for i in range(size)])
 
 
+def bins_kernel(place_ref, x_ref, own_ref, next_ref, part_ref, rest_ref, padded):
+    segment, window, model = place_ref[0], place_ref[1], place_ref[2]
+    odd = lax.rem(model, 2)
+    bins = rest_ref.shape[0]
+    margin = (own_ref.shape[0] - bins) // 2
+    start = segment * bins
+    padded[:margin] = jnp.zeros((margin, padded.shape[1]), F32)
+    padded[padded.shape[0] - margin :] = jnp.zeros((margin, padded.shape[1]), F32)
+
+    def turned(block):
+        first = pl.multiple_of(block * padded.shape[1], 16)
+        columns = x_ref[pl.ds(first, padded.shape[1]), :].astype(F32)
+        padded[margin : padded.shape[0] - margin] = columns.T
+
+    def cut(out, first):
+        out[...] = padded[pl.ds(pl.multiple_of(start + first, 8), out.shape[0])].astype(BF16)
+
+    turned(lax.rem(window + 1 + 2 * odd, 4))
+    cut(next_ref, 0)
+    turned(lax.rem(window + 2, 4))
+    cut(part_ref, odd * (own_ref.shape[0] - part_ref.shape[0]))
+    turned(window)
+    cut(own_ref, 0)
+    turned(model)
+    cut(rest_ref, margin)
+
+
+def pack_kernel(place_ref, *refs):
+    *parts, o_ref = refs
+    segments = sum(x.shape[1] for x in parts) // o_ref.shape[1]
+    for s in range(segments):
+
+        @pl.when(place_ref[0] == s)
+        def _():
+            at = 0
+            for x in parts:
+                width = x.shape[1] // segments
+                o_ref[:, at : at + width] = x[:, s * width : (s + 1) * width]
+                at += width
+
+
 def conv_kernel(x_ref, w_ref, o_ref):
+    taps(x_ref[...].astype(F32), w_ref, o_ref)
+
+
+def parts_conv_kernel(place_ref, own_ref, other_ref, w_ref, o_ref):
+    even = lax.rem(place_ref[2], 2) == 0
+    own, other = own_ref[...].astype(F32), other_ref[...].astype(F32)
+    rows = o_ref.shape[0] + (w_ref.shape[0] - 1) * DILATION_STEP
+    low = jnp.where(even, own, other)
+    high = jnp.where(even, other, own)[2 * own.shape[0] - rows :]
+    taps(jnp.concatenate([low, high], axis=0), w_ref, o_ref)
+
+
+def taps(x, w_ref, o_ref):
     bins = o_ref.shape[0]
-    x = x_ref[...].astype(F32)
     total = jnp.zeros(o_ref.shape, F32)
     for tap in range(w_ref.shape[0]):
         start = tap * DILATION_STEP
@@ -141,25 +195,26 @@
     reach = (tap_count - 1) // 2 * DILATION_STEP
     plane = ("segment", "mp")
 
-    def part_of_segment(x):
-        size = x.shape[1] // segments
-        return lax.dynamic_slice_in_dim(x, segment_index * size, size, 1)
-
-    attention_own = jnp.concatenate(
-        [part_of_segment(qkv_weight), part_of_segment(out_weight)], axis=1
-    )
-    head_own = part_of_segment(head_weight)
+    place = jnp.stack([segment_index, win_index, model_index]).astype(jnp.int32)
+
+    def part_of_segment(*parts):
+        width = sum(x.shape[1] for x in parts) // segments
+        own = jax.ShapeDtypeStruct((row_count, width), BF16)
+        return call_kernel(pack_kernel, own, place, *parts)
+
+    attention_own = part_of_segment(qkv_weight, out_weight)
+    head_cols = head_weight.shape[1] // segments
+    head_own = lax.dynamic_slice_in_dim(head_weight, segment_index * head_cols, head_cols, 1)
     heads = qkv_weight.shape[1] // segments // SPAN
-    stepwise = windows <= 8 and row_count == out_cols
-
-    def gathered(own, after):
+    stepwise = windows == 4 and models == 4
+
+    def gathered(own, after, later):
         if not stepwise:
             return [lax.all_gather(own, "win", axis=0, tiled=True)]
         sent, _ = lax.optimization_barrier((own, after))
-        if windows != 4:
-            return [own] + [shifted(sent, "win", by) for by in range(1, windows)]
         below, above = shifted(sent, "win", 1), shifted(sent, "win", -1)
         handed = jnp.where(win_index == 1, above, jnp.where(win_index == 2, below, sent))
+        handed, _ = lax.optimization_barrier((handed, later))
         across = lax.ppermute(handed, "win", [(0, 2), (1, 0), (2, 3), (3, 1)])
         return [own, below, across, above]
 
@@ -168,41 +223,68 @@
     bias_part = lax.dynamic_slice_in_dim(head_bias, segment_index * track_cols, track_cols, 0)
     counts = gene_counts(exon_lists[:, 0], bin_count)
 
-    taps = jnp.transpose(convolution_kernel_weight, (1, 0, 2))
-    padded = jnp.pad(feats[0].T, ((reach, reach), (0, 0)))
-    own_bins = lax.dynamic_slice_in_dim(padded, segment_index * bins, bins + 2 * reach, 0)
-
-    def rows_for(window):
-        return lax.dynamic_slice_in_dim(own_bins, window * row_count, row_count, 1)
-
-    def conv_of(x, dtype):
+    tap_weights = jnp.transpose(convolution_kernel_weight, (1, 0, 2))
+
+    def conv_of(dtype, *operands):
         return call_kernel(
-            conv_kernel,
+            conv_kernel if len(operands) == 1 else parts_conv_kernel,
             jax.ShapeDtypeStruct((bins, out_cols), dtype),
-            x,
-            taps,
+            *operands,
+            tap_weights,
             flops=2 * bins * out_cols * row_count * tap_count,
         )
 
     if stepwise:
-        arrived = [
-            shifted(rows_for(lax.rem(win_index + by, windows)), "win", by)
-            for by in range(1, windows)
+        block = jax.ShapeDtypeStruct((bins + 2 * reach, row_count), BF16)
+        part = jax.ShapeDtypeStruct(((bins + 2 * reach) // 32 * 16 + 16, row_count), BF16)
+        own_rows, next_rows, part_rows, own_feats = call_kernel(
+            bins_kernel,
+            [block, block, part, jax.ShapeDtypeStruct((bins, out_cols), BF16)],
+            place,
+            feats[0],
+            scratch=[pltpu.VMEM((bin_count + 2 * reach, row_count), F32)],
+        )
+
+        def turned_by(x, even, odd):
+            pairs = [
+                (w * models + m, (w + (odd if m % 2 else even)) % windows * models + m)
+                for w in range(windows)
+                for m in range(models)
+            ]
+            return lax.ppermute(x, ("win", "mp"), pairs)
+
+        def swapped(x):
+            return lax.ppermute(x, "mp", [(m, m ^ 1) for m in range(models)])
+
+        next_in, part_in = turned_by(next_rows, 1, -1), turned_by(part_rows, 2, 2)
+        arrived = [next_in, part_in]
+        swaps = [swapped(next_in), swapped(part_in)]
+        conv_pre = conv_of(F32, own_rows)
+        partials = [
+            conv_of(BF16, next_in),
+            conv_of(BF16, swaps[0]),
+            conv_of(BF16, place, part_in, swaps[1]),
         ]
-        attention_pieces = gathered(attention_own, arrived)
-        conv_pre = conv_of(rows_for(win_index), F32)
-        for by, x in enumerate(arrived, 1):
-            conv_pre = conv_pre + shifted(conv_of(x, BF16), "win", -by).astype(F32)
+        returned = [
+            turned_by(partials[0], -1, 1),
+            turned_by(partials[1], 1, -1),
+            turned_by(partials[2], 2, 2),
+        ]
+        attention_pieces = gathered(attention_own, arrived[0], returned[:2])
+        for x in returned:
+            conv_pre = conv_pre + x.astype(F32)
     else:
+        padded = jnp.pad(feats[0].T, ((reach, reach), (0, 0)))
+        own_bins = lax.dynamic_slice_in_dim(padded, segment_index * bins, bins + 2 * reach, 0)
+        own_feats = lax.dynamic_slice(own_bins, (reach, model_index * out_cols), (bins, out_cols))
         blocks = own_bins.reshape(own_bins.shape[0], windows, row_count).transpose(1, 0, 2)
         arrived = lax.all_to_all(blocks, "win", 0, 0, tiled=True)
-        attention_pieces = gathered(attention_own, None)
-        partial = jnp.stack([conv_of(arrived[w], BF16) for w in range(windows)])
+        attention_pieces = gathered(attention_own, None, None)
+        partial = jnp.stack([conv_of(BF16, arrived[w]) for w in range(windows)])
         conv_pre = lax.all_to_all(partial, "win", 0, 0, tiled=True).astype(F32).sum(axis=0)
 
-    own_feats = lax.dynamic_slice(own_bins, (reach, model_index * out_cols), (bins, out_cols))
     conv_out = (own_feats + jax.nn.gelu(conv_pre + conv_bias)).astype(BF16)
-    head_pieces = gathered(head_own, conv_out)
+    head_pieces = gathered(head_own, conv_out, ())
     all_chan = lax.all_gather(conv_out, plane, axis=0)
 
     partial = call_kernel(

time: 103 us -> 95.5 us (0.927)
  waiting for transfers between devices: 28.3 us -> 21.3 us
  starting transfers between devices: 32.4 us -> 25.8 us
  Pallas kernels: 5.38 us -> 9.65 us
  local copies, waits for them, and re-layouts: 4.67 us -> 6.25 us
    ppermute x10 -> x4, starting transfers between devices: 17.8 us -> 7.69 us  [shifted(): return lax.ppermute(x, axis, [(i, (i + by) % size) for i in range(size)])]
    ppermute x10 -> x4, waiting for transfers between devices: 20.4 us -> 10.8 us  [shifted(): return lax.ppermute(x, axis, [(i, (i + by) % size) for i in range(size)])]
    ppermute x0 -> x7, starting transfers between devices: none -> 9.5 us  [the longest x5 8.99 us: turned_by(): return lax.ppermute(x, ('win', 'mp'), pairs)]
    ppermute x2, starting transfers between devices: 11 us -> 4.95 us  [gathered(): across = lax.ppermute(handed, 'win', [(0, 2), (1, 0), (2, 3), (3, 1)])]
    ppermute x0 -> x7, waiting for transfers between devices: none -> 5.78 us  [the longest x5 5.77 us: turned_by(): return lax.ppermute(x, ('win', 'mp'), pairs)]
    pallas_call x6 -> x8, Pallas kernels: 5.38 us -> 9.65 us  [call_kernel(): pl.pallas_call(body, out_shape=out_shape, in_specs=[scalars if x.dtype ==...]
    all_to_all x1, waiting for transfers between devices: 7.91 us -> 4.68 us  [local(): lax.all_to_all(partial, plane, 0, 0, tiled=True).astype(F32).sum(axis=0)]
    unnamed x17 -> x28, local copies, waits for them, and re-layouts: 1.59 us -> 4.2 us
  transfers between devices with their start and end apart: 13 -> 14, of which waited for: 6 -> 7; matrix products, arithmetic and copies ran while one was open for 3% -> 3% of each run, Pallas kernels for 4% -> 8%
where the time goes in v4:
time: 95.5 us; the launch traced here: 95 us
  blocking collectives  30.2 us (32%)
  starting transfers between devices  25.8 us (27%)
  waiting for transfers between devices  21.3 us (22%)
  Pallas kernels  9.65 us (10%)
  local copies, waits for them, and re-layouts  6.25 us (7%)
  other arithmetic  1.57 us (2%)
    ppermute x4, waiting for transfers between devices, shifted(): return lax.ppermute(x, axis, [(i, (i + by) % size) for i in range(size)])  10.8 us
    all_gather x1, blocking collectives, local(): all_chan = lax.all_gather(conv_out, plane, axis=0)  10.4 us
    all_gather x1, blocking collectives, local(): all_resid = lax.all_gather(resid, plane, axis=0)  10.4 us
    pallas_call x8, Pallas kernels, call_kernel(): pl.pallas_call(body, out_shape=out_shape, in_specs=[scalars if x.dtype ==...  9.65 us
    all_to_all x1, blocking collectives, local(): lax.all_to_all(sums.reshape(owners, GENE_DEV, track_cols), ('segment', 'w...  9.37 us
    ppermute x5, starting transfers between devices, turned_by(): return lax.ppermute(x, ('win', 'mp'), pairs)  8.99 us
    ppermute x4, starting transfers between devices, shifted(): return lax.ppermute(x, axis, [(i, (i + by) % size) for i in range(size)])  7.69 us
    ppermute x5, waiting for transfers between devices, turned_by(): return lax.ppermute(x, ('win', 'mp'), pairs)  5.77 us
  transfers between devices with their start and end apart: 14, of which 7 were waited for; matrix products, arithmetic and copies ran while one was open for 3% of the time, Pallas kernels for 8%

profile of v4, /device:TPU:0, one launch (start us, length us, event | category | flops | bytes accessed | tf_op | source)
XLA Modules:
  0.0 95.0 jit_solution(15514114938778092411)
XLA Ops:
  0.0 0.1 pad_add_fusion.place_ref
  0.1 1.3 %copy-done.2 = bf16[1,1536,256]{2,1,0:T(8,128)(2,1)S(1)} copy-done((bf16[1,1536,256]{2,1,0:T(8,128)(2,1)S(1)}, bf16[1,1536,256]{2,1,0:T(8,128)(2,1)}, u32[]{:S(2)}) %copy-start.2) | copy-done | bytes 786456
  1.4 0.9 shard_map.82
  2.2 3.1 %collective-permute-start = (bf16[144,384]{1,0:T(8,128)(2,1)S(1)}, bf16[144,384]{1,0:T(8,128)(2,1)S(1)}, u32[]{:S(2)}, u32[]{:S(2)}) collective-permute-start(bf16[144,384]{1,0:T(8,128)(2,1)S(1)} %get-tuple-element.14), channel_id=1, source_target_pairs={{0,4},{1,13},{2,6},{3,15},{4,8},{5,1},{6,10},{7,3},{8,12},{9,5},{1... | collective-permute-start | bytes 331784 | tf_op jit(solution)/shard_map/ppermute | solution.py:254
  5.3 2.6 %collective-permute-start.4 = (bf16[80,384]{1,0:T(8,128)(2,1)S(1)}, bf16[80,384]{1,0:T(8,128)(2,1)}, u32[]{:S(2)}, u32[]{:S(2)}) collective-permute-start(bf16[80,384]{1,0:T(8,128)(2,1)S(1)} %get-tuple-element.15), channel_id=1, source_target_pairs={{0,8},{1,9},{2,10},{3,11},{4,12},{5,13},{6,14},{7,15},{8,0},{9,1},... | collective-permute-start | bytes 184328 | tf_op jit(solution)/shard_map/ppermute | solution.py:254
  7.9 1.0 %copy-done.3 = bf16[384,640]{1,0:T(8,128)(2,1)S(1)} copy-done((bf16[384,640]{1,0:T(8,128)(2,1)S(1)}, bf16[384,640]{1,0:T(8,128)(2,1)}, u32[]{:S(2)}) %copy-start.3) | copy-done | bytes 491544
  8.9 1.0 %copy-done.4 = bf16[384,384]{1,0:T(8,128)(2,1)S(1)} copy-done((bf16[384,384]{1,0:T(8,128)(2,1)S(1)}, bf16[384,384]{1,0:T(8,128)(2,1)}, u32[]{:S(2)}) %copy-start.4) | copy-done | bytes 294936
  9.9 0.7 shard_map.87.refs_0_
  10.6 0.7 collective-permute-done.x_ref
  11.3 1.0 %collective-permute-start.7 = (bf16[384,512]{1,0:T(8,128)(2,1)S(1)}, bf16[384,512]{1,0:T(8,128)(2,1)S(1)}, u32[]{:S(2)}, u32[]{:S(2)}) collective-permute-start(bf16[384,512]{1,0:T(8,128)(2,1)S(1)} %shard_map.87.refs_0_), channel_id=1, source_target_pairs={{0,4},{4,8},{8,12},{12,0},{1,5},{5,9},{9,13},{13,1},{2,6},{6,10},{... | collective-permute-start | bytes 1179656 | tf_op jit(solution)/shard_map/ppermute | solution.py:37
  12.3 2.8 %collective-permute-start.8 = (bf16[384,512]{1,0:T(8,128)(2,1)S(1)}, bf16[384,512]{1,0:T(8,128)(2,1)}, u32[]{:S(2)}, u32[]{:S(2)}) collective-permute-start(bf16[384,512]{1,0:T(8,128)(2,1)S(1)} %shard_map.87.refs_0_), channel_id=1, source_target_pairs={{0,12},{4,0},{8,4},{12,8},{1,13},{5,1},{9,5},{13,9},{2,14},{6,2},{... | collective-permute-start | bytes 1179656 | tf_op jit(solution)/shard_map/ppermute | solution.py:37
  15.1 1.3 %slice_bitcast_fusion.2 = (s32[8,8]{1,0:T(8,128)}, s32[8,8]{1,0:T(8,128)}, s32[8,8]{1,0:T(8,128)}) fusion(s32[3,1,8,8]{3,2,1,0:T(8,128)} %param.15), kind=kLoop, calls=%fused_computation.23 | loop fusion | bytes 1536 | tf_op jit(solution)/shard_map/eq | solution.py:171
  16.5 0.5 collective-permute-start.2
  17.0 0.9 copy-done.6
  17.9 0.5 shard_map.83
  18.4 0.5 shard_map.84
  18.8 0.7 collective-permute-start.1
  19.6 1.3 %shard_map.86 = bf16[128,384]{1,0:T(8,128)(2,1)S(1)} custom-call(s32[3]{0:T(128)S(1)} %pad_add_fusion.place_ref, bf16[80,384]{1,0:T(8,128)(2,1)} %collective-permute-done.4.own_ref, bf16[80,384]{1,0:T(8,128)(2,1)} %collective-permute-done.5.other_ref, bf16[5,384,384]{2,1,0:T(8,128)(2,1)S(1)} %bitcast.26), custom_call_target="tpu_custom_call" | custom-call | flops 188743680 | bytes 1048576 | tf_op jit(solution)/shard_map/pallas_call | solution.py:24
  20.9 0.0 copy-start.12
  20.9 0.6 collective-permute-start.6
  21.5 1.3 %shard_map.85 = bf16[128,384]{1,0:T(8,128)(2,1)S(1)} custom-call(bf16[144,384]{1,0:T(8,128)(2,1)} %collective-permute-done.2.x_ref, bf16[5,384,384]{2,1,0:T(8,128)(2,1)S(1)} %bitcast.27), custom_call_target="tpu_custom_call" | custom-call | flops 188743680 | bytes 1048576 | tf_op jit(solution)/shard_map/pallas_call | solution.py:24
  22.8 2.1 %collective-permute-start.3 = (bf16[128,384]{1,0:T(8,128)(2,1)S(1)}, bf16[128,384]{1,0:T(8,128)(2,1)S(1)}, u32[]{:S(2)}, u32[]{:S(2)}) collective-permute-start(bf16[128,384]{1,0:T(8,128)(2,1)S(1)} %shard_map.85), channel_id=1, source_target_pairs={{0,4},{1,13},{2,6},{3,15},{4,8},{5,1},{6,10},{7,3},{8,12},{9,5},{1... | collective-permute-start | bytes 294920 | tf_op jit(solution)/shard_map/ppermute | solution.py:254
  24.9 0.3 collective-permute-done.7.refs_1_
  25.2 7.1 %collective-permute-done.8.refs_3_ = bf16[384,512]{1,0:T(8,128)(2,1)} collective-permute-done((bf16[384,512]{1,0:T(8,128)(2,1)S(1)}, bf16[384,512]{1,0:T(8,128)(2,1)}, u32[]{:S(2)}, u32[]{:S(2)}) %collective-permute-start.8) | collective-permute-done | bytes 393248 | tf_op jit(solution)/shard_map/ppermute | solution.py:37
  32.3 0.1 select_select_fusion.1
  32.3 1.6 %collective-permute-done.1 = bf16[128,384]{1,0:T(8,128)(2,1)S(1)} collective-permute-done((bf16[128,384]{1,0:T(8,128)(2,1)S(1)}, bf16[128,384]{1,0:T(8,128)(2,1)S(1)}, u32[]{:S(2)}, u32[]{:S(2)}) %collective-permute-start.1) | collective-permute-done | bytes 98336 | tf_op jit(solution)/shard_map/ppermute | solution.py:254
  34.0 3.4 %collective-permute-done.3 = bf16[128,384]{1,0:T(8,128)(2,1)S(1)} collective-permute-done((bf16[128,384]{1,0:T(8,128)(2,1)S(1)}, bf16[128,384]{1,0:T(8,128)(2,1)S(1)}, u32[]{:S(2)}, u32[]{:S(2)}) %collective-permute-start.3) | collective-permute-done | bytes 98336 | tf_op jit(solution)/shard_map/ppermute | solution.py:254
  37.4 2.8 %collective-permute-start.9 = (bf16[384,512]{1,0:T(8,128)(2,1)S(1)}, bf16[384,512]{1,0:T(8,128)(2,1)S(1)}, u32[]{:S(2)}, u32[]{:S(2)}) collective-permute-start(bf16[384,512]{1,0:T(8,128)(2,1)S(1)} %select_select_fusion.1), channel_id=1, source_target_pairs={{0,8},{4,0},{8,12},{12,4},{1,9},{5,1},{9,13},{13,5},{2,10},{6,2},{... | collective-permute-start | bytes 1179656 | tf_op jit(solution)/shard_map/ppermute | solution.py:218
  40.2 0.0 collective-permute-done.6
  40.2 0.1 fusion.8
  40.3 0.1 collective-permute-start.10
  40.4 3.8 %collective-permute-start.11 = (bf16[384,512]{1,0:T(8,128)(2,1)S(1)}, bf16[384,512]{1,0:T(8,128)(2,1)S(1)}, u32[]{:S(2)}, u32[]{:S(2)}) collective-permute-start(bf16[384,512]{1,0:T(8,128)(2,1)S(1)} %constant_dynamic-slice_fusion.refs_0_), channel_id=1, source_target_pairs={{0,12},{4,0},{8,4},{12,8},{1,13},{5,1},{9,5},{13,9},{2,14},{6,2},{... | collective-permute-start | bytes 1179656 | tf_op jit(solution)/shard_map/ppermute | solution.py:37
  44.2 10.4 %all-gather = bf16[1024,384]{1,0:T(8,128)(2,1)S(1)} all-gather(bf16[128,384]{1,0:T(8,128)(2,1)S(1)} %fusion.8), channel_id=2, replica_groups=mesh['segment'=2,'win'=4,'mp'=4] {'segment','mp'}, dimensions={0}, use_global_device_ids=true | all-gather | bytes 884736 | tf_op jit(solution)/shard_map/all_gather | solution.py:288
  54.6 0.0 collective-permute-done.9.refs_2_
  54.6 3.5 %shard_map.88 = bf16[8,128,384]{2,1,0:T(8,128)(2,1)} custom-call(s32[1]{0:T(128)} %bitcast.win_ref, bf16[8,128,384]{2,1,0:T(8,128)(2,1)S(1)} %bitcast.29, bf16[384,512]{1,0:T(8,128)(2,1)S(1)} %shard_map.87.refs_0_, bf16[384,512]{1,0:T(8,128)(2,1)S(1)} %collective-permute-done.7.refs_1_, bf16[384,512]{1,0:T(8,128)(2,1)S(1)} %collective-permute-done.9.refs_2_, ...), custom_call_target="tpu_custom_call" | custom-call | bytes 1048576 | tf_op jit(solution)/shard_map/pallas_call | solution.py:24
  58.1 3.7 %all-to-all-start = ((bf16[8,128,384]{2,1,0:T(8,128)(2,1)}), bf16[8,128,384]{2,1,0:T(8,128)(2,1)S(1)}, u32[]{:S(2)}, u32[]{:S(2)}) async-start(bf16[8,128,384]{2,1,0:T(8,128)(2,1)} %shard_map.88), calls=%async_computation | async-start | bytes 1572864 | tf_op jit(solution)/shard_map/all_to_all | solution.py:297
  61.8 0.1 dynamic_slice.6
  61.9 0.1 fusion.9
  62.0 0.2 convert_reduce_fusion.1
  62.3 3.5 %collective-permute-done.11.refs_3_ = bf16[384,512]{1,0:T(8,128)(2,1)S(1)} collective-permute-done((bf16[384,512]{1,0:T(8,128)(2,1)S(1)}, bf16[384,512]{1,0:T(8,128)(2,1)S(1)}, u32[]{:S(2)}, u32[]{:S(2)}) %collective-permute-start.11) | collective-permute-done | bytes 393248 | tf_op jit(solution)/shard_map/ppermute | solution.py:37
  65.7 0.8 select_select_fusion
  66.5 2.1 %collective-permute-start.12 = (bf16[384,512]{1,0:T(8,128)(2,1)}, bf16[384,512]{1,0:T(8,128)(2,1)S(1)}, u32[]{:S(2)}, u32[]{:S(2)}) collective-permute-start(bf16[384,512]{1,0:T(8,128)(2,1)} %select_select_fusion), channel_id=1, source_target_pairs={{0,8},{4,0},{8,12},{12,4},{1,9},{5,1},{9,13},{13,5},{2,10},{6,2},{... | collective-permute-start | bytes 1179656 | tf_op jit(solution)/shard_map/ppermute | solution.py:218
  68.7 4.7 %all-to-all-done = bf16[8,128,384]{2,1,0:T(8,128)(2,1)S(1)} async-done(((bf16[8,128,384]{2,1,0:T(8,128)(2,1)}), bf16[8,128,384]{2,1,0:T(8,128)(2,1)S(1)}, u32[]{:S(2)}, u32[]{:S(2)}) %all-to-all-start) | async-done | bytes 786464 | tf_op jit(solution)/shard_map/all_to_all | solution.py:297
  73.4 0.1 convert_reduce_fusion
  73.5 10.4 %all-gather.1 = bf16[1024,384]{1,0:T(8,128)(2,1)S(1)} all-gather(bf16[128,384]{1,0:T(8,128)(2,1)S(1)} %add_convert_fusion), channel_id=3, replica_groups=mesh['segment'=2,'win'=4,'mp'=4] {'segment','mp'}, dimensions={0}, use_global_device_ids=true | all-gather | bytes 884736 | tf_op jit(solution)/shard_map/all_gather | solution.py:299
  83.9 1.1 %shard_map.89 = bf16[64,512]{1,0:T(8,128)(2,1)S(1)} custom-call(s32[1]{0:T(128)} %bitcast.win_ref, bf16[8,128,384]{2,1,0:T(8,128)(2,1)S(1)} %bitcast.28, f32[1,512]{1,0:T(1,128)S(1)} %bitcast.33, bf16[64,256]{1,0:T(8,128)(2,1)S(1)} %bitcast.32, bf16[384,512]{1,0:T(8,128)(2,1)S(1)} %constant_dynamic-slice_fusion.refs_0_, ...), custom_call_target="tpu_custom_call" | custom-call | bytes 1048576 | tf_op jit(solution)/shard_map/pallas_call | solution.py:24
  85.0 9.4 %all_to_all.10 = bf16[8,8,512]{2,1,0:T(8,128)(2,1)S(1)} all-to-all(bf16[8,8,512]{2,1,0:T(8,128)(2,1)S(1)} %bitcast.31), channel_id=1, replica_groups=mesh['segment'=2,'win'=4,'mp'=4] {'segment','win'}, dimensions={0} | all-to-all | bytes 131072 | tf_op jit(solution)/shard_map/all_to_all | solution.py:311
  94.4 0.6 log1p.9
  (33 shorter events, 0.1 us)
Async XLA Ops:
  0.0 17.0 %copy-start = (bf16[384,1024]{1,0:T(8,128)(2,1)S(1)}, bf16[384,1024]{1,0:T(8,128)(2,1)}, u32[]{:S(2)}) copy-start(bf16[384,1024]{1,0:T(8,128)(2,1)} %param.13) | copy-start | bytes 2359300
  0.0 17.0 %copy-start.1 = (bf16[384,5,384]{2,0,1:T(8,128)(2,1)S(1)}, bf16[384,5,384]{2,0,1:T(8,128)(2,1)}, u32[]{:S(2)}) copy-start(bf16[384,5,384]{2,0,1:T(8,128)(2,1)} %param.9) | copy-start | bytes 4423684
  0.1 1.3 %copy-start.2 = (bf16[1,1536,256]{2,1,0:T(8,128)(2,1)S(1)}, bf16[1,1536,256]{2,1,0:T(8,128)(2,1)}, u32[]{:S(2)}) copy-start(bf16[1,1536,256]{2,1,0:T(8,128)(2,1)} %param.8) | copy-start | bytes 2359300
  2.2 9.1 %copy-start.5 = (bf16[144,384]{1,0:T(8,128)(2,1)}, bf16[144,384]{1,0:T(8,128)(2,1)S(1)}, u32[]{:S(2)}) copy-start(bf16[144,384]{1,0:T(8,128)(2,1)S(1)} %get-tuple-element.13.x_ref) | copy-start | bytes 331780
  2.2 10.1 %copy-start.7 = (bf16[128,384]{1,0:T(8,128)(2,1)}, bf16[128,384]{1,0:T(8,128)(2,1)S(1)}, u32[]{:S(2)}) copy-start(bf16[128,384]{1,0:T(8,128)(2,1)S(1)} %get-tuple-element.12) | copy-start | bytes 294916
  2.2 9.1 %collective-permute-start = (bf16[144,384]{1,0:T(8,128)(2,1)S(1)}, bf16[144,384]{1,0:T(8,128)(2,1)S(1)}, u32[]{:S(2)}, u32[]{:S(2)}) collective-permute-start(bf16[144,384]{1,0:T(8,128)(2,1)S(1)} %get-tuple-element.14), channel_id=1, source_target_pairs={{0,4},{1,13},{2,6},{3,15},{4,8},{5,1},{6,10},{7,3},{8,12},{9,5},{1... | collective-permute-start | bytes 331784 | tf_op jit(solution)/shard_map/ppermute | solution.py:254
  5.3 11.1 %collective-permute-start.4 = (bf16[80,384]{1,0:T(8,128)(2,1)S(1)}, bf16[80,384]{1,0:T(8,128)(2,1)}, u32[]{:S(2)}, u32[]{:S(2)}) collective-permute-start(bf16[80,384]{1,0:T(8,128)(2,1)S(1)} %get-tuple-element.15), channel_id=1, source_target_pairs={{0,8},{1,9},{2,10},{3,11},{4,12},{5,13},{6,14},{7,15},{8,0},{9,1},... | collective-permute-start | bytes 184328 | tf_op jit(solution)/shard_map/ppermute | solution.py:254
  7.9 1.0 %copy-start.3 = (bf16[384,640]{1,0:T(8,128)(2,1)S(1)}, bf16[384,640]{1,0:T(8,128)(2,1)}, u32[]{:S(2)}) copy-start(bf16[384,640]{1,0:T(8,128)(2,1)} %refs_0_.1) | copy-start | bytes 1474564
  8.9 1.0 %copy-start.4 = (bf16[384,384]{1,0:T(8,128)(2,1)S(1)}, bf16[384,384]{1,0:T(8,128)(2,1)}, u32[]{:S(2)}) copy-start(bf16[384,384]{1,0:T(8,128)(2,1)} %refs_1_.1) | copy-start | bytes 884740
  11.3 13.9 %collective-permute-start.7 = (bf16[384,512]{1,0:T(8,128)(2,1)S(1)}, bf16[384,512]{1,0:T(8,128)(2,1)S(1)}, u32[]{:S(2)}, u32[]{:S(2)}) collective-permute-start(bf16[384,512]{1,0:T(8,128)(2,1)S(1)} %shard_map.87.refs_0_), channel_id=1, source_target_pairs={{0,4},{4,8},{8,12},{12,0},{1,5},{5,9},{9,13},{13,1},{2,6},{6,10},{... | collective-permute-start | bytes 1179656 | tf_op jit(solution)/shard_map/ppermute | solution.py:37
  12.3 19.9 %collective-permute-start.8 = (bf16[384,512]{1,0:T(8,128)(2,1)S(1)}, bf16[384,512]{1,0:T(8,128)(2,1)}, u32[]{:S(2)}, u32[]{:S(2)}) collective-permute-start(bf16[384,512]{1,0:T(8,128)(2,1)S(1)} %shard_map.87.refs_0_), channel_id=1, source_target_pairs={{0,12},{4,0},{8,4},{12,8},{1,13},{5,1},{9,5},{13,9},{2,14},{6,2},{... | collective-permute-start | bytes 1179656 | tf_op jit(solution)/shard_map/ppermute | solution.py:37
  16.5 3.1 %collective-permute-start.5 = (bf16[80,384]{1,0:T(8,128)(2,1)}, bf16[80,384]{1,0:T(8,128)(2,1)}, u32[]{:S(2)}, u32[]{:S(2)}) collective-permute-start(bf16[80,384]{1,0:T(8,128)(2,1)} %collective-permute-done.4.own_ref), channel_id=1, source_target_pairs={{0,1},{1,0},{2,3},{3,2},{4,5},{5,4},{6,7},{7,6},{8,9},{9,8},{10,11... | collective-permute-start | bytes 184328 | tf_op jit(solution)/shard_map/ppermute | solution.py:257
  16.5 5.0 %collective-permute-start.2 = (bf16[144,384]{1,0:T(8,128)(2,1)S(1)}, bf16[144,384]{1,0:T(8,128)(2,1)}, u32[]{:S(2)}, u32[]{:S(2)}) collective-permute-start(bf16[144,384]{1,0:T(8,128)(2,1)S(1)} %collective-permute-done.x_ref), channel_id=1, source_target_pairs={{0,1},{1,0},{2,3},{3,2},{4,5},{5,4},{6,7},{7,6},{8,9},{9,8},{10,11... | collective-permute-start | bytes 331784 | tf_op jit(solution)/shard_map/ppermute | solution.py:257
  17.0 0.9 copy-start.6
  18.8 15.1 %collective-permute-start.1 = (bf16[128,384]{1,0:T(8,128)(2,1)S(1)}, bf16[128,384]{1,0:T(8,128)(2,1)S(1)}, u32[]{:S(2)}, u32[]{:S(2)}) collective-permute-start(bf16[128,384]{1,0:T(8,128)(2,1)S(1)} %shard_map.84), channel_id=1, source_target_pairs={{0,12},{1,5},{2,14},{3,7},{4,0},{5,9},{6,2},{7,11},{8,4},{9,13},{1... | collective-permute-start | bytes 294920 | tf_op jit(solution)/shard_map/ppermute | solution.py:254
  20.9 19.3 %copy-start.8 = (bf16[128,384]{1,0:T(8,128)(2,1)S(1)}, bf16[128,384]{1,0:T(8,128)(2,1)}, u32[]{:S(2)}) copy-start(bf16[128,384]{1,0:T(8,128)(2,1)} %copy-done.7) | copy-start | bytes 294916
  20.9 19.3 %copy-start.12 = (f32[384]{0:T(512)S(1)}, f32[384]{0:T(512)}, u32[]{:S(2)}) copy-start(f32[384]{0:T(512)} %param.10) | copy-start | bytes 4612
  20.9 19.3 %collective-permute-start.6 = (bf16[128,384]{1,0:T(8,128)(2,1)S(1)}, bf16[128,384]{1,0:T(8,128)(2,1)S(1)}, u32[]{:S(2)}, u32[]{:S(2)}) collective-permute-start(bf16[128,384]{1,0:T(8,128)(2,1)S(1)} %shard_map.86), channel_id=1, source_target_pairs={{0,8},{1,9},{2,10},{3,11},{4,12},{5,13},{6,14},{7,15},{8,0},{9,1},... | collective-permute-start | bytes 294920 | tf_op jit(solution)/shard_map/ppermute | solution.py:254
  22.8 14.5 %collective-permute-start.3 = (bf16[128,384]{1,0:T(8,128)(2,1)S(1)}, bf16[128,384]{1,0:T(8,128)(2,1)S(1)}, u32[]{:S(2)}, u32[]{:S(2)}) collective-permute-start(bf16[128,384]{1,0:T(8,128)(2,1)S(1)} %shard_map.85), channel_id=1, source_target_pairs={{0,4},{1,13},{2,6},{3,15},{4,8},{5,1},{6,10},{7,3},{8,12},{9,5},{1... | collective-permute-start | bytes 294920 | tf_op jit(solution)/shard_map/ppermute | solution.py:254
  37.4 17.3 %collective-permute-start.9 = (bf16[384,512]{1,0:T(8,128)(2,1)S(1)}, bf16[384,512]{1,0:T(8,128)(2,1)S(1)}, u32[]{:S(2)}, u32[]{:S(2)}) collective-permute-start(bf16[384,512]{1,0:T(8,128)(2,1)S(1)} %select_select_fusion.1), channel_id=1, source_target_pairs={{0,8},{4,0},{8,12},{12,4},{1,9},{5,1},{9,13},{13,5},{2,10},{6,2},{... | collective-permute-start | bytes 1179656 | tf_op jit(solution)/shard_map/ppermute | solution.py:218
  40.3 21.9 %collective-permute-start.10 = (bf16[384,512]{1,0:T(8,128)(2,1)S(1)}, bf16[384,512]{1,0:T(8,128)(2,1)S(1)}, u32[]{:S(2)}, u32[]{:S(2)}) collective-permute-start(bf16[384,512]{1,0:T(8,128)(2,1)S(1)} %constant_dynamic-slice_fusion.refs_0_), channel_id=1, source_target_pairs={{0,4},{4,8},{8,12},{12,0},{1,5},{5,9},{9,13},{13,1},{2,6},{6,10},{... | collective-permute-start | bytes 1179656 | tf_op jit(solution)/shard_map/ppermute | solution.py:37
  40.4 25.3 %collective-permute-start.11 = (bf16[384,512]{1,0:T(8,128)(2,1)S(1)}, bf16[384,512]{1,0:T(8,128)(2,1)S(1)}, u32[]{:S(2)}, u32[]{:S(2)}) collective-permute-start(bf16[384,512]{1,0:T(8,128)(2,1)S(1)} %constant_dynamic-slice_fusion.refs_0_), channel_id=1, source_target_pairs={{0,12},{4,0},{8,4},{12,8},{1,13},{5,1},{9,5},{13,9},{2,14},{6,2},{... | collective-permute-start | bytes 1179656 | tf_op jit(solution)/shard_map/ppermute | solution.py:37
  58.1 3.7 %copy-start.9 = (s32[8,8]{1,0:T(8,128)S(1)}, s32[8,8]{1,0:T(8,128)}, u32[]{:S(2)}) copy-start(s32[8,8]{1,0:T(8,128)} %get-tuple-element.19) | copy-start | bytes 772
  58.1 3.7 %copy-start.13 = (f32[1024]{0:T(1024)S(1)}, f32[1024]{0:T(1024)}, u32[]{:S(2)}) copy-start(f32[1024]{0:T(1024)} %param.14) | copy-start | bytes 12292
  58.1 3.8 %copy-start.10 = (s32[8,8]{1,0:T(8,128)S(1)}, s32[8,8]{1,0:T(8,128)}, u32[]{:S(2)}) copy-start(s32[8,8]{1,0:T(8,128)} %get-tuple-element.20) | copy-start | bytes 772
  58.1 3.8 %copy-start.11 = (s32[8,8]{1,0:T(8,128)S(1)}, s32[8,8]{1,0:T(8,128)}, u32[]{:S(2)}) copy-start(s32[8,8]{1,0:T(8,128)} %get-tuple-element.21) | copy-start | bytes 772
  58.1 15.3 %all-to-all-start = ((bf16[8,128,384]{2,1,0:T(8,128)(2,1)}), bf16[8,128,384]{2,1,0:T(8,128)(2,1)S(1)}, u32[]{:S(2)}, u32[]{:S(2)}) async-start(bf16[8,128,384]{2,1,0:T(8,128)(2,1)} %shard_map.88), calls=%async_computation | async-start | bytes 1572864 | tf_op jit(solution)/shard_map/all_to_all | solution.py:297
  66.5 17.3 %collective-permute-start.12 = (bf16[384,512]{1,0:T(8,128)(2,1)}, bf16[384,512]{1,0:T(8,128)(2,1)S(1)}, u32[]{:S(2)}, u32[]{:S(2)}) collective-permute-start(bf16[384,512]{1,0:T(8,128)(2,1)} %select_select_fusion), channel_id=1, source_target_pairs={{0,8},{4,0},{8,12},{12,4},{1,9},{5,1},{9,13},{13,5},{2,10},{6,2},{... | collective-permute-start | bytes 1179656 | tf_op jit(solution)/shard_map/ppermute | solution.py:218

commit v5 on v4

--- a/solution.py
+++ b/solution.py
@@ -123,11 +123,10 @@
     return total
 
 
-def attention_kernel(segments, heads, win_ref, x_ref, *refs):
-    *pieces, o_ref = refs
-    models = o_ref.shape[0] // segments
-    bins = o_ref.shape[1]
-    width = o_ref.shape[2]
+def attention_kernel(segments, heads, place_ref, win_ref, x_ref, *refs):
+    *pieces, keep_ref, give_ref = refs
+    models = x_ref.shape[0] // segments
+    bins, width = x_ref.shape[1:]
     rows = contract_blocks(x_ref, segments, win_ref, pieces, slice(0, heads * SPAN)).astype(BF16)
     outputs = []
     for head in range(heads):
@@ -140,20 +139,41 @@
         probs = (weights / jnp.sum(weights, axis=1, keepdims=True)).astype(BF16)
         outputs.append(jnp.dot(probs, value, preferred_element_type=F32).astype(BF16))
     att = jnp.concatenate(outputs, axis=1)
+    odd = lax.rem(place_ref[2], 2)
+
+    def put(segment, block, value):
+        at = segment * (models // 2) + lax.div(block, 2)
+
+        @pl.when(lax.rem(block, 2) == odd)
+        def _():
+            keep_ref[at] = value
+
+        @pl.when(lax.rem(block, 2) != odd)
+        def _():
+            give_ref[at] = value
+
     for by, piece in enumerate(pieces):
         term = lax.dot_general(
             att,
             piece[:, heads * SPAN :],
             (((1,), (1,)), ((), ())),
             preferred_element_type=F32,
-        ).astype(o_ref.dtype)
+        ).astype(BF16)
         for s in range(segments):
             own = term[s * bins : (s + 1) * bins]
             if len(pieces) > 1:
-                o_ref[s * models + block_of(win_ref, by, len(pieces))] = own
+                put(s, block_of(win_ref, by, len(pieces)), own)
             else:
                 for m in range(models):
-                    o_ref[s * models + m] = own[:, m * width : (m + 1) * width]
+                    put(s, jnp.int32(m), own[:, m * width : (m + 1) * width])
+
+
+def pair_kernel(place_ref, keep_ref, got_ref, *out_refs):
+    segment, chip = place_ref[0], lax.div(place_ref[2], 2)
+    for across, out in enumerate(out_refs):
+        over_segment, over_mp = across % 2, across // 2
+        at = (1 - segment if over_segment else segment) * 2 + (1 - chip if over_mp else chip)
+        out[...] = (keep_ref[at].astype(F32) + got_ref[at].astype(F32)).astype(out.dtype)
 
 
 def head_kernel(segments, win_ref, x_ref, b_ref, counts_ref, *refs):
@@ -234,6 +254,9 @@
             flops=2 * bins * out_cols * row_count * tap_count,
         )
 
+    def swapped(x):
+        return lax.ppermute(x, "mp", [(m, m ^ 1) for m in range(models)])
+
     if stepwise:
         block = jax.ShapeDtypeStruct((bins + 2 * reach, row_count), BF16)
         part = jax.ShapeDtypeStruct(((bins + 2 * reach) // 32 * 16 + 16, row_count), BF16)
@@ -252,9 +275,6 @@
                 for m in range(models)
             ]
             return lax.ppermute(x, ("win", "mp"), pairs)
-
-        def swapped(x):
-            return lax.ppermute(x, "mp", [(m, m ^ 1) for m in range(models)])
 
         next_in, part_in = turned_by(next_rows, 1, -1), turned_by(part_rows, 2, 2)
         arrived = [next_in, part_in]
@@ -287,14 +307,31 @@
     head_pieces = gathered(head_own, conv_out, ())
     all_chan = lax.all_gather(conv_out, plane, axis=0)
 
-    partial = call_kernel(
+    half = jax.ShapeDtypeStruct((segments * models // 2, bins, out_cols), BF16)
+    keep, give = call_kernel(
         functools.partial(attention_kernel, segments, heads),
-        jax.ShapeDtypeStruct(all_chan.shape, BF16),
+        [half, half],
+        place,
         win_ref,
         all_chan,
         *attention_pieces,
     )
-    summed = lax.all_to_all(partial, plane, 0, 0, tiled=True).astype(F32).sum(axis=0)
+    one = jax.ShapeDtypeStruct((bins, out_cols), BF16)
+    own_sum, *sent_sums = call_kernel(
+        pair_kernel,
+        [jax.ShapeDtypeStruct(one.shape, F32), one, one, one],
+        place,
+        keep,
+        swapped(give),
+    )
+    summed = own_sum
+    for across, x in enumerate(sent_sums, 1):
+        pairs = [
+            (s * models + m, (s ^ across % 2) * models + (m ^ across // 2 * 2))
+            for s in range(segments)
+            for m in range(models)
+        ]
+        summed = summed + lax.ppermute(x, plane, pairs).astype(F32)
     resid = (conv_out.astype(F32) + summed).astype(BF16)
     all_resid = lax.all_gather(resid, plane, axis=0)
 

time: 95.5 us -> 92.2 us (0.965)
  waiting for transfers between devices: 21.3 us -> 16.5 us
  blocking collectives: 30.2 us -> 31.6 us
    all_to_all x1 -> x0, waiting for transfers between devices: 4.68 us -> none  [local(): lax.all_to_all(partial, plane, 0, 0, tiled=True).astype(F32).sum(axis=0)]
    all_to_all x1 -> x0, starting transfers between devices: 3.69 us -> none  [local(): lax.all_to_all(partial, plane, 0, 0, tiled=True).astype(F32).sum(axis=0)]
    ppermute x0 -> x3, starting transfers between devices: none -> 3.55 us  [local(): summed = summed + lax.ppermute(x, plane, pairs).astype(F32)]
    ppermute x4, waiting for transfers between devices: 10.8 us -> 8.97 us  [shifted(): return lax.ppermute(x, axis, [(i, (i + by) % size) for i in range(size)])]
    all_to_all x1, blocking collectives: 9.37 us -> 10.8 us  [local(): lax.all_to_all(sums.reshape(owners, GENE_DEV, track_cols), ('segment', 'w...]
    pallas_call x8 -> x9, Pallas kernels: 9.65 us -> 10.3 us  [call_kernel(): pl.pallas_call(body, out_shape=out_shape, in_specs=[scalars if x.dtype ==...]
  transfers between devices with their start and end apart: 14 -> 17, of which waited for: 7 -> 9; matrix products, arithmetic and copies ran while one was open for 3% -> 2% of each run, Pallas kernels for 8% -> 9%
where the time goes in v5:
time: 92.2 us; the launch traced here: 91.8 us
  blocking collectives  31.6 us (34%)
  starting transfers between devices  26.1 us (28%)
  waiting for transfers between devices  16.5 us (18%)
  Pallas kernels  10.3 us (11%)
  local copies, waits for them, and re-layouts  6.26 us (7%)
    all_to_all x1, blocking collectives, local(): lax.all_to_all(sums.reshape(owners, GENE_DEV, track_cols), ('segment', 'w...  10.8 us
    all_gather x1, blocking collectives, local(): all_chan = lax.all_gather(conv_out, plane, axis=0)  10.4 us
    all_gather x1, blocking collectives, local(): all_resid = lax.all_gather(resid, plane, axis=0)  10.4 us
    pallas_call x9, Pallas kernels, call_kernel(): pl.pallas_call(body, out_shape=out_shape, in_specs=[scalars if x.dtype ==...  10.3 us
    ppermute x5, starting transfers between devices, turned_by(): return lax.ppermute(x, ('win', 'mp'), pairs)  9 us
    ppermute x4, waiting for transfers between devices, shifted(): return lax.ppermute(x, axis, [(i, (i + by) % size) for i in range(size)])  8.97 us
    ppermute x4, starting transfers between devices, shifted(): return lax.ppermute(x, axis, [(i, (i + by) % size) for i in range(size)])  7.69 us
    ppermute x5, waiting for transfers between devices, turned_by(): return lax.ppermute(x, ('win', 'mp'), pairs)  5.77 us
  transfers between devices with their start and end apart: 17, of which 9 were waited for; matrix products, arithmetic and copies ran while one was open for 2% of the time, Pallas kernels for 9%

profile of v5, /device:TPU:0, one launch (start us, length us, event | category | flops | bytes accessed | tf_op | source)
XLA Modules:
  0.0 91.8 jit_solution(16699625550835713387)
XLA Ops:
  0.0 0.1 pad_add_fusion.place_ref
  0.1 1.3 %copy-done.2 = bf16[1,1536,256]{2,1,0:T(8,128)(2,1)S(1)} copy-done((bf16[1,1536,256]{2,1,0:T(8,128)(2,1)S(1)}, bf16[1,1536,256]{2,1,0:T(8,128)(2,1)}, u32[]{:S(2)}) %copy-start.2) | copy-done | bytes 786456
  1.4 0.9 shard_map.82
  2.2 3.1 %collective-permute-start = (bf16[144,384]{1,0:T(8,128)(2,1)S(1)}, bf16[144,384]{1,0:T(8,128)(2,1)S(1)}, u32[]{:S(2)}, u32[]{:S(2)}) collective-permute-start(bf16[144,384]{1,0:T(8,128)(2,1)S(1)} %get-tuple-element.20), channel_id=1, source_target_pairs={{0,4},{1,13},{2,6},{3,15},{4,8},{5,1},{6,10},{7,3},{8,12},{9,5},{1... | collective-permute-start | bytes 331784 | tf_op jit(solution)/shard_map/ppermute | solution.py:277
  5.3 2.6 %collective-permute-start.4 = (bf16[80,384]{1,0:T(8,128)(2,1)S(1)}, bf16[80,384]{1,0:T(8,128)(2,1)}, u32[]{:S(2)}, u32[]{:S(2)}) collective-permute-start(bf16[80,384]{1,0:T(8,128)(2,1)S(1)} %get-tuple-element.21), channel_id=1, source_target_pairs={{0,8},{1,9},{2,10},{3,11},{4,12},{5,13},{6,14},{7,15},{8,0},{9,1},... | collective-permute-start | bytes 184328 | tf_op jit(solution)/shard_map/ppermute | solution.py:277
  7.9 1.0 %copy-done.3 = bf16[384,640]{1,0:T(8,128)(2,1)S(1)} copy-done((bf16[384,640]{1,0:T(8,128)(2,1)S(1)}, bf16[384,640]{1,0:T(8,128)(2,1)}, u32[]{:S(2)}) %copy-start.3) | copy-done | bytes 491544
  8.9 1.0 %copy-done.4 = bf16[384,384]{1,0:T(8,128)(2,1)S(1)} copy-done((bf16[384,384]{1,0:T(8,128)(2,1)S(1)}, bf16[384,384]{1,0:T(8,128)(2,1)}, u32[]{:S(2)}) %copy-start.4) | copy-done | bytes 294936
  9.9 0.7 shard_map.87.refs_0_
  10.6 0.7 collective-permute-done.x_ref
  11.3 1.0 %collective-permute-start.7 = (bf16[384,512]{1,0:T(8,128)(2,1)S(1)}, bf16[384,512]{1,0:T(8,128)(2,1)S(1)}, u32[]{:S(2)}, u32[]{:S(2)}) collective-permute-start(bf16[384,512]{1,0:T(8,128)(2,1)S(1)} %shard_map.87.refs_0_), channel_id=1, source_target_pairs={{0,4},{4,8},{8,12},{12,0},{1,5},{5,9},{9,13},{13,1},{2,6},{6,10},{... | collective-permute-start | bytes 1179656 | tf_op jit(solution)/shard_map/ppermute | solution.py:37
  12.3 2.8 %collective-permute-start.8 = (bf16[384,512]{1,0:T(8,128)(2,1)S(1)}, bf16[384,512]{1,0:T(8,128)(2,1)}, u32[]{:S(2)}, u32[]{:S(2)}) collective-permute-start(bf16[384,512]{1,0:T(8,128)(2,1)S(1)} %shard_map.87.refs_0_), channel_id=1, source_target_pairs={{0,12},{4,0},{8,4},{12,8},{1,13},{5,1},{9,5},{13,9},{2,14},{6,2},{... | collective-permute-start | bytes 1179656 | tf_op jit(solution)/shard_map/ppermute | solution.py:37
  15.1 1.3 %slice_bitcast_fusion.2 = (s32[8,8]{1,0:T(8,128)}, s32[8,8]{1,0:T(8,128)}, s32[8,8]{1,0:T(8,128)}) fusion(s32[3,1,8,8]{3,2,1,0:T(8,128)} %param.15), kind=kLoop, calls=%fused_computation.22 | loop fusion | bytes 1536 | tf_op jit(solution)/shard_map/eq | solution.py:191
  16.5 0.5 collective-permute-start.2
  17.0 0.9 copy-done.6
  17.9 0.5 shard_map.83
  18.4 0.5 shard_map.84
  18.9 0.7 collective-permute-start.1
  19.6 1.3 %shard_map.86 = bf16[128,384]{1,0:T(8,128)(2,1)S(1)} custom-call(s32[3]{0:T(128)S(1)} %pad_add_fusion.place_ref, bf16[80,384]{1,0:T(8,128)(2,1)} %collective-permute-done.4.own_ref, bf16[80,384]{1,0:T(8,128)(2,1)} %collective-permute-done.5.other_ref, bf16[5,384,384]{2,1,0:T(8,128)(2,1)S(1)} %bitcast.26), custom_call_target="tpu_custom_call" | custom-call | flops 188743680 | bytes 1048576 | tf_op jit(solution)/shard_map/pallas_call | solution.py:24
  20.9 0.6 collective-permute-start.6
  21.5 1.3 %shard_map.85 = bf16[128,384]{1,0:T(8,128)(2,1)S(1)} custom-call(bf16[144,384]{1,0:T(8,128)(2,1)} %collective-permute-done.2.x_ref, bf16[5,384,384]{2,1,0:T(8,128)(2,1)S(1)} %bitcast.27), custom_call_target="tpu_custom_call" | custom-call | flops 188743680 | bytes 1048576 | tf_op jit(solution)/shard_map/pallas_call | solution.py:24
  22.8 2.1 %collective-permute-start.3 = (bf16[128,384]{1,0:T(8,128)(2,1)S(1)}, bf16[128,384]{1,0:T(8,128)(2,1)S(1)}, u32[]{:S(2)}, u32[]{:S(2)}) collective-permute-start(bf16[128,384]{1,0:T(8,128)(2,1)S(1)} %shard_map.85), channel_id=1, source_target_pairs={{0,4},{1,13},{2,6},{3,15},{4,8},{5,1},{6,10},{7,3},{8,12},{9,5},{1... | collective-permute-start | bytes 294920 | tf_op jit(solution)/shard_map/ppermute | solution.py:277
  24.9 0.3 collective-permute-done.7.refs_1_
  25.2 7.1 %collective-permute-done.8.refs_3_ = bf16[384,512]{1,0:T(8,128)(2,1)} collective-permute-done((bf16[384,512]{1,0:T(8,128)(2,1)S(1)}, bf16[384,512]{1,0:T(8,128)(2,1)}, u32[]{:S(2)}, u32[]{:S(2)}) %collective-permute-start.8) | collective-permute-done | bytes 393248 | tf_op jit(solution)/shard_map/ppermute | solution.py:37
  32.3 1.6 %collective-permute-done.1 = bf16[128,384]{1,0:T(8,128)(2,1)S(1)} collective-permute-done((bf16[128,384]{1,0:T(8,128)(2,1)S(1)}, bf16[128,384]{1,0:T(8,128)(2,1)S(1)}, u32[]{:S(2)}, u32[]{:S(2)}) %collective-permute-start.1) | collective-permute-done | bytes 98336 | tf_op jit(solution)/shard_map/ppermute | solution.py:277
  34.0 3.4 %collective-permute-done.3 = bf16[128,384]{1,0:T(8,128)(2,1)S(1)} collective-permute-done((bf16[128,384]{1,0:T(8,128)(2,1)S(1)}, bf16[128,384]{1,0:T(8,128)(2,1)S(1)}, u32[]{:S(2)}, u32[]{:S(2)}) %collective-permute-start.3) | collective-permute-done | bytes 98336 | tf_op jit(solution)/shard_map/ppermute | solution.py:277
  37.4 2.8 %collective-permute-start.9 = (bf16[384,512]{1,0:T(8,128)(2,1)S(1)}, bf16[384,512]{1,0:T(8,128)(2,1)S(1)}, u32[]{:S(2)}, u32[]{:S(2)}) collective-permute-start(bf16[384,512]{1,0:T(8,128)(2,1)S(1)} %select_select_fusion.1), channel_id=1, source_target_pairs={{0,8},{4,0},{8,12},{12,4},{1,9},{5,1},{9,13},{13,5},{2,10},{6,2},{... | collective-permute-start | bytes 1179656 | tf_op jit(solution)/shard_map/ppermute | solution.py:238
  40.2 0.1 fusion.8
  40.4 0.1 collective-permute-start.14
  40.4 3.8 %collective-permute-start.15 = (bf16[384,512]{1,0:T(8,128)(2,1)S(1)}, bf16[384,512]{1,0:T(8,128)(2,1)S(1)}, u32[]{:S(2)}, u32[]{:S(2)}) collective-permute-start(bf16[384,512]{1,0:T(8,128)(2,1)S(1)} %constant_dynamic-slice_fusion.refs_0_), channel_id=1, source_target_pairs={{0,12},{4,0},{8,4},{12,8},{1,13},{5,1},{9,5},{13,9},{2,14},{6,2},{... | collective-permute-start | bytes 1179656 | tf_op jit(solution)/shard_map/ppermute | solution.py:37
  44.3 10.4 %all-gather = bf16[1024,384]{1,0:T(8,128)(2,1)S(1)} all-gather(bf16[128,384]{1,0:T(8,128)(2,1)S(1)} %fusion.8), channel_id=2, replica_groups=mesh['segment'=2,'win'=4,'mp'=4] {'segment','mp'}, dimensions={0}, use_global_device_ids=true | all-gather | bytes 884736 | tf_op jit(solution)/shard_map/all_gather | solution.py:308
  54.7 3.4 %shard_map.88 = (bf16[4,128,384]{2,1,0:T(8,128)(2,1)S(1)}, bf16[4,128,384]{2,1,0:T(8,128)(2,1)S(1)}) custom-call(s32[3]{0:T(128)S(1)} %pad_add_fusion.place_ref, s32[1]{0:T(128)} %bitcast.win_ref, bf16[8,128,384]{2,1,0:T(8,128)(2,1)S(1)} %bitcast.29, bf16[384,512]{1,0:T(8,128)(2,1)S(1)} %shard_map.87.refs_0_, ...), custom_call_target="tpu_custom_call" | custom-call | bytes 1048576 | tf_op jit(solution)/shard_map/pallas_call | solution.py:24
  58.1 0.4 collective-permute-start.10
  58.6 0.1 dynamic_slice.6
  58.6 0.1 fusion.9
  58.7 0.2 convert_reduce_fusion
  59.0 0.9 %collective-permute-done.10.got_ref = bf16[4,128,384]{2,1,0:T(8,128)(2,1)S(1)} collective-permute-done((bf16[4,128,384]{2,1,0:T(8,128)(2,1)S(1)}, bf16[4,128,384]{2,1,0:T(8,128)(2,1)S(1)}, u32[]{:S(2)}, u32[]{:S(2)}) %collective-permute-start.10) | collective-permute-done | bytes 393248 | tf_op jit(solution)/shard_map/ppermute | solution.py:258
  59.9 0.6 shard_map.89
  60.6 1.5 %collective-permute-start.13 = (bf16[128,384]{1,0:T(8,128)(2,1)S(1)}, bf16[128,384]{1,0:T(8,128)(2,1)S(1)}, u32[]{:S(2)}, u32[]{:S(2)}) collective-permute-start(bf16[128,384]{1,0:T(8,128)(2,1)S(1)} %get-tuple-element.29), channel_id=1, source_target_pairs={{0,18},{1,19},{2,16},{3,17},{16,2},{17,3},{18,0},{19,1},{4,22},{5,... | collective-permute-start | bytes 294920 | tf_op jit(solution)/shard_map/ppermute | solution.py:334
  62.1 1.5 %collective-permute-start.12 = (bf16[128,384]{1,0:T(8,128)(2,1)S(1)}, bf16[128,384]{1,0:T(8,128)(2,1)S(1)}, u32[]{:S(2)}, u32[]{:S(2)}) collective-permute-start(bf16[128,384]{1,0:T(8,128)(2,1)S(1)} %get-tuple-element.28), channel_id=1, source_target_pairs={{0,2},{1,3},{2,0},{3,1},{16,18},{17,19},{18,16},{19,17},{4,6},{5,7... | collective-permute-start | bytes 294920 | tf_op jit(solution)/shard_map/ppermute | solution.py:334
  63.6 0.5 collective-permute-start.11
  64.1 1.6 %collective-permute-done.15.refs_3_ = bf16[384,512]{1,0:T(8,128)(2,1)S(1)} collective-permute-done((bf16[384,512]{1,0:T(8,128)(2,1)S(1)}, bf16[384,512]{1,0:T(8,128)(2,1)S(1)}, u32[]{:S(2)}, u32[]{:S(2)}) %collective-permute-start.15) | collective-permute-done | bytes 393248 | tf_op jit(solution)/shard_map/ppermute | solution.py:37
  65.8 2.1 %collective-permute-start.16 = (bf16[384,512]{1,0:T(8,128)(2,1)S(1)}, bf16[384,512]{1,0:T(8,128)(2,1)S(1)}, u32[]{:S(2)}, u32[]{:S(2)}) collective-permute-start(bf16[384,512]{1,0:T(8,128)(2,1)S(1)} %select_select_fusion), channel_id=1, source_target_pairs={{0,8},{4,0},{8,12},{12,4},{1,9},{5,1},{9,13},{13,5},{2,10},{6,2},{... | collective-permute-start | bytes 1179656 | tf_op jit(solution)/shard_map/ppermute | solution.py:238
  67.9 0.7 collective-permute-done.12
  68.7 0.1 add_convert_fusion
  68.8 10.4 %all-gather.1 = bf16[1024,384]{1,0:T(8,128)(2,1)S(1)} all-gather(bf16[128,384]{1,0:T(8,128)(2,1)S(1)} %add_convert_fusion), channel_id=3, replica_groups=mesh['segment'=2,'win'=4,'mp'=4] {'segment','mp'}, dimensions={0}, use_global_device_ids=true | all-gather | bytes 884736 | tf_op jit(solution)/shard_map/all_gather | solution.py:336
  79.2 1.1 %shard_map.90 = bf16[64,512]{1,0:T(8,128)(2,1)S(1)} custom-call(s32[1]{0:T(128)} %bitcast.win_ref, bf16[8,128,384]{2,1,0:T(8,128)(2,1)S(1)} %bitcast.28, f32[1,512]{1,0:T(1,128)S(1)} %bitcast.33, bf16[64,256]{1,0:T(8,128)(2,1)S(1)} %bitcast.32, bf16[384,512]{1,0:T(8,128)(2,1)S(1)} %constant_dynamic-slice_fusion.refs_0_, ...), custom_call_target="tpu_custom_call" | custom-call | bytes 1048576 | tf_op jit(solution)/shard_map/pallas_call | solution.py:24
  80.3 10.8 %all_to_all.5 = bf16[8,8,512]{2,1,0:T(8,128)(2,1)S(1)} all-to-all(bf16[8,8,512]{2,1,0:T(8,128)(2,1)S(1)} %bitcast.31), channel_id=1, replica_groups=mesh['segment'=2,'win'=4,'mp'=4] {'segment','win'}, dimensions={0} | all-to-all | bytes 131072 | tf_op jit(solution)/shard_map/all_to_all | solution.py:348
  91.1 0.6 log1p.9
  (39 shorter events, 0.3 us)
Async XLA Ops:
  0.0 17.0 %copy-start = (bf16[384,1024]{1,0:T(8,128)(2,1)S(1)}, bf16[384,1024]{1,0:T(8,128)(2,1)}, u32[]{:S(2)}) copy-start(bf16[384,1024]{1,0:T(8,128)(2,1)} %param.13) | copy-start | bytes 2359300
  0.0 17.0 %copy-start.1 = (bf16[384,5,384]{2,0,1:T(8,128)(2,1)S(1)}, bf16[384,5,384]{2,0,1:T(8,128)(2,1)}, u32[]{:S(2)}) copy-start(bf16[384,5,384]{2,0,1:T(8,128)(2,1)} %param.9) | copy-start | bytes 4423684
  0.1 1.3 %copy-start.2 = (bf16[1,1536,256]{2,1,0:T(8,128)(2,1)S(1)}, bf16[1,1536,256]{2,1,0:T(8,128)(2,1)}, u32[]{:S(2)}) copy-start(bf16[1,1536,256]{2,1,0:T(8,128)(2,1)} %param.8) | copy-start | bytes 2359300
  2.2 9.1 %copy-start.5 = (bf16[144,384]{1,0:T(8,128)(2,1)}, bf16[144,384]{1,0:T(8,128)(2,1)S(1)}, u32[]{:S(2)}) copy-start(bf16[144,384]{1,0:T(8,128)(2,1)S(1)} %get-tuple-element.19.x_ref) | copy-start | bytes 331780
  2.2 10.1 %copy-start.7 = (bf16[128,384]{1,0:T(8,128)(2,1)}, bf16[128,384]{1,0:T(8,128)(2,1)S(1)}, u32[]{:S(2)}) copy-start(bf16[128,384]{1,0:T(8,128)(2,1)S(1)} %get-tuple-element.18) | copy-start | bytes 294916
  2.2 9.1 %collective-permute-start = (bf16[144,384]{1,0:T(8,128)(2,1)S(1)}, bf16[144,384]{1,0:T(8,128)(2,1)S(1)}, u32[]{:S(2)}, u32[]{:S(2)}) collective-permute-start(bf16[144,384]{1,0:T(8,128)(2,1)S(1)} %get-tuple-element.20), channel_id=1, source_target_pairs={{0,4},{1,13},{2,6},{3,15},{4,8},{5,1},{6,10},{7,3},{8,12},{9,5},{1... | collective-permute-start | bytes 331784 | tf_op jit(solution)/shard_map/ppermute | solution.py:277
  5.3 11.2 %collective-permute-start.4 = (bf16[80,384]{1,0:T(8,128)(2,1)S(1)}, bf16[80,384]{1,0:T(8,128)(2,1)}, u32[]{:S(2)}, u32[]{:S(2)}) collective-permute-start(bf16[80,384]{1,0:T(8,128)(2,1)S(1)} %get-tuple-element.21), channel_id=1, source_target_pairs={{0,8},{1,9},{2,10},{3,11},{4,12},{5,13},{6,14},{7,15},{8,0},{9,1},... | collective-permute-start | bytes 184328 | tf_op jit(solution)/shard_map/ppermute | solution.py:277
  7.9 1.0 %copy-start.3 = (bf16[384,640]{1,0:T(8,128)(2,1)S(1)}, bf16[384,640]{1,0:T(8,128)(2,1)}, u32[]{:S(2)}) copy-start(bf16[384,640]{1,0:T(8,128)(2,1)} %refs_0_.1) | copy-start | bytes 1474564
  8.9 1.0 %copy-start.4 = (bf16[384,384]{1,0:T(8,128)(2,1)S(1)}, bf16[384,384]{1,0:T(8,128)(2,1)}, u32[]{:S(2)}) copy-start(bf16[384,384]{1,0:T(8,128)(2,1)} %refs_1_.1) | copy-start | bytes 884740
  11.3 13.9 %collective-permute-start.7 = (bf16[384,512]{1,0:T(8,128)(2,1)S(1)}, bf16[384,512]{1,0:T(8,128)(2,1)S(1)}, u32[]{:S(2)}, u32[]{:S(2)}) collective-permute-start(bf16[384,512]{1,0:T(8,128)(2,1)S(1)} %shard_map.87.refs_0_), channel_id=1, source_target_pairs={{0,4},{4,8},{8,12},{12,0},{1,5},{5,9},{9,13},{13,1},{2,6},{6,10},{... | collective-permute-start | bytes 1179656 | tf_op jit(solution)/shard_map/ppermute | solution.py:37
  12.3 19.9 %collective-permute-start.8 = (bf16[384,512]{1,0:T(8,128)(2,1)S(1)}, bf16[384,512]{1,0:T(8,128)(2,1)}, u32[]{:S(2)}, u32[]{:S(2)}) collective-permute-start(bf16[384,512]{1,0:T(8,128)(2,1)S(1)} %shard_map.87.refs_0_), channel_id=1, source_target_pairs={{0,12},{4,0},{8,4},{12,8},{1,13},{5,1},{9,5},{13,9},{2,14},{6,2},{... | collective-permute-start | bytes 1179656 | tf_op jit(solution)/shard_map/ppermute | solution.py:37
  16.5 3.1 %collective-permute-start.5 = (bf16[80,384]{1,0:T(8,128)(2,1)}, bf16[80,384]{1,0:T(8,128)(2,1)}, u32[]{:S(2)}, u32[]{:S(2)}) collective-permute-start(bf16[80,384]{1,0:T(8,128)(2,1)} %collective-permute-done.4.own_ref), channel_id=1, source_target_pairs={{0,1},{1,0},{2,3},{3,2},{4,5},{5,4},{6,7},{7,6},{8,9},{9,8},{10,11... | collective-permute-start | bytes 184328 | tf_op jit(solution)/shard_map/ppermute | solution.py:258
  16.5 5.0 %collective-permute-start.2 = (bf16[144,384]{1,0:T(8,128)(2,1)S(1)}, bf16[144,384]{1,0:T(8,128)(2,1)}, u32[]{:S(2)}, u32[]{:S(2)}) collective-permute-start(bf16[144,384]{1,0:T(8,128)(2,1)S(1)} %collective-permute-done.x_ref), channel_id=1, source_target_pairs={{0,1},{1,0},{2,3},{3,2},{4,5},{5,4},{6,7},{7,6},{8,9},{9,8},{10,11... | collective-permute-start | bytes 331784 | tf_op jit(solution)/shard_map/ppermute | solution.py:258
  17.0 0.9 copy-start.6
  18.9 15.1 %collective-permute-start.1 = (bf16[128,384]{1,0:T(8,128)(2,1)S(1)}, bf16[128,384]{1,0:T(8,128)(2,1)S(1)}, u32[]{:S(2)}, u32[]{:S(2)}) collective-permute-start(bf16[128,384]{1,0:T(8,128)(2,1)S(1)} %shard_map.84), channel_id=1, source_target_pairs={{0,12},{1,5},{2,14},{3,7},{4,0},{5,9},{6,2},{7,11},{8,4},{9,13},{1... | collective-permute-start | bytes 294920 | tf_op jit(solution)/shard_map/ppermute | solution.py:277
  20.9 19.3 %copy-start.8 = (bf16[128,384]{1,0:T(8,128)(2,1)S(1)}, bf16[128,384]{1,0:T(8,128)(2,1)}, u32[]{:S(2)}) copy-start(bf16[128,384]{1,0:T(8,128)(2,1)} %copy-done.7) | copy-start | bytes 294916
  20.9 19.3 %copy-start.12 = (f32[384]{0:T(512)S(1)}, f32[384]{0:T(512)}, u32[]{:S(2)}) copy-start(f32[384]{0:T(512)} %param.10) | copy-start | bytes 4612
  20.9 19.3 %collective-permute-start.6 = (bf16[128,384]{1,0:T(8,128)(2,1)S(1)}, bf16[128,384]{1,0:T(8,128)(2,1)S(1)}, u32[]{:S(2)}, u32[]{:S(2)}) collective-permute-start(bf16[128,384]{1,0:T(8,128)(2,1)S(1)} %shard_map.86), channel_id=1, source_target_pairs={{0,8},{1,9},{2,10},{3,11},{4,12},{5,13},{6,14},{7,15},{8,0},{9,1},... | collective-permute-start | bytes 294920 | tf_op jit(solution)/shard_map/ppermute | solution.py:277
  22.8 14.5 %collective-permute-start.3 = (bf16[128,384]{1,0:T(8,128)(2,1)S(1)}, bf16[128,384]{1,0:T(8,128)(2,1)S(1)}, u32[]{:S(2)}, u32[]{:S(2)}) collective-permute-start(bf16[128,384]{1,0:T(8,128)(2,1)S(1)} %shard_map.85), channel_id=1, source_target_pairs={{0,4},{1,13},{2,6},{3,15},{4,8},{5,1},{6,10},{7,3},{8,12},{9,5},{1... | collective-permute-start | bytes 294920 | tf_op jit(solution)/shard_map/ppermute | solution.py:277
  37.4 17.3 %collective-permute-start.9 = (bf16[384,512]{1,0:T(8,128)(2,1)S(1)}, bf16[384,512]{1,0:T(8,128)(2,1)S(1)}, u32[]{:S(2)}, u32[]{:S(2)}) collective-permute-start(bf16[384,512]{1,0:T(8,128)(2,1)S(1)} %select_select_fusion.1), channel_id=1, source_target_pairs={{0,8},{4,0},{8,12},{12,4},{1,9},{5,1},{9,13},{13,5},{2,10},{6,2},{... | collective-permute-start | bytes 1179656 | tf_op jit(solution)/shard_map/ppermute | solution.py:238
  40.3 18.2 %copy-start.9 = (s32[8,8]{1,0:T(8,128)S(1)}, s32[8,8]{1,0:T(8,128)}, u32[]{:S(2)}) copy-start(s32[8,8]{1,0:T(8,128)} %get-tuple-element.31) | copy-start | bytes 772
  40.3 18.2 %copy-start.13 = (f32[1024]{0:T(1024)S(1)}, f32[1024]{0:T(1024)}, u32[]{:S(2)}) copy-start(f32[1024]{0:T(1024)} %param.14) | copy-start | bytes 12292
  40.4 18.3 %copy-start.10 = (s32[8,8]{1,0:T(8,128)S(1)}, s32[8,8]{1,0:T(8,128)}, u32[]{:S(2)}) copy-start(s32[8,8]{1,0:T(8,128)} %get-tuple-element.32) | copy-start | bytes 772
  40.4 18.3 %copy-start.11 = (s32[8,8]{1,0:T(8,128)S(1)}, s32[8,8]{1,0:T(8,128)}, u32[]{:S(2)}) copy-start(s32[8,8]{1,0:T(8,128)} %get-tuple-element.33) | copy-start | bytes 772
  40.4 23.7 %collective-permute-start.14 = (bf16[384,512]{1,0:T(8,128)(2,1)S(1)}, bf16[384,512]{1,0:T(8,128)(2,1)S(1)}, u32[]{:S(2)}, u32[]{:S(2)}) collective-permute-start(bf16[384,512]{1,0:T(8,128)(2,1)S(1)} %constant_dynamic-slice_fusion.refs_0_), channel_id=1, source_target_pairs={{0,4},{4,8},{8,12},{12,0},{1,5},{5,9},{9,13},{13,1},{2,6},{6,10},{... | collective-permute-start | bytes 1179656 | tf_op jit(solution)/shard_map/ppermute | solution.py:37
  40.4 25.3 %collective-permute-start.15 = (bf16[384,512]{1,0:T(8,128)(2,1)S(1)}, bf16[384,512]{1,0:T(8,128)(2,1)S(1)}, u32[]{:S(2)}, u32[]{:S(2)}) collective-permute-start(bf16[384,512]{1,0:T(8,128)(2,1)S(1)} %constant_dynamic-slice_fusion.refs_0_), channel_id=1, source_target_pairs={{0,12},{4,0},{8,4},{12,8},{1,13},{5,1},{9,5},{13,9},{2,14},{6,2},{... | collective-permute-start | bytes 1179656 | tf_op jit(solution)/shard_map/ppermute | solution.py:37
  58.1 1.8 %collective-permute-start.10 = (bf16[4,128,384]{2,1,0:T(8,128)(2,1)S(1)}, bf16[4,128,384]{2,1,0:T(8,128)(2,1)S(1)}, u32[]{:S(2)}, u32[]{:S(2)}) collective-permute-start(bf16[4,128,384]{2,1,0:T(8,128)(2,1)S(1)} %get-tuple-element.25), channel_id=1, source_target_pairs={{0,1},{1,0},{2,3},{3,2},{4,5},{5,4},{6,7},{7,6},{8,9},{9,8},{10,11... | collective-permute-start | bytes 1179656 | tf_op jit(solution)/shard_map/ppermute | solution.py:258
  60.6 7.4 %collective-permute-start.13 = (bf16[128,384]{1,0:T(8,128)(2,1)S(1)}, bf16[128,384]{1,0:T(8,128)(2,1)S(1)}, u32[]{:S(2)}, u32[]{:S(2)}) collective-permute-start(bf16[128,384]{1,0:T(8,128)(2,1)S(1)} %get-tuple-element.29), channel_id=1, source_target_pairs={{0,18},{1,19},{2,16},{3,17},{16,2},{17,3},{18,0},{19,1},{4,22},{5,... | collective-permute-start | bytes 294920 | tf_op jit(solution)/shard_map/ppermute | solution.py:334
  62.1 6.6 %collective-permute-start.12 = (bf16[128,384]{1,0:T(8,128)(2,1)S(1)}, bf16[128,384]{1,0:T(8,128)(2,1)S(1)}, u32[]{:S(2)}, u32[]{:S(2)}) collective-permute-start(bf16[128,384]{1,0:T(8,128)(2,1)S(1)} %get-tuple-element.28), channel_id=1, source_target_pairs={{0,2},{1,3},{2,0},{3,1},{16,18},{17,19},{18,16},{19,17},{4,6},{5,7... | collective-permute-start | bytes 294920 | tf_op jit(solution)/shard_map/ppermute | solution.py:334
  63.6 5.1 %collective-permute-start.11 = (bf16[128,384]{1,0:T(8,128)(2,1)S(1)}, bf16[128,384]{1,0:T(8,128)(2,1)S(1)}, u32[]{:S(2)}, u32[]{:S(2)}) collective-permute-start(bf16[128,384]{1,0:T(8,128)(2,1)S(1)} %get-tuple-element.27), channel_id=1, source_target_pairs={{0,16},{1,17},{2,18},{3,19},{16,0},{17,1},{18,2},{19,3},{4,20},{5,... | collective-permute-start | bytes 294920 | tf_op jit(solution)/shard_map/ppermute | solution.py:334
  65.8 13.4 %collective-permute-start.16 = (bf16[384,512]{1,0:T(8,128)(2,1)S(1)}, bf16[384,512]{1,0:T(8,128)(2,1)S(1)}, u32[]{:S(2)}, u32[]{:S(2)}) collective-permute-start(bf16[384,512]{1,0:T(8,128)(2,1)S(1)} %select_select_fusion), channel_id=1, source_target_pairs={{0,8},{4,0},{8,12},{12,4},{1,9},{5,1},{9,13},{13,5},{2,10},{6,2},{... | collective-permute-start | bytes 1179656 | tf_op jit(solution)/shard_map/ppermute | solution.py:238

commit v6 on v5

--- a/solution.py
+++ b/solution.py
@@ -64,18 +64,13 @@
     cut(rest_ref, margin)
 
 
-def pack_kernel(place_ref, *refs):
-    *parts, o_ref = refs
-    segments = sum(x.shape[1] for x in parts) // o_ref.shape[1]
-    for s in range(segments):
+def turn_kernel(place_ref, x_ref, o_ref):
+    width = o_ref.shape[0]
+    for s in range(x_ref.shape[1] // width):
 
         @pl.when(place_ref[0] == s)
         def _():
-            at = 0
-            for x in parts:
-                width = x.shape[1] // segments
-                o_ref[:, at : at + width] = x[:, s * width : (s + 1) * width]
-                at += width
+            o_ref[...] = x_ref[:, s * width : (s + 1) * width].astype(F32).T.astype(BF16)
 
 
 def conv_kernel(x_ref, w_ref, o_ref):
@@ -106,28 +101,53 @@
     return lax.rem(win_ref[0] + windows - by, windows)
 
 
-def contract_blocks(x_ref, segments, win_ref, pieces, cols):
+def place_blocks(place_ref, refs, x_ref):
+    segment, model = place_ref[0], place_ref[2]
+    for at, ref in enumerate(refs):
+        over_segment, over_mp = at % 2, at // 2
+        s = 1 - segment if over_segment else segment
+        pair = lax.div(model, 2)
+        pair = 1 - pair if over_mp // 2 else pair
+        odd = lax.rem(model, 2)
+        odd = 1 - odd if over_mp % 2 else odd
+        x_ref[s * 4 + pair * 2 + odd] = ref[...]
+
+
+def block_rows(x_ref, segments, win_ref, by, pieces):
     models = x_ref.shape[0] // segments
-    total = None
-    for by, piece in enumerate(pieces):
-        if len(pieces) == 1:
-            rows = [
-                jnp.concatenate([x_ref[s * models + m] for m in range(models)], axis=1)
-                for s in range(segments)
-            ]
-        else:
-            block = block_of(win_ref, by, len(pieces))
-            rows = [x_ref[s * models + block] for s in range(segments)]
-        term = jnp.dot(jnp.concatenate(rows, axis=0), piece[:, cols], preferred_element_type=F32)
-        total = term if total is None else total + term
-    return total
-
-
-def attention_kernel(segments, heads, place_ref, win_ref, x_ref, *refs):
-    *pieces, keep_ref, give_ref = refs
+    if pieces == 1:
+        rows = [
+            jnp.concatenate([x_ref[s * models + m] for m in range(models)], axis=1)
+            for s in range(segments)
+        ]
+    else:
+        block = block_of(win_ref, by, pieces)
+        rows = [x_ref[s * models + block] for s in range(segments)]
+    return jnp.concatenate(rows, axis=0)
+
+
+def attention_kernel(segments, place_ref, win_ref, x_ref, *refs):
+    *parts, keep_ref, give_ref = refs
     models = x_ref.shape[0] // segments
     bins, width = x_ref.shape[1:]
-    rows = contract_blocks(x_ref, segments, win_ref, pieces, slice(0, heads * SPAN)).astype(BF16)
+    if len(parts) == 2:
+        qkv, out = [parts[0][...]], [parts[1][...]]
+    else:
+        *sides, across = parts
+        qkv, out = ([x[...] for x in side] for side in (sides[:3], sides[3:]))
+        qkv.insert(2, across[: qkv[0].shape[0]])
+        out.insert(2, across[qkv[0].shape[0] :])
+    heads = qkv[0].shape[0] // SPAN
+    rows = None
+    for by, piece in enumerate(qkv):
+        term = lax.dot_general(
+            block_rows(x_ref, segments, win_ref, by, len(qkv)),
+            piece,
+            (((1,), (1,)), ((), ())),
+            preferred_element_type=F32,
+        )
+        rows = term if rows is None else rows + term
+    rows = rows.astype(BF16)
     outputs = []
     for head in range(heads):
         own = rows[:, head * SPAN : (head + 1) * SPAN]
@@ -152,17 +172,12 @@
         def _():
             give_ref[at] = value
 
-    for by, piece in enumerate(pieces):
-        term = lax.dot_general(
-            att,
-            piece[:, heads * SPAN :],
-            (((1,), (1,)), ((), ())),
-            preferred_element_type=F32,
-        ).astype(BF16)
+    for by, piece in enumerate(out):
+        term = jnp.dot(att, piece, preferred_element_type=F32).astype(BF16)
         for s in range(segments):
             own = term[s * bins : (s + 1) * bins]
-            if len(pieces) > 1:
-                put(s, block_of(win_ref, by, len(pieces)), own)
+            if len(out) > 1:
+                put(s, block_of(win_ref, by, len(out)), own)
             else:
                 for m in range(models):
                     put(s, jnp.int32(m), own[:, m * width : (m + 1) * width])
@@ -176,9 +191,13 @@
         out[...] = (keep_ref[at].astype(F32) + got_ref[at].astype(F32)).astype(out.dtype)
 
 
-def head_kernel(segments, win_ref, x_ref, b_ref, counts_ref, *refs):
-    *pieces, o_ref = refs
-    logits = contract_blocks(x_ref, segments, win_ref, pieces, slice(None)) + b_ref[...]
+def head_kernel(segments, place_ref, win_ref, b_ref, counts_ref, *refs):
+    blocks, (*pieces, o_ref, x_ref) = refs[:8], refs[8:]
+    place_blocks(place_ref, blocks, x_ref)
+    logits = b_ref[...]
+    for by, piece in enumerate(pieces):
+        rows = block_rows(x_ref, segments, win_ref, by, len(pieces))
+        logits = logits + jnp.dot(rows, piece[...], preferred_element_type=F32)
     tracks = jax.nn.softplus(logits).astype(BF16)
     sums = jnp.dot(counts_ref[...], tracks, preferred_element_type=F32)
     o_ref[...] = sums.astype(o_ref.dtype)
@@ -217,26 +236,28 @@
 
     place = jnp.stack([segment_index, win_index, model_index]).astype(jnp.int32)
 
-    def part_of_segment(*parts):
-        width = sum(x.shape[1] for x in parts) // segments
-        own = jax.ShapeDtypeStruct((row_count, width), BF16)
-        return call_kernel(pack_kernel, own, place, *parts)
-
-    attention_own = part_of_segment(qkv_weight, out_weight)
+    def turned_part(x):
+        own = jax.ShapeDtypeStruct((x.shape[1] // segments, row_count), BF16)
+        return call_kernel(turn_kernel, own, place, x)
+
+    qkv_own, out_own = turned_part(qkv_weight), turned_part(out_weight)
     head_cols = head_weight.shape[1] // segments
     head_own = lax.dynamic_slice_in_dim(head_weight, segment_index * head_cols, head_cols, 1)
-    heads = qkv_weight.shape[1] // segments // SPAN
     stepwise = windows == 4 and models == 4
 
-    def gathered(own, after, later):
+    def first_stage(own, axis, *after):
         if not stepwise:
-            return [lax.all_gather(own, "win", axis=0, tiled=True)]
-        sent, _ = lax.optimization_barrier((own, after))
-        below, above = shifted(sent, "win", 1), shifted(sent, "win", -1)
-        handed = jnp.where(win_index == 1, above, jnp.where(win_index == 2, below, sent))
-        handed, _ = lax.optimization_barrier((handed, later))
-        across = lax.ppermute(handed, "win", [(0, 2), (1, 0), (2, 3), (3, 1)])
-        return [own, below, across, above]
+            return [lax.all_gather(own, "win", axis=axis, tiled=True)]
+        return [own] + [
+            shifted(lax.optimization_barrier((own, tie))[0], "win", by)
+            for by, tie in zip((1, -1), after)
+        ]
+
+    def across(pieces, after):
+        own, below, above = pieces
+        handed = jnp.where(win_index == 1, above, jnp.where(win_index == 2, below, own))
+        handed, _ = lax.optimization_barrier((handed, after))
+        return lax.ppermute(handed, "win", [(0, 2), (1, 0), (2, 3), (3, 1)])
 
     win_ref = win_index.astype(jnp.int32)[None]
     track_cols = head_own.shape[1]
@@ -256,6 +277,21 @@
 
     def swapped(x):
         return lax.ppermute(x, "mp", [(m, m ^ 1) for m in range(models)])
+
+    def over_plane(x, hop):
+        pairs = [
+            (s * models + m, (s ^ hop % 2) * models + (m ^ hop // 2 * 2))
+            for s in range(segments)
+            for m in range(models)
+        ]
+        return lax.ppermute(x, plane, pairs)
+
+    def plane_blocks(x):
+        same = [x] + [over_plane(x, hop) for hop in range(1, 4)]
+        other = [swapped(b) for b in same]
+        return [same[0], same[1], other[0], other[1], same[2], same[3], other[2], other[3]]
+
+    all_blocks = [pltpu.VMEM((segments * models, bins, out_cols), BF16)]
 
     if stepwise:
         block = jax.ShapeDtypeStruct((bins + 2 * reach, row_count), BF16)
@@ -290,7 +326,10 @@
             turned_by(partials[1], 1, -1),
             turned_by(partials[2], 2, 2),
         ]
-        attention_pieces = gathered(attention_own, arrived[0], returned[:2])
+        qkv_pieces = first_stage(qkv_own, 1, arrived[0], arrived[0])
+        out_pieces = first_stage(out_own, 1, (), ())
+        both = [jnp.concatenate(x, axis=0) for x in zip(qkv_pieces, out_pieces)]
+        attention_pieces = [*qkv_pieces, *out_pieces, across(both, returned[:2])]
         for x in returned:
             conv_pre = conv_pre + x.astype(F32)
     else:
@@ -299,17 +338,19 @@
         own_feats = lax.dynamic_slice(own_bins, (reach, model_index * out_cols), (bins, out_cols))
         blocks = own_bins.reshape(own_bins.shape[0], windows, row_count).transpose(1, 0, 2)
         arrived = lax.all_to_all(blocks, "win", 0, 0, tiled=True)
-        attention_pieces = gathered(attention_own, None, None)
+        attention_pieces = first_stage(qkv_own, 1) + first_stage(out_own, 1)
         partial = jnp.stack([conv_of(BF16, arrived[w]) for w in range(windows)])
         conv_pre = lax.all_to_all(partial, "win", 0, 0, tiled=True).astype(F32).sum(axis=0)
 
     conv_out = (own_feats + jax.nn.gelu(conv_pre + conv_bias)).astype(BF16)
-    head_pieces = gathered(head_own, conv_out, ())
+    head_pieces = first_stage(head_own, 0, conv_out, conv_out)
+    if stepwise:
+        head_pieces.insert(2, across(head_pieces, ()))
     all_chan = lax.all_gather(conv_out, plane, axis=0)
 
     half = jax.ShapeDtypeStruct((segments * models // 2, bins, out_cols), BF16)
     keep, give = call_kernel(
-        functools.partial(attention_kernel, segments, heads),
+        functools.partial(attention_kernel, segments),
         [half, half],
         place,
         win_ref,
@@ -325,24 +366,26 @@
         swapped(give),
     )
     summed = own_sum
-    for across, x in enumerate(sent_sums, 1):
+    for hop, x in enumerate(sent_sums, 1):
         pairs = [
-            (s * models + m, (s ^ across % 2) * models + (m ^ across // 2 * 2))
+            (s * models + m, (s ^ hop % 2) * models + (m ^ hop // 2 * 2))
             for s in range(segments)
             for m in range(models)
         ]
         summed = summed + lax.ppermute(x, plane, pairs).astype(F32)
     resid = (conv_out.astype(F32) + summed).astype(BF16)
-    all_resid = lax.all_gather(resid, plane, axis=0)
+    all_resid = plane_blocks(resid)
 
     sums = call_kernel(
         functools.partial(head_kernel, segments),
         jax.ShapeDtypeStruct((counts.shape[0], track_cols), BF16),
+        place,
         win_ref,
-        all_resid,
         bias_part[None, :],
         counts,
+        *all_resid,
         *head_pieces,
+        scratch=all_blocks,
     )
     owners = segments * windows
     got = lax.all_to_all(

time: 92.2 us -> 92 us (level)
  blocking collectives: 31.6 us -> 21.3 us
  starting transfers between devices: 26.1 us -> 34.1 us
  waiting for transfers between devices: 16.5 us -> 21 us
  local copies, waits for them, and re-layouts: 6.26 us -> 4.55 us
    all_gather x1 -> x0, blocking collectives: 10.4 us -> none  [local(): all_resid = lax.all_gather(resid, plane, axis=0)]
    ppermute x2 -> x5, waiting for transfers between devices: 0.01 us -> 5.18 us  [the longest x3 4.91 us: over_plane(): return lax.ppermute(x, plane, pairs)]
    ppermute x2 -> x5, starting transfers between devices: 4.97 us -> 8.11 us  [the longest x2 4.56 us: across(): return lax.ppermute(handed, 'win', [(0, 2), (1, 0), (2, 3), (3, 1)])]
    ppermute x5, starting transfers between devices: 9 us -> 12.1 us  [turned_by(): return lax.ppermute(x, ('win', 'mp'), pairs)]
    ppermute x4 -> x6, starting transfers between devices: 7.69 us -> 9.78 us  [shifted(): return lax.ppermute(x, axis, [(i, (i + by) % size) for i in range(size)])]
    ppermute x4 -> x6, waiting for transfers between devices: 8.97 us -> 7.07 us  [shifted(): return lax.ppermute(x, axis, [(i, (i + by) % size) for i in range(size)])]
    eq x1, local copies, waits for them, and re-layouts: 1.32 us -> 0.01 us  [gene_counts(): chosen = ranges[2][:, None, :] == slots[None, :, None]]
    ppermute x3 -> x7, waiting for transfers between devices: 0.94 us -> 2.06 us  [swapped(): return lax.ppermute(x, 'mp', [(m, m ^ 1) for m in range(models)])]
  transfers between devices with their start and end apart: 17 -> 26, of which waited for: 9 -> 11; matrix products, arithmetic and copies ran while one was open for 2% -> 1% of each run, Pallas kernels for 9% -> 8%
where the time goes in v6:
time: 92 us; the launch traced here: 91.7 us
  starting transfers between devices  34.1 us (37%)
  blocking collectives  21.3 us (23%)
  waiting for transfers between devices  21 us (23%)
  Pallas kernels  9.65 us (10%)
  local copies, waits for them, and re-layouts  4.55 us (5%)
  other arithmetic  0.96 us (1%)
    ppermute x5, starting transfers between devices, turned_by(): return lax.ppermute(x, ('win', 'mp'), pairs)  12.1 us
    all_to_all x1, blocking collectives, local(): lax.all_to_all(sums.reshape(owners, GENE_DEV, track_cols), ('segment', 'w...  10.9 us
    all_gather x1, blocking collectives, local(): all_chan = lax.all_gather(conv_out, plane, axis=0)  10.4 us
    ppermute x6, starting transfers between devices, shifted(): return lax.ppermute(x, axis, [(i, (i + by) % size) for i in range(size)])  9.78 us
    pallas_call x10, Pallas kernels, call_kernel(): pl.pallas_call(body, out_shape=out_shape, in_specs=[scalars if x.dtype ==...  9.65 us
    ppermute x6, waiting for transfers between devices, shifted(): return lax.ppermute(x, axis, [(i, (i + by) % size) for i in range(size)])  7.07 us
    ppermute x5, waiting for transfers between devices, turned_by(): return lax.ppermute(x, ('win', 'mp'), pairs)  6.65 us
    ppermute x3, waiting for transfers between devices, over_plane(): return lax.ppermute(x, plane, pairs)  4.91 us
  transfers between devices with their start and end apart: 26, of which 11 were waited for; matrix products, arithmetic and copies ran while one was open for 1% of the time, Pallas kernels for 8%

profile of v6, /device:TPU:0, one launch (start us, length us, event | category | flops | bytes accessed | tf_op | source)
XLA Modules:
  0.0 91.7 jit_solution(2081785154788275414)
XLA Ops:
  0.1 1.2 %copy-done.1 = bf16[1,1536,256]{2,1,0:T(8,128)(2,1)S(1)} copy-done((bf16[1,1536,256]{2,1,0:T(8,128)(2,1)S(1)}, bf16[1,1536,256]{2,1,0:T(8,128)(2,1)}, u32[]{:S(2)}) %copy-start.1) | copy-done | bytes 786456
  1.3 0.9 shard_map.82
  2.2 3.1 %collective-permute-start = (bf16[144,384]{1,0:T(8,128)(2,1)S(1)}, bf16[144,384]{1,0:T(8,128)(2,1)S(1)}, u32[]{:S(2)}, u32[]{:S(2)}) collective-permute-start(bf16[144,384]{1,0:T(8,128)(2,1)S(1)} %get-tuple-element.20), channel_id=1, source_target_pairs={{0,4},{1,13},{2,6},{3,15},{4,8},{5,1},{6,10},{7,3},{8,12},{9,5},{1... | collective-permute-start | bytes 331784 | tf_op jit(solution)/shard_map/ppermute | solution.py:313
  5.3 2.6 %collective-permute-start.4 = (bf16[80,384]{1,0:T(8,128)(2,1)S(1)}, bf16[80,384]{1,0:T(8,128)(2,1)S(1)}, u32[]{:S(2)}, u32[]{:S(2)}) collective-permute-start(bf16[80,384]{1,0:T(8,128)(2,1)S(1)} %get-tuple-element.21), channel_id=1, source_target_pairs={{0,8},{1,9},{2,10},{3,11},{4,12},{5,13},{6,14},{7,15},{8,0},{9,1},... | collective-permute-start | bytes 184328 | tf_op jit(solution)/shard_map/ppermute | solution.py:313
  7.8 1.0 %copy-done.2 = bf16[384,640]{1,0:T(8,128)(2,1)S(1)} copy-done((bf16[384,640]{1,0:T(8,128)(2,1)S(1)}, bf16[384,640]{1,0:T(8,128)(2,1)}, u32[]{:S(2)}) %copy-start.2) | copy-done | bytes 491544
  8.9 0.7 shard_map.87.refs_0_
  9.6 1.7 %collective-permute-done.x_ref = bf16[144,384]{1,0:T(8,128)(2,1)S(1)} collective-permute-done((bf16[144,384]{1,0:T(8,128)(2,1)S(1)}, bf16[144,384]{1,0:T(8,128)(2,1)S(1)}, u32[]{:S(2)}, u32[]{:S(2)}) %collective-permute-start) | collective-permute-done | bytes 110624 | tf_op jit(solution)/shard_map/ppermute | solution.py:313
  11.2 1.1 %collective-permute-start.7 = (bf16[320,384]{1,0:T(8,128)(2,1)S(1)}, bf16[320,384]{1,0:T(8,128)(2,1)S(1)}, u32[]{:S(2)}, u32[]{:S(2)}) collective-permute-start(bf16[320,384]{1,0:T(8,128)(2,1)S(1)} %shard_map.87.refs_0_), channel_id=1, source_target_pairs={{0,4},{4,8},{8,12},{12,0},{1,5},{5,9},{9,13},{13,1},{2,6},{6,10},{... | collective-permute-start | bytes 737288 | tf_op jit(solution)/shard_map/ppermute | solution.py:37
  12.4 2.7 %collective-permute-start.8 = (bf16[320,384]{1,0:T(8,128)(2,1)S(1)}, bf16[320,384]{1,0:T(8,128)(2,1)S(1)}, u32[]{:S(2)}, u32[]{:S(2)}) collective-permute-start(bf16[320,384]{1,0:T(8,128)(2,1)S(1)} %shard_map.87.refs_0_), channel_id=1, source_target_pairs={{0,12},{4,0},{8,4},{12,8},{1,13},{5,1},{9,5},{13,9},{2,14},{6,2},{... | collective-permute-start | bytes 737288 | tf_op jit(solution)/shard_map/ppermute | solution.py:37
  15.1 1.0 %copy-done.3 = bf16[384,384]{1,0:T(8,128)(2,1)S(1)} copy-done((bf16[384,384]{1,0:T(8,128)(2,1)S(1)}, bf16[384,384]{1,0:T(8,128)(2,1)}, u32[]{:S(2)}) %copy-start.3) | copy-done | bytes 294936
  16.0 0.7 shard_map.88.refs_3_
  16.7 1.6 %collective-permute-start.10 = (bf16[192,384]{1,0:T(8,128)(2,1)S(1)}, bf16[192,384]{1,0:T(8,128)(2,1)S(1)}, u32[]{:S(2)}, u32[]{:S(2)}) collective-permute-start(bf16[192,384]{1,0:T(8,128)(2,1)S(1)} %shard_map.88.refs_3_), channel_id=1, source_target_pairs={{0,12},{4,0},{8,4},{12,8},{1,13},{5,1},{9,5},{13,9},{2,14},{6,2},{... | collective-permute-start | bytes 442376 | tf_op jit(solution)/shard_map/ppermute | solution.py:37
  18.3 0.5 collective-permute-start.9
  18.8 0.5 shard_map.83
  19.4 0.6 copy-done.4
  20.0 0.5 shard_map.84
  20.4 1.0 %shard_map.86 = bf16[128,384]{1,0:T(8,128)(2,1)S(1)} custom-call(s32[3]{0:T(128)S(1)} %pad_add_fusion.place_ref, bf16[80,384]{1,0:T(8,128)(2,1)S(1)} %collective-permute-done.4.own_ref, bf16[80,384]{1,0:T(8,128)(2,1)S(1)} %collective-permute-done.5.other_ref, bf16[5,384,384]{2,1,0:T(8,128)(2,1)S(1)} %bitcast.25), custom_call_target="tpu_custom_call" | custom-call | flops 188743680 | bytes 1048576 | tf_op jit(solution)/shard_map/pallas_call | solution.py:24
  21.5 3.4 %collective-permute-start.1 = (bf16[128,384]{1,0:T(8,128)(2,1)S(1)}, bf16[128,384]{1,0:T(8,128)(2,1)S(1)}, u32[]{:S(2)}, u32[]{:S(2)}) collective-permute-start(bf16[128,384]{1,0:T(8,128)(2,1)S(1)} %shard_map.84), channel_id=1, source_target_pairs={{0,12},{1,5},{2,14},{3,7},{4,0},{5,9},{6,2},{7,11},{8,4},{9,13},{1... | collective-permute-start | bytes 294920 | tf_op jit(solution)/shard_map/ppermute | solution.py:313
  24.9 0.5 shard_map.85
  25.3 3.6 %collective-permute-done.10.refs_5_ = bf16[192,384]{1,0:T(8,128)(2,1)S(1)} collective-permute-done((bf16[192,384]{1,0:T(8,128)(2,1)S(1)}, bf16[192,384]{1,0:T(8,128)(2,1)S(1)}, u32[]{:S(2)}, u32[]{:S(2)}) %collective-permute-start.10) | collective-permute-done | bytes 147488 | tf_op jit(solution)/shard_map/ppermute | solution.py:37
  29.0 1.7 %collective-permute-start.6 = (bf16[128,384]{1,0:T(8,128)(2,1)S(1)}, bf16[128,384]{1,0:T(8,128)(2,1)S(1)}, u32[]{:S(2)}, u32[]{:S(2)}) collective-permute-start(bf16[128,384]{1,0:T(8,128)(2,1)S(1)} %shard_map.86), channel_id=1, source_target_pairs={{0,8},{1,9},{2,10},{3,11},{4,12},{5,13},{6,14},{7,15},{8,0},{9,1},... | collective-permute-start | bytes 294920 | tf_op jit(solution)/shard_map/ppermute | solution.py:313
  30.7 1.2 %collective-permute-done.9.refs_4_ = bf16[192,384]{1,0:T(8,128)(2,1)S(1)} collective-permute-done((bf16[192,384]{1,0:T(8,128)(2,1)S(1)}, bf16[192,384]{1,0:T(8,128)(2,1)S(1)}, u32[]{:S(2)}, u32[]{:S(2)}) %collective-permute-start.9) | collective-permute-done | bytes 147488 | tf_op jit(solution)/shard_map/ppermute | solution.py:37
  31.8 1.4 %collective-permute-start.3 = (bf16[128,384]{1,0:T(8,128)(2,1)S(1)}, bf16[128,384]{1,0:T(8,128)(2,1)S(1)}, u32[]{:S(2)}, u32[]{:S(2)}) collective-permute-start(bf16[128,384]{1,0:T(8,128)(2,1)S(1)} %shard_map.85), channel_id=1, source_target_pairs={{0,4},{1,13},{2,6},{3,15},{4,8},{5,1},{6,10},{7,3},{8,12},{9,5},{1... | collective-permute-start | bytes 294920 | tf_op jit(solution)/shard_map/ppermute | solution.py:313
  33.4 5.0 %collective-permute-done.3 = bf16[128,384]{1,0:T(8,128)(2,1)S(1)} collective-permute-done((bf16[128,384]{1,0:T(8,128)(2,1)S(1)}, bf16[128,384]{1,0:T(8,128)(2,1)S(1)}, u32[]{:S(2)}, u32[]{:S(2)}) %collective-permute-start.3) | collective-permute-done | bytes 98336 | tf_op jit(solution)/shard_map/ppermute | solution.py:313
  38.3 1.8 %collective-permute-start.11 = (bf16[512,384]{1,0:T(8,128)(2,1)S(1)}, bf16[512,384]{1,0:T(8,128)(2,1)S(1)}, u32[]{:S(2)}, u32[]{:S(2)}) collective-permute-start(bf16[512,384]{1,0:T(8,128)(2,1)S(1)} %maximum_select_fusion), channel_id=1, source_target_pairs={{0,8},{4,0},{8,12},{12,4},{1,9},{5,1},{9,13},{13,5},{2,10},{6,2},{... | collective-permute-start | bytes 1179656 | tf_op jit(solution)/shard_map/ppermute | solution.py:260
  40.3 0.3 collective-permute-start.23
  40.6 3.6 %collective-permute-start.24 = (bf16[384,512]{1,0:T(8,128)(2,1)S(1)}, bf16[384,512]{1,0:T(8,128)(2,1)S(1)}, u32[]{:S(2)}, u32[]{:S(2)}) collective-permute-start(bf16[384,512]{1,0:T(8,128)(2,1)S(1)} %constant_dynamic-slice_fusion.refs_8_), channel_id=1, source_target_pairs={{0,12},{4,0},{8,4},{12,8},{1,13},{5,1},{9,5},{13,9},{2,14},{6,2},{... | collective-permute-start | bytes 1179656 | tf_op jit(solution)/shard_map/ppermute | solution.py:37
  44.1 10.4 %all-gather = bf16[1024,384]{1,0:T(8,128)(2,1)S(1)} all-gather(bf16[128,384]{1,0:T(8,128)(2,1)S(1)} %fusion.8), channel_id=2, replica_groups=mesh['segment'=2,'win'=4,'mp'=4] {'segment','mp'}, dimensions={0}, use_global_device_ids=true | all-gather | bytes 884736 | tf_op jit(solution)/shard_map/all_gather | solution.py:349
  54.5 2.7 %shard_map.89 = (bf16[4,128,384]{2,1,0:T(8,128)(2,1)S(1)}, bf16[4,128,384]{2,1,0:T(8,128)(2,1)S(1)}) custom-call(s32[3]{0:T(128)S(1)} %pad_add_fusion.place_ref, s32[1]{0:T(128)} %bitcast.1.win_ref, bf16[8,128,384]{2,1,0:T(8,128)(2,1)S(1)} %bitcast.27, bf16[320,384]{1,0:T(8,128)(2,1)S(1)} %shard_map.87.refs_0_, ...), custom_call_target="tpu_custom_call" | custom-call | bytes 1048576 | tf_op jit(solution)/shard_map/pallas_call | solution.py:24
  57.3 0.4 collective-permute-start.12
  57.8 1.3 %collective-permute-done.12.got_ref = bf16[4,128,384]{2,1,0:T(8,128)(2,1)S(1)} collective-permute-done((bf16[4,128,384]{2,1,0:T(8,128)(2,1)S(1)}, bf16[4,128,384]{2,1,0:T(8,128)(2,1)S(1)}, u32[]{:S(2)}, u32[]{:S(2)}) %collective-permute-start.12) | collective-permute-done | bytes 393248 | tf_op jit(solution)/shard_map/ppermute | solution.py:279
  59.1 0.6 shard_map.90
  59.7 1.6 %collective-permute-start.13 = (bf16[128,384]{1,0:T(8,128)(2,1)S(1)}, bf16[128,384]{1,0:T(8,128)(2,1)S(1)}, u32[]{:S(2)}, u32[]{:S(2)}) collective-permute-start(bf16[128,384]{1,0:T(8,128)(2,1)S(1)} %get-tuple-element.27), channel_id=1, source_target_pairs={{0,16},{1,17},{2,18},{3,19},{16,0},{17,1},{18,2},{19,3},{4,20},{5,... | collective-permute-start | bytes 294920 | tf_op jit(solution)/shard_map/ppermute | solution.py:375
  61.3 0.5 collective-permute-start.14
  61.8 1.5 %collective-permute-start.15 = (bf16[128,384]{1,0:T(8,128)(2,1)S(1)}, bf16[128,384]{1,0:T(8,128)(2,1)S(1)}, u32[]{:S(2)}, u32[]{:S(2)}) collective-permute-start(bf16[128,384]{1,0:T(8,128)(2,1)S(1)} %get-tuple-element.29), channel_id=1, source_target_pairs={{0,18},{1,19},{2,16},{3,17},{16,2},{17,3},{18,0},{19,1},{4,22},{5,... | collective-permute-start | bytes 294920 | tf_op jit(solution)/shard_map/ppermute | solution.py:375
  63.3 2.2 %collective-permute-done.24.refs_11_ = bf16[384,512]{1,0:T(8,128)(2,1)S(1)} collective-permute-done((bf16[384,512]{1,0:T(8,128)(2,1)S(1)}, bf16[384,512]{1,0:T(8,128)(2,1)S(1)}, u32[]{:S(2)}, u32[]{:S(2)}) %collective-permute-start.24) | collective-permute-done | bytes 393248 | tf_op jit(solution)/shard_map/ppermute | solution.py:37
  65.7 2.8 %collective-permute-start.25 = (bf16[384,512]{1,0:T(8,128)(2,1)S(1)}, bf16[384,512]{1,0:T(8,128)(2,1)S(1)}, u32[]{:S(2)}, u32[]{:S(2)}) collective-permute-start(bf16[384,512]{1,0:T(8,128)(2,1)S(1)} %select_select_fusion), channel_id=1, source_target_pairs={{0,8},{4,0},{8,12},{12,4},{1,9},{5,1},{9,13},{13,5},{2,10},{6,2},{... | collective-permute-start | bytes 1179656 | tf_op jit(solution)/shard_map/ppermute | solution.py:260
  68.6 1.6 %collective-permute-start.16 = (bf16[128,384]{1,0:T(8,128)(2,1)S(1)}, bf16[128,384]{1,0:T(8,128)(2,1)S(1)}, u32[]{:S(2)}, u32[]{:S(2)}) collective-permute-start(bf16[128,384]{1,0:T(8,128)(2,1)S(1)} %add_convert_fusion.refs_0_), channel_id=1, source_target_pairs={{0,16},{1,17},{2,18},{3,19},{16,0},{17,1},{18,2},{19,3},{4,20},{5,... | collective-permute-start | bytes 294920 | tf_op jit(solution)/shard_map/ppermute | solution.py:287
  70.1 1.5 %collective-permute-start.19 = (bf16[128,384]{1,0:T(8,128)(2,1)S(1)}, bf16[128,384]{1,0:T(8,128)(2,1)S(1)}, u32[]{:S(2)}, u32[]{:S(2)}) collective-permute-start(bf16[128,384]{1,0:T(8,128)(2,1)S(1)} %add_convert_fusion.refs_0_), channel_id=1, source_target_pairs={{0,2},{1,3},{2,0},{3,1},{16,18},{17,19},{18,16},{19,17},{4,6},{5,7... | collective-permute-start | bytes 294920 | tf_op jit(solution)/shard_map/ppermute | solution.py:287
  71.7 0.5 collective-permute-start.20
  72.3 1.0 %collective-permute-done.16.refs_1_ = bf16[128,384]{1,0:T(8,128)(2,1)S(1)} collective-permute-done((bf16[128,384]{1,0:T(8,128)(2,1)S(1)}, bf16[128,384]{1,0:T(8,128)(2,1)S(1)}, u32[]{:S(2)}, u32[]{:S(2)}) %collective-permute-start.16) | collective-permute-done | bytes 98336 | tf_op jit(solution)/shard_map/ppermute | solution.py:287
  73.3 2.5 %collective-permute-done.19.refs_4_ = bf16[128,384]{1,0:T(8,128)(2,1)S(1)} collective-permute-done((bf16[128,384]{1,0:T(8,128)(2,1)S(1)}, bf16[128,384]{1,0:T(8,128)(2,1)S(1)}, u32[]{:S(2)}, u32[]{:S(2)}) %collective-permute-start.19) | collective-permute-done | bytes 98336 | tf_op jit(solution)/shard_map/ppermute | solution.py:287
  75.8 1.4 %collective-permute-done.20.refs_5_ = bf16[128,384]{1,0:T(8,128)(2,1)S(1)} collective-permute-done((bf16[128,384]{1,0:T(8,128)(2,1)S(1)}, bf16[128,384]{1,0:T(8,128)(2,1)S(1)}, u32[]{:S(2)}, u32[]{:S(2)}) %collective-permute-start.20) | collective-permute-done | bytes 98336 | tf_op jit(solution)/shard_map/ppermute | solution.py:287
  77.4 0.3 collective-permute-done.25.refs_10_
  77.7 0.8 collective-permute-done.22.refs_7_
  78.5 1.7 %shard_map.91 = bf16[64,512]{1,0:T(8,128)(2,1)S(1)} custom-call(s32[3]{0:T(128)S(1)} %pad_add_fusion.place_ref, s32[1]{0:T(128)} %bitcast.1.win_ref, f32[1,512]{1,0:T(1,128)S(1)} %bitcast.31, bf16[64,256]{1,0:T(8,128)(2,1)S(1)} %bitcast.30, bf16[128,384]{1,0:T(8,128)(2,1)S(1)} %add_convert_fusion.refs_0_, ...), custom_call_target="tpu_custom_call" | custom-call | bytes 1048576 | tf_op jit(solution)/shard_map/pallas_call | solution.py:24
  80.2 10.9 %all_to_all.5 = bf16[8,8,512]{2,1,0:T(8,128)(2,1)S(1)} all-to-all(bf16[8,8,512]{2,1,0:T(8,128)(2,1)S(1)} %bitcast.29), channel_id=1, replica_groups=mesh['segment'=2,'win'=4,'mp'=4] {'segment','win'}, dimensions={0} | all-to-all | bytes 131072 | tf_op jit(solution)/shard_map/all_to_all | solution.py:391
  91.1 0.6 log1p.9
  (45 shorter events, 1.2 us)
Async XLA Ops:
  0.0 18.8 %copy-start = (bf16[384,5,384]{2,0,1:T(8,128)(2,1)S(1)}, bf16[384,5,384]{2,0,1:T(8,128)(2,1)}, u32[]{:S(2)}) copy-start(bf16[384,5,384]{2,0,1:T(8,128)(2,1)} %param.9) | copy-start | bytes 4423684
  0.1 1.2 %copy-start.1 = (bf16[1,1536,256]{2,1,0:T(8,128)(2,1)S(1)}, bf16[1,1536,256]{2,1,0:T(8,128)(2,1)}, u32[]{:S(2)}) copy-start(bf16[1,1536,256]{2,1,0:T(8,128)(2,1)} %param.8) | copy-start | bytes 2359300
  2.2 9.1 %collective-permute-start = (bf16[144,384]{1,0:T(8,128)(2,1)S(1)}, bf16[144,384]{1,0:T(8,128)(2,1)S(1)}, u32[]{:S(2)}, u32[]{:S(2)}) collective-permute-start(bf16[144,384]{1,0:T(8,128)(2,1)S(1)} %get-tuple-element.20), channel_id=1, source_target_pairs={{0,4},{1,13},{2,6},{3,15},{4,8},{5,1},{6,10},{7,3},{8,12},{9,5},{1... | collective-permute-start | bytes 331784 | tf_op jit(solution)/shard_map/ppermute | solution.py:313
  5.3 9.8 %collective-permute-start.4 = (bf16[80,384]{1,0:T(8,128)(2,1)S(1)}, bf16[80,384]{1,0:T(8,128)(2,1)S(1)}, u32[]{:S(2)}, u32[]{:S(2)}) collective-permute-start(bf16[80,384]{1,0:T(8,128)(2,1)S(1)} %get-tuple-element.21), channel_id=1, source_target_pairs={{0,8},{1,9},{2,10},{3,11},{4,12},{5,13},{6,14},{7,15},{8,0},{9,1},... | collective-permute-start | bytes 184328 | tf_op jit(solution)/shard_map/ppermute | solution.py:313
  7.8 1.0 %copy-start.2 = (bf16[384,640]{1,0:T(8,128)(2,1)S(1)}, bf16[384,640]{1,0:T(8,128)(2,1)}, u32[]{:S(2)}) copy-start(bf16[384,640]{1,0:T(8,128)(2,1)} %x_ref.2) | copy-start | bytes 1474564
  11.2 21.9 %collective-permute-start.7 = (bf16[320,384]{1,0:T(8,128)(2,1)S(1)}, bf16[320,384]{1,0:T(8,128)(2,1)S(1)}, u32[]{:S(2)}, u32[]{:S(2)}) collective-permute-start(bf16[320,384]{1,0:T(8,128)(2,1)S(1)} %shard_map.87.refs_0_), channel_id=1, source_target_pairs={{0,4},{4,8},{8,12},{12,0},{1,5},{5,9},{9,13},{13,1},{2,6},{6,10},{... | collective-permute-start | bytes 737288 | tf_op jit(solution)/shard_map/ppermute | solution.py:37
  12.4 20.8 %collective-permute-start.8 = (bf16[320,384]{1,0:T(8,128)(2,1)S(1)}, bf16[320,384]{1,0:T(8,128)(2,1)S(1)}, u32[]{:S(2)}, u32[]{:S(2)}) collective-permute-start(bf16[320,384]{1,0:T(8,128)(2,1)S(1)} %shard_map.87.refs_0_), channel_id=1, source_target_pairs={{0,12},{4,0},{8,4},{12,8},{1,13},{5,1},{9,5},{13,9},{2,14},{6,2},{... | collective-permute-start | bytes 737288 | tf_op jit(solution)/shard_map/ppermute | solution.py:37
  15.1 4.2 %collective-permute-start.5 = (bf16[80,384]{1,0:T(8,128)(2,1)S(1)}, bf16[80,384]{1,0:T(8,128)(2,1)S(1)}, u32[]{:S(2)}, u32[]{:S(2)}) collective-permute-start(bf16[80,384]{1,0:T(8,128)(2,1)S(1)} %collective-permute-done.4.own_ref), channel_id=1, source_target_pairs={{0,1},{1,0},{2,3},{3,2},{4,5},{5,4},{6,7},{7,6},{8,9},{9,8},{10,11... | collective-permute-start | bytes 184328 | tf_op jit(solution)/shard_map/ppermute | solution.py:279
  15.1 1.0 %copy-start.3 = (bf16[384,384]{1,0:T(8,128)(2,1)S(1)}, bf16[384,384]{1,0:T(8,128)(2,1)}, u32[]{:S(2)}) copy-start(bf16[384,384]{1,0:T(8,128)(2,1)} %x_ref.3) | copy-start | bytes 884740
  16.7 12.2 %collective-permute-start.10 = (bf16[192,384]{1,0:T(8,128)(2,1)S(1)}, bf16[192,384]{1,0:T(8,128)(2,1)S(1)}, u32[]{:S(2)}, u32[]{:S(2)}) collective-permute-start(bf16[192,384]{1,0:T(8,128)(2,1)S(1)} %shard_map.88.refs_3_), channel_id=1, source_target_pairs={{0,12},{4,0},{8,4},{12,8},{1,13},{5,1},{9,5},{13,9},{2,14},{6,2},{... | collective-permute-start | bytes 442376 | tf_op jit(solution)/shard_map/ppermute | solution.py:37
  18.3 13.5 %collective-permute-start.9 = (bf16[192,384]{1,0:T(8,128)(2,1)S(1)}, bf16[192,384]{1,0:T(8,128)(2,1)S(1)}, u32[]{:S(2)}, u32[]{:S(2)}) collective-permute-start(bf16[192,384]{1,0:T(8,128)(2,1)S(1)} %shard_map.88.refs_3_), channel_id=1, source_target_pairs={{0,4},{4,8},{8,12},{12,0},{1,5},{5,9},{9,13},{13,1},{2,6},{6,10},{... | collective-permute-start | bytes 442376 | tf_op jit(solution)/shard_map/ppermute | solution.py:37
  18.8 1.1 %copy-start.4 = (bf16[384,1024]{1,0:T(8,128)(2,1)S(1)}, bf16[384,1024]{1,0:T(8,128)(2,1)}, u32[]{:S(2)}) copy-start(bf16[384,1024]{1,0:T(8,128)(2,1)} %param.13) | copy-start | bytes 2359300
  19.3 2.2 %collective-permute-start.2 = (bf16[144,384]{1,0:T(8,128)(2,1)S(1)}, bf16[144,384]{1,0:T(8,128)(2,1)S(1)}, u32[]{:S(2)}, u32[]{:S(2)}) collective-permute-start(bf16[144,384]{1,0:T(8,128)(2,1)S(1)} %collective-permute-done.x_ref), channel_id=1, source_target_pairs={{0,1},{1,0},{2,3},{3,2},{4,5},{5,4},{6,7},{7,6},{8,9},{9,8},{10,11... | collective-permute-start | bytes 331784 | tf_op jit(solution)/shard_map/ppermute | solution.py:279
  21.4 18.7 %copy-start.6 = (f32[384]{0:T(512)S(1)}, f32[384]{0:T(512)}, u32[]{:S(2)}) copy-start(f32[384]{0:T(512)} %param.10) | copy-start | bytes 4612
  21.5 11.9 %collective-permute-start.1 = (bf16[128,384]{1,0:T(8,128)(2,1)S(1)}, bf16[128,384]{1,0:T(8,128)(2,1)S(1)}, u32[]{:S(2)}, u32[]{:S(2)}) collective-permute-start(bf16[128,384]{1,0:T(8,128)(2,1)S(1)} %shard_map.84), channel_id=1, source_target_pairs={{0,12},{1,5},{2,14},{3,7},{4,0},{5,9},{6,2},{7,11},{8,4},{9,13},{1... | collective-permute-start | bytes 294920 | tf_op jit(solution)/shard_map/ppermute | solution.py:313
  29.0 11.1 %collective-permute-start.6 = (bf16[128,384]{1,0:T(8,128)(2,1)S(1)}, bf16[128,384]{1,0:T(8,128)(2,1)S(1)}, u32[]{:S(2)}, u32[]{:S(2)}) collective-permute-start(bf16[128,384]{1,0:T(8,128)(2,1)S(1)} %shard_map.86), channel_id=1, source_target_pairs={{0,8},{1,9},{2,10},{3,11},{4,12},{5,13},{6,14},{7,15},{8,0},{9,1},... | collective-permute-start | bytes 294920 | tf_op jit(solution)/shard_map/ppermute | solution.py:313
  31.8 6.5 %collective-permute-start.3 = (bf16[128,384]{1,0:T(8,128)(2,1)S(1)}, bf16[128,384]{1,0:T(8,128)(2,1)S(1)}, u32[]{:S(2)}, u32[]{:S(2)}) collective-permute-start(bf16[128,384]{1,0:T(8,128)(2,1)S(1)} %shard_map.85), channel_id=1, source_target_pairs={{0,4},{1,13},{2,6},{3,15},{4,8},{5,1},{6,10},{7,3},{8,12},{9,5},{1... | collective-permute-start | bytes 294920 | tf_op jit(solution)/shard_map/ppermute | solution.py:313
  38.3 16.2 %collective-permute-start.11 = (bf16[512,384]{1,0:T(8,128)(2,1)S(1)}, bf16[512,384]{1,0:T(8,128)(2,1)S(1)}, u32[]{:S(2)}, u32[]{:S(2)}) collective-permute-start(bf16[512,384]{1,0:T(8,128)(2,1)S(1)} %maximum_select_fusion), channel_id=1, source_target_pairs={{0,8},{4,0},{8,12},{12,4},{1,9},{5,1},{9,13},{13,5},{2,10},{6,2},{... | collective-permute-start | bytes 1179656 | tf_op jit(solution)/shard_map/ppermute | solution.py:260
  40.3 17.4 %copy-start.5 = (s32[3,1,8,8]{3,2,1,0:T(8,128)S(1)}, s32[3,1,8,8]{3,2,1,0:T(8,128)}, u32[]{:S(2)}) copy-start(s32[3,1,8,8]{3,2,1,0:T(8,128)} %param.15) | copy-start | bytes 2308
  40.3 23.0 %collective-permute-start.23 = (bf16[384,512]{1,0:T(8,128)(2,1)S(1)}, bf16[384,512]{1,0:T(8,128)(2,1)S(1)}, u32[]{:S(2)}, u32[]{:S(2)}) collective-permute-start(bf16[384,512]{1,0:T(8,128)(2,1)S(1)} %constant_dynamic-slice_fusion.refs_8_), channel_id=1, source_target_pairs={{0,4},{4,8},{8,12},{12,0},{1,5},{5,9},{9,13},{13,1},{2,6},{6,10},{... | collective-permute-start | bytes 1179656 | tf_op jit(solution)/shard_map/ppermute | solution.py:37
  40.6 24.9 %collective-permute-start.24 = (bf16[384,512]{1,0:T(8,128)(2,1)S(1)}, bf16[384,512]{1,0:T(8,128)(2,1)S(1)}, u32[]{:S(2)}, u32[]{:S(2)}) collective-permute-start(bf16[384,512]{1,0:T(8,128)(2,1)S(1)} %constant_dynamic-slice_fusion.refs_8_), channel_id=1, source_target_pairs={{0,12},{4,0},{8,4},{12,8},{1,13},{5,1},{9,5},{13,9},{2,14},{6,2},{... | collective-permute-start | bytes 1179656 | tf_op jit(solution)/shard_map/ppermute | solution.py:37
  57.3 1.8 %collective-permute-start.12 = (bf16[4,128,384]{2,1,0:T(8,128)(2,1)S(1)}, bf16[4,128,384]{2,1,0:T(8,128)(2,1)S(1)}, u32[]{:S(2)}, u32[]{:S(2)}) collective-permute-start(bf16[4,128,384]{2,1,0:T(8,128)(2,1)S(1)} %get-tuple-element.25), channel_id=1, source_target_pairs={{0,1},{1,0},{2,3},{3,2},{4,5},{5,4},{6,7},{7,6},{8,9},{9,8},{10,11... | collective-permute-start | bytes 1179656 | tf_op jit(solution)/shard_map/ppermute | solution.py:279
  59.1 13.1 %copy-start.7 = (f32[1024]{0:T(1024)S(1)}, f32[1024]{0:T(1024)}, u32[]{:S(2)}) copy-start(f32[1024]{0:T(1024)} %param.14) | copy-start | bytes 12292
  59.7 8.8 %collective-permute-start.13 = (bf16[128,384]{1,0:T(8,128)(2,1)S(1)}, bf16[128,384]{1,0:T(8,128)(2,1)S(1)}, u32[]{:S(2)}, u32[]{:S(2)}) collective-permute-start(bf16[128,384]{1,0:T(8,128)(2,1)S(1)} %get-tuple-element.27), channel_id=1, source_target_pairs={{0,16},{1,17},{2,18},{3,19},{16,0},{17,1},{18,2},{19,3},{4,20},{5,... | collective-permute-start | bytes 294920 | tf_op jit(solution)/shard_map/ppermute | solution.py:375
  61.3 7.2 %collective-permute-start.14 = (bf16[128,384]{1,0:T(8,128)(2,1)S(1)}, bf16[128,384]{1,0:T(8,128)(2,1)S(1)}, u32[]{:S(2)}, u32[]{:S(2)}) collective-permute-start(bf16[128,384]{1,0:T(8,128)(2,1)S(1)} %get-tuple-element.28), channel_id=1, source_target_pairs={{0,2},{1,3},{2,0},{3,1},{16,18},{17,19},{18,16},{19,17},{4,6},{5,7... | collective-permute-start | bytes 294920 | tf_op jit(solution)/shard_map/ppermute | solution.py:375
  61.8 6.7 %collective-permute-start.15 = (bf16[128,384]{1,0:T(8,128)(2,1)S(1)}, bf16[128,384]{1,0:T(8,128)(2,1)S(1)}, u32[]{:S(2)}, u32[]{:S(2)}) collective-permute-start(bf16[128,384]{1,0:T(8,128)(2,1)S(1)} %get-tuple-element.29), channel_id=1, source_target_pairs={{0,18},{1,19},{2,16},{3,17},{16,2},{17,3},{18,0},{19,1},{4,22},{5,... | collective-permute-start | bytes 294920 | tf_op jit(solution)/shard_map/ppermute | solution.py:375
  65.7 12.0 %collective-permute-start.25 = (bf16[384,512]{1,0:T(8,128)(2,1)S(1)}, bf16[384,512]{1,0:T(8,128)(2,1)S(1)}, u32[]{:S(2)}, u32[]{:S(2)}) collective-permute-start(bf16[384,512]{1,0:T(8,128)(2,1)S(1)} %select_select_fusion), channel_id=1, source_target_pairs={{0,8},{4,0},{8,12},{12,4},{1,9},{5,1},{9,13},{13,5},{2,10},{6,2},{... | collective-permute-start | bytes 1179656 | tf_op jit(solution)/shard_map/ppermute | solution.py:260
  68.6 4.7 %collective-permute-start.16 = (bf16[128,384]{1,0:T(8,128)(2,1)S(1)}, bf16[128,384]{1,0:T(8,128)(2,1)S(1)}, u32[]{:S(2)}, u32[]{:S(2)}) collective-permute-start(bf16[128,384]{1,0:T(8,128)(2,1)S(1)} %add_convert_fusion.refs_0_), channel_id=1, source_target_pairs={{0,16},{1,17},{2,18},{3,19},{16,0},{17,1},{18,2},{19,3},{4,20},{5,... | collective-permute-start | bytes 294920 | tf_op jit(solution)/shard_map/ppermute | solution.py:287
  70.1 5.7 %collective-permute-start.19 = (bf16[128,384]{1,0:T(8,128)(2,1)S(1)}, bf16[128,384]{1,0:T(8,128)(2,1)S(1)}, u32[]{:S(2)}, u32[]{:S(2)}) collective-permute-start(bf16[128,384]{1,0:T(8,128)(2,1)S(1)} %add_convert_fusion.refs_0_), channel_id=1, source_target_pairs={{0,2},{1,3},{2,0},{3,1},{16,18},{17,19},{18,16},{19,17},{4,6},{5,7... | collective-permute-start | bytes 294920 | tf_op jit(solution)/shard_map/ppermute | solution.py:287
  71.7 5.5 %collective-permute-start.20 = (bf16[128,384]{1,0:T(8,128)(2,1)S(1)}, bf16[128,384]{1,0:T(8,128)(2,1)S(1)}, u32[]{:S(2)}, u32[]{:S(2)}) collective-permute-start(bf16[128,384]{1,0:T(8,128)(2,1)S(1)} %add_convert_fusion.refs_0_), channel_id=1, source_target_pairs={{0,18},{1,19},{2,16},{3,17},{16,2},{17,3},{18,0},{19,1},{4,22},{5,... | collective-permute-start | bytes 294920 | tf_op jit(solution)/shard_map/ppermute | solution.py:287
  72.2 5.5 %collective-permute-start.17 = (bf16[128,384]{1,0:T(8,128)(2,1)S(1)}, bf16[128,384]{1,0:T(8,128)(2,1)S(1)}, u32[]{:S(2)}, u32[]{:S(2)}) collective-permute-start(bf16[128,384]{1,0:T(8,128)(2,1)S(1)} %add_convert_fusion.refs_0_), channel_id=1, source_target_pairs={{0,1},{1,0},{2,3},{3,2},{4,5},{5,4},{6,7},{7,6},{8,9},{9,8},{10,11... | collective-permute-start | bytes 294920 | tf_op jit(solution)/shard_map/ppermute | solution.py:279
  73.3 4.4 %collective-permute-start.18 = (bf16[128,384]{1,0:T(8,128)(2,1)S(1)}, bf16[128,384]{1,0:T(8,128)(2,1)S(1)}, u32[]{:S(2)}, u32[]{:S(2)}) collective-permute-start(bf16[128,384]{1,0:T(8,128)(2,1)S(1)} %collective-permute-done.16.refs_1_), channel_id=1, source_target_pairs={{0,1},{1,0},{2,3},{3,2},{4,5},{5,4},{6,7},{7,6},{8,9},{9,8},{10,11... | collective-permute-start | bytes 294920 | tf_op jit(solution)/shard_map/ppermute | solution.py:279
  75.8 1.9 %collective-permute-start.21 = (bf16[128,384]{1,0:T(8,128)(2,1)S(1)}, bf16[128,384]{1,0:T(8,128)(2,1)S(1)}, u32[]{:S(2)}, u32[]{:S(2)}) collective-permute-start(bf16[128,384]{1,0:T(8,128)(2,1)S(1)} %collective-permute-done.19.refs_4_), channel_id=1, source_target_pairs={{0,1},{1,0},{2,3},{3,2},{4,5},{5,4},{6,7},{7,6},{8,9},{9,8},{10,11... | collective-permute-start | bytes 294920 | tf_op jit(solution)/shard_map/ppermute | solution.py:279
  77.2 1.3 %collective-permute-start.22 = (bf16[128,384]{1,0:T(8,128)(2,1)S(1)}, bf16[128,384]{1,0:T(8,128)(2,1)S(1)}, u32[]{:S(2)}, u32[]{:S(2)}) collective-permute-start(bf16[128,384]{1,0:T(8,128)(2,1)S(1)} %collective-permute-done.20.refs_5_), channel_id=1, source_target_pairs={{0,1},{1,0},{2,3},{3,2},{4,5},{5,4},{6,7},{7,6},{8,9},{9,8},{10,11... | collective-permute-start | bytes 294920 | tf_op jit(solution)/shard_map/ppermute | solution.py:279

commit v7 on v6

--- a/solution.py
+++ b/solution.py
@@ -191,16 +191,34 @@
         out[...] = (keep_ref[at].astype(F32) + got_ref[at].astype(F32)).astype(out.dtype)
 
 
-def head_kernel(segments, place_ref, win_ref, b_ref, counts_ref, *refs):
-    blocks, (*pieces, o_ref, x_ref) = refs[:8], refs[8:]
-    place_blocks(place_ref, blocks, x_ref)
-    logits = b_ref[...]
-    for by, piece in enumerate(pieces):
-        rows = block_rows(x_ref, segments, win_ref, by, len(pieces))
-        logits = logits + jnp.dot(rows, piece[...], preferred_element_type=F32)
-    tracks = jax.nn.softplus(logits).astype(BF16)
+def gene_sums(logits, b_ref, counts_ref, o_ref):
+    tracks = jax.nn.softplus(logits + b_ref[...]).astype(BF16)
     sums = jnp.dot(counts_ref[...], tracks, preferred_element_type=F32)
     o_ref[...] = sums.astype(o_ref.dtype)
+
+
+def head_kernel(segments, place_ref, win_ref, b_ref, counts_ref, *refs):
+    blocks, (w_ref, o_ref, x_ref) = refs[:8], refs[8:]
+    place_blocks(place_ref, blocks, x_ref)
+    rows = block_rows(x_ref, segments, win_ref, 0, 1)
+    gene_sums(jnp.dot(rows, w_ref[...], preferred_element_type=F32), b_ref, counts_ref, o_ref)
+
+
+def near_head_kernel(segments, place_ref, win_ref, *refs):
+    blocks, (own, below, above, logits_ref, rows_ref, x_ref) = refs[:8], refs[8:]
+    place_blocks(place_ref, blocks, x_ref)
+    logits = None
+    for by, piece in ((0, own), (1, below), (3, above)):
+        rows = block_rows(x_ref, segments, win_ref, by, 4)
+        term = jnp.dot(rows, piece[...], preferred_element_type=F32)
+        logits = term if logits is None else logits + term
+    logits_ref[...] = logits
+    rows_ref[...] = block_rows(x_ref, segments, win_ref, 2, 4)
+
+
+def far_head_kernel(logits_ref, rows_ref, w_ref, b_ref, counts_ref, o_ref):
+    term = jnp.dot(rows_ref[...], w_ref[...], preferred_element_type=F32)
+    gene_sums(logits_ref[...] + term, b_ref, counts_ref, o_ref)
 
 
 def gene_counts(ranges, bins):
@@ -326,10 +344,10 @@
             turned_by(partials[1], 1, -1),
             turned_by(partials[2], 2, 2),
         ]
-        qkv_pieces = first_stage(qkv_own, 1, arrived[0], arrived[0])
-        out_pieces = first_stage(out_own, 1, (), ())
+        qkv_pieces = first_stage(qkv_own, 1, (), arrived[0])
+        out_pieces = first_stage(out_own, 1, partials[0], partials[0])
         both = [jnp.concatenate(x, axis=0) for x in zip(qkv_pieces, out_pieces)]
-        attention_pieces = [*qkv_pieces, *out_pieces, across(both, returned[:2])]
+        attention_pieces = [*qkv_pieces, *out_pieces, across(both, returned[1])]
         for x in returned:
             conv_pre = conv_pre + x.astype(F32)
     else:
@@ -338,12 +356,13 @@
         own_feats = lax.dynamic_slice(own_bins, (reach, model_index * out_cols), (bins, out_cols))
         blocks = own_bins.reshape(own_bins.shape[0], windows, row_count).transpose(1, 0, 2)
         arrived = lax.all_to_all(blocks, "win", 0, 0, tiled=True)
-        attention_pieces = first_stage(qkv_own, 1) + first_stage(out_own, 1)
+        qkv_pieces = first_stage(qkv_own, 1)
+        attention_pieces = qkv_pieces + first_stage(out_own, 1)
         partial = jnp.stack([conv_of(BF16, arrived[w]) for w in range(windows)])
         conv_pre = lax.all_to_all(partial, "win", 0, 0, tiled=True).astype(F32).sum(axis=0)
 
     conv_out = (own_feats + jax.nn.gelu(conv_pre + conv_bias)).astype(BF16)
-    head_pieces = first_stage(head_own, 0, conv_out, conv_out)
+    head_pieces = first_stage(head_own, 0, qkv_pieces[1:], conv_out)
     if stepwise:
         head_pieces.insert(2, across(head_pieces, ()))
     all_chan = lax.all_gather(conv_out, plane, axis=0)
@@ -376,17 +395,38 @@
     resid = (conv_out.astype(F32) + summed).astype(BF16)
     all_resid = plane_blocks(resid)
 
-    sums = call_kernel(
-        functools.partial(head_kernel, segments),
-        jax.ShapeDtypeStruct((counts.shape[0], track_cols), BF16),
-        place,
-        win_ref,
-        bias_part[None, :],
-        counts,
-        *all_resid,
-        *head_pieces,
-        scratch=all_blocks,
-    )
+    sums_shape = jax.ShapeDtypeStruct((counts.shape[0], track_cols), BF16)
+    if stepwise:
+        own, below, far, above = head_pieces
+        logits, far_rows = call_kernel(
+            functools.partial(near_head_kernel, segments),
+            [
+                jax.ShapeDtypeStruct((bin_count, track_cols), F32),
+                jax.ShapeDtypeStruct((bin_count, row_count), BF16),
+            ],
+            place,
+            win_ref,
+            *all_resid,
+            own,
+            below,
+            above,
+            scratch=all_blocks,
+        )
+        sums = call_kernel(
+            far_head_kernel, sums_shape, logits, far_rows, far, bias_part[None, :], counts
+        )
+    else:
+        sums = call_kernel(
+            functools.partial(head_kernel, segments),
+            sums_shape,
+            place,
+            win_ref,
+            bias_part[None, :],
+            counts,
+            *all_resid,
+            *head_pieces,
+            scratch=all_blocks,
+        )
     owners = segments * windows
     got = lax.all_to_all(
         sums.reshape(owners, GENE_DEV, track_cols), ("segment", "win"), 0, 0, tiled=True

time: 92 us -> 90.2 us (0.980)
  starting transfers between devices: 34.1 us -> 32.9 us
    ppermute x6, starting transfers between devices: 9.78 us -> 7.65 us  [shifted(): return lax.ppermute(x, axis, [(i, (i + by) % size) for i in range(size)])]
    ppermute x5, starting transfers between devices: 12.1 us -> 14 us  [turned_by(): return lax.ppermute(x, ('win', 'mp'), pairs)]
    ppermute x6, waiting for transfers between devices: 7.07 us -> 8.05 us  [shifted(): return lax.ppermute(x, axis, [(i, (i + by) % size) for i in range(size)])]
    pallas_call x10 -> x11, Pallas kernels: 9.65 us -> 9.82 us  [call_kernel(): pl.pallas_call(body, out_shape=out_shape, in_specs=[scalars if x.dtype ==...]
  transfers between devices with their start and end apart: 26 -> 26, of which waited for: 11 -> 9; matrix products, arithmetic and copies ran while one was open for 1% -> 1% of each run, Pallas kernels for 8% -> 9%
where the time goes in v7:
time: 90.2 us; the launch traced here: 89.9 us
  starting transfers between devices  32.9 us (36%)
  waiting for transfers between devices  21.4 us (24%)
  blocking collectives  20.5 us (23%)
  Pallas kernels  9.82 us (11%)
  local copies, waits for them, and re-layouts  3.98 us (4%)
  other arithmetic  0.96 us (1%)
    ppermute x5, starting transfers between devices, turned_by(): return lax.ppermute(x, ('win', 'mp'), pairs)  14 us
    all_gather x1, blocking collectives, local(): all_chan = lax.all_gather(conv_out, plane, axis=0)  10.4 us
    all_to_all x1, blocking collectives, local(): lax.all_to_all(sums.reshape(owners, GENE_DEV, track_cols), ('segment', 'w...  10.1 us
    pallas_call x11, Pallas kernels, call_kernel(): pl.pallas_call(body, out_shape=out_shape, in_specs=[scalars if x.dtype ==...  9.82 us
    ppermute x6, waiting for transfers between devices, shifted(): return lax.ppermute(x, axis, [(i, (i + by) % size) for i in range(size)])  8.05 us
    ppermute x6, starting transfers between devices, shifted(): return lax.ppermute(x, axis, [(i, (i + by) % size) for i in range(size)])  7.65 us
    ppermute x5, waiting for transfers between devices, turned_by(): return lax.ppermute(x, ('win', 'mp'), pairs)  5.75 us
    ppermute x3, waiting for transfers between devices, over_plane(): return lax.ppermute(x, plane, pairs)  4.94 us
  transfers between devices with their start and end apart: 26, of which 9 were waited for; matrix products, arithmetic and copies ran while one was open for 1% of the time, Pallas kernels for 9%

profile of v7, /device:TPU:0, one launch (start us, length us, event | category | flops | bytes accessed | tf_op | source)
XLA Modules:
  0.0 89.9 jit_solution(9886809262484373304)
XLA Ops:
  0.1 1.2 %copy-done.1 = bf16[1,1536,256]{2,1,0:T(8,128)(2,1)S(1)} copy-done((bf16[1,1536,256]{2,1,0:T(8,128)(2,1)S(1)}, bf16[1,1536,256]{2,1,0:T(8,128)(2,1)}, u32[]{:S(2)}) %copy-start.1) | copy-done | bytes 786456
  1.3 0.9 shard_map.82
  2.2 3.1 %collective-permute-start = (bf16[144,384]{1,0:T(8,128)(2,1)S(1)}, bf16[144,384]{1,0:T(8,128)(2,1)S(1)}, u32[]{:S(2)}, u32[]{:S(2)}) collective-permute-start(bf16[144,384]{1,0:T(8,128)(2,1)S(1)} %get-tuple-element.24), channel_id=1, source_target_pairs={{0,4},{1,13},{2,6},{3,15},{4,8},{5,1},{6,10},{7,3},{8,12},{9,5},{1... | collective-permute-start | bytes 331784 | tf_op jit(solution)/shard_map/ppermute | solution.py:331
  5.3 2.6 %collective-permute-start.4 = (bf16[80,384]{1,0:T(8,128)(2,1)S(1)}, bf16[80,384]{1,0:T(8,128)(2,1)S(1)}, u32[]{:S(2)}, u32[]{:S(2)}) collective-permute-start(bf16[80,384]{1,0:T(8,128)(2,1)S(1)} %get-tuple-element.25), channel_id=1, source_target_pairs={{0,8},{1,9},{2,10},{3,11},{4,12},{5,13},{6,14},{7,15},{8,0},{9,1},... | collective-permute-start | bytes 184328 | tf_op jit(solution)/shard_map/ppermute | solution.py:331
  7.8 1.0 %copy-done.2 = bf16[384,640]{1,0:T(8,128)(2,1)S(1)} copy-done((bf16[384,640]{1,0:T(8,128)(2,1)S(1)}, bf16[384,640]{1,0:T(8,128)(2,1)}, u32[]{:S(2)}) %copy-start.2) | copy-done | bytes 491544
  8.9 0.7 shard_map.87.refs_0_
  9.6 0.1 collective-permute-start.7
  9.7 1.5 %collective-permute-done.x_ref = bf16[144,384]{1,0:T(8,128)(2,1)S(1)} collective-permute-done((bf16[144,384]{1,0:T(8,128)(2,1)S(1)}, bf16[144,384]{1,0:T(8,128)(2,1)S(1)}, u32[]{:S(2)}, u32[]{:S(2)}) %collective-permute-start) | collective-permute-done | bytes 110624 | tf_op jit(solution)/shard_map/ppermute | solution.py:331
  11.2 2.5 %collective-permute-start.8 = (bf16[320,384]{1,0:T(8,128)(2,1)S(1)}, bf16[320,384]{1,0:T(8,128)(2,1)S(1)}, u32[]{:S(2)}, u32[]{:S(2)}) collective-permute-start(bf16[320,384]{1,0:T(8,128)(2,1)S(1)} %shard_map.87.refs_0_), channel_id=1, source_target_pairs={{0,12},{4,0},{8,4},{12,8},{1,13},{5,1},{9,5},{13,9},{2,14},{6,2},{... | collective-permute-start | bytes 737288 | tf_op jit(solution)/shard_map/ppermute | solution.py:37
  13.8 1.0 %copy-done.3 = bf16[384,384]{1,0:T(8,128)(2,1)S(1)} copy-done((bf16[384,384]{1,0:T(8,128)(2,1)S(1)}, bf16[384,384]{1,0:T(8,128)(2,1)}, u32[]{:S(2)}) %copy-start.3) | copy-done | bytes 294936
  14.7 0.7 shard_map.88.refs_3_
  15.4 0.5 shard_map.83
  15.9 0.5 shard_map.84
  16.4 3.0 %collective-permute-start.10 = (bf16[192,384]{1,0:T(8,128)(2,1)S(1)}, bf16[192,384]{1,0:T(8,128)(2,1)S(1)}, u32[]{:S(2)}, u32[]{:S(2)}) collective-permute-start(bf16[192,384]{1,0:T(8,128)(2,1)S(1)} %shard_map.88.refs_3_), channel_id=1, source_target_pairs={{0,12},{4,0},{8,4},{12,8},{1,13},{5,1},{9,5},{13,9},{2,14},{6,2},{... | collective-permute-start | bytes 442376 | tf_op jit(solution)/shard_map/ppermute | solution.py:37
  19.3 0.2 collective-permute-start.2
  19.6 1.0 %shard_map.86 = bf16[128,384]{1,0:T(8,128)(2,1)S(1)} custom-call(s32[3]{0:T(128)S(1)} %pad_add_fusion.place_ref, bf16[80,384]{1,0:T(8,128)(2,1)S(1)} %collective-permute-done.4.own_ref, bf16[80,384]{1,0:T(8,128)(2,1)S(1)} %collective-permute-done.5.other_ref, bf16[5,384,384]{2,1,0:T(8,128)(2,1)S(1)} %bitcast.25), custom_call_target="tpu_custom_call" | custom-call | flops 188743680 | bytes 1048576 | tf_op jit(solution)/shard_map/pallas_call | solution.py:24
  20.6 3.8 %collective-permute-start.1 = (bf16[128,384]{1,0:T(8,128)(2,1)S(1)}, bf16[128,384]{1,0:T(8,128)(2,1)S(1)}, u32[]{:S(2)}, u32[]{:S(2)}) collective-permute-start(bf16[128,384]{1,0:T(8,128)(2,1)S(1)} %shard_map.84), channel_id=1, source_target_pairs={{0,12},{1,5},{2,14},{3,7},{4,0},{5,9},{6,2},{7,11},{8,4},{9,13},{1... | collective-permute-start | bytes 294920 | tf_op jit(solution)/shard_map/ppermute | solution.py:331
  24.5 0.5 shard_map.85
  24.9 4.5 %collective-permute-start.6 = (bf16[128,384]{1,0:T(8,128)(2,1)S(1)}, bf16[128,384]{1,0:T(8,128)(2,1)S(1)}, u32[]{:S(2)}, u32[]{:S(2)}) collective-permute-start(bf16[128,384]{1,0:T(8,128)(2,1)S(1)} %shard_map.86), channel_id=1, source_target_pairs={{0,8},{1,9},{2,10},{3,11},{4,12},{5,13},{6,14},{7,15},{8,0},{9,1},... | collective-permute-start | bytes 294920 | tf_op jit(solution)/shard_map/ppermute | solution.py:331
  29.4 2.6 %collective-permute-done.9.refs_4_ = bf16[192,384]{1,0:T(8,128)(2,1)S(1)} collective-permute-done((bf16[192,384]{1,0:T(8,128)(2,1)S(1)}, bf16[192,384]{1,0:T(8,128)(2,1)S(1)}, u32[]{:S(2)}, u32[]{:S(2)}) %collective-permute-start.9) | collective-permute-done | bytes 147488 | tf_op jit(solution)/shard_map/ppermute | solution.py:37
  32.0 0.1 maximum_select_fusion
  32.2 4.2 %collective-permute-done.3 = bf16[128,384]{1,0:T(8,128)(2,1)S(1)} collective-permute-done((bf16[128,384]{1,0:T(8,128)(2,1)S(1)}, bf16[128,384]{1,0:T(8,128)(2,1)S(1)}, u32[]{:S(2)}, u32[]{:S(2)}) %collective-permute-start.3) | collective-permute-done | bytes 98336 | tf_op jit(solution)/shard_map/ppermute | solution.py:331
  36.4 3.7 %collective-permute-start.11 = (bf16[512,384]{1,0:T(8,128)(2,1)S(1)}, bf16[512,384]{1,0:T(8,128)(2,1)S(1)}, u32[]{:S(2)}, u32[]{:S(2)}) collective-permute-start(bf16[512,384]{1,0:T(8,128)(2,1)S(1)} %maximum_select_fusion), channel_id=1, source_target_pairs={{0,8},{4,0},{8,12},{12,4},{1,9},{5,1},{9,13},{13,5},{2,10},{6,2},{... | collective-permute-start | bytes 1179656 | tf_op jit(solution)/shard_map/ppermute | solution.py:278
  40.1 0.1 fusion.8
  40.3 0.5 collective-permute-start.24
  40.8 10.4 %all-gather = bf16[1024,384]{1,0:T(8,128)(2,1)S(1)} all-gather(bf16[128,384]{1,0:T(8,128)(2,1)S(1)} %fusion.8), channel_id=2, replica_groups=mesh['segment'=2,'win'=4,'mp'=4] {'segment','mp'}, dimensions={0}, use_global_device_ids=true | all-gather | bytes 884736 | tf_op jit(solution)/shard_map/all_gather | solution.py:368
  51.2 1.6 %collective-permute-start.23 = (bf16[384,512]{1,0:T(8,128)(2,1)S(1)}, bf16[384,512]{1,0:T(8,128)(2,1)S(1)}, u32[]{:S(2)}, u32[]{:S(2)}) collective-permute-start(bf16[384,512]{1,0:T(8,128)(2,1)S(1)} %constant_dynamic-slice_fusion.refs_8_), channel_id=1, source_target_pairs={{0,4},{4,8},{8,12},{12,0},{1,5},{5,9},{9,13},{13,1},{2,6},{6,10},{... | collective-permute-start | bytes 1179656 | tf_op jit(solution)/shard_map/ppermute | solution.py:37
  52.8 2.7 %shard_map.89 = (bf16[4,128,384]{2,1,0:T(8,128)(2,1)S(1)}, bf16[4,128,384]{2,1,0:T(8,128)(2,1)S(1)}) custom-call(s32[3]{0:T(128)S(1)} %pad_add_fusion.place_ref, s32[1]{0:T(128)} %bitcast.1.win_ref, bf16[8,128,384]{2,1,0:T(8,128)(2,1)S(1)} %bitcast.27, bf16[320,384]{1,0:T(8,128)(2,1)S(1)} %shard_map.87.refs_0_, ...), custom_call_target="tpu_custom_call" | custom-call | bytes 1048576 | tf_op jit(solution)/shard_map/pallas_call | solution.py:24
  55.5 0.1 collective-permute-start.12
  55.7 1.6 %collective-permute-done.12.got_ref = bf16[4,128,384]{2,1,0:T(8,128)(2,1)S(1)} collective-permute-done((bf16[4,128,384]{2,1,0:T(8,128)(2,1)S(1)}, bf16[4,128,384]{2,1,0:T(8,128)(2,1)S(1)}, u32[]{:S(2)}, u32[]{:S(2)}) %collective-permute-start.12) | collective-permute-done | bytes 393248 | tf_op jit(solution)/shard_map/ppermute | solution.py:297
  57.3 0.6 shard_map.90
  57.9 1.6 %collective-permute-start.13 = (bf16[128,384]{1,0:T(8,128)(2,1)S(1)}, bf16[128,384]{1,0:T(8,128)(2,1)S(1)}, u32[]{:S(2)}, u32[]{:S(2)}) collective-permute-start(bf16[128,384]{1,0:T(8,128)(2,1)S(1)} %get-tuple-element.32), channel_id=1, source_target_pairs={{0,16},{1,17},{2,18},{3,19},{16,0},{17,1},{18,2},{19,3},{4,20},{5,... | collective-permute-start | bytes 294920 | tf_op jit(solution)/shard_map/ppermute | solution.py:394
  59.5 0.5 collective-permute-start.14
  60.0 1.5 %collective-permute-start.15 = (bf16[128,384]{1,0:T(8,128)(2,1)S(1)}, bf16[128,384]{1,0:T(8,128)(2,1)S(1)}, u32[]{:S(2)}, u32[]{:S(2)}) collective-permute-start(bf16[128,384]{1,0:T(8,128)(2,1)S(1)} %get-tuple-element.34), channel_id=1, source_target_pairs={{0,18},{1,19},{2,16},{3,17},{16,2},{17,3},{18,0},{19,1},{4,22},{5,... | collective-permute-start | bytes 294920 | tf_op jit(solution)/shard_map/ppermute | solution.py:394
  61.5 5.5 %collective-permute-done.23.refs_9_ = bf16[384,512]{1,0:T(8,128)(2,1)S(1)} collective-permute-done((bf16[384,512]{1,0:T(8,128)(2,1)S(1)}, bf16[384,512]{1,0:T(8,128)(2,1)S(1)}, u32[]{:S(2)}, u32[]{:S(2)}) %collective-permute-start.23) | collective-permute-done | bytes 393248 | tf_op jit(solution)/shard_map/ppermute | solution.py:37
  66.9 0.2 select_select_fusion
  67.3 1.6 %collective-permute-start.16 = (bf16[128,384]{1,0:T(8,128)(2,1)S(1)}, bf16[128,384]{1,0:T(8,128)(2,1)S(1)}, u32[]{:S(2)}, u32[]{:S(2)}) collective-permute-start(bf16[128,384]{1,0:T(8,128)(2,1)S(1)} %add_convert_fusion.refs_0_), channel_id=1, source_target_pairs={{0,16},{1,17},{2,18},{3,19},{16,0},{17,1},{18,2},{19,3},{4,20},{5,... | collective-permute-start | bytes 294920 | tf_op jit(solution)/shard_map/ppermute | solution.py:305
  68.9 1.5 %collective-permute-start.19 = (bf16[128,384]{1,0:T(8,128)(2,1)S(1)}, bf16[128,384]{1,0:T(8,128)(2,1)S(1)}, u32[]{:S(2)}, u32[]{:S(2)}) collective-permute-start(bf16[128,384]{1,0:T(8,128)(2,1)S(1)} %add_convert_fusion.refs_0_), channel_id=1, source_target_pairs={{0,2},{1,3},{2,0},{3,1},{16,18},{17,19},{18,16},{19,17},{4,6},{5,7... | collective-permute-start | bytes 294920 | tf_op jit(solution)/shard_map/ppermute | solution.py:305
  70.4 0.4 collective-permute-start.20
  71.0 1.0 %collective-permute-done.16.refs_1_ = bf16[128,384]{1,0:T(8,128)(2,1)S(1)} collective-permute-done((bf16[128,384]{1,0:T(8,128)(2,1)S(1)}, bf16[128,384]{1,0:T(8,128)(2,1)S(1)}, u32[]{:S(2)}, u32[]{:S(2)}) %collective-permute-start.16) | collective-permute-done | bytes 98336 | tf_op jit(solution)/shard_map/ppermute | solution.py:305
  72.0 2.6 %collective-permute-done.19.refs_4_ = bf16[128,384]{1,0:T(8,128)(2,1)S(1)} collective-permute-done((bf16[128,384]{1,0:T(8,128)(2,1)S(1)}, bf16[128,384]{1,0:T(8,128)(2,1)S(1)}, u32[]{:S(2)}, u32[]{:S(2)}) %collective-permute-start.19) | collective-permute-done | bytes 98336 | tf_op jit(solution)/shard_map/ppermute | solution.py:305
  74.6 1.4 %collective-permute-done.20.refs_5_ = bf16[128,384]{1,0:T(8,128)(2,1)S(1)} collective-permute-done((bf16[128,384]{1,0:T(8,128)(2,1)S(1)}, bf16[128,384]{1,0:T(8,128)(2,1)S(1)}, u32[]{:S(2)}, u32[]{:S(2)}) %collective-permute-start.20) | collective-permute-done | bytes 98336 | tf_op jit(solution)/shard_map/ppermute | solution.py:305
  75.9 0.2 convert_reduce_fusion
  76.2 1.0 %collective-permute-done.22.refs_7_ = bf16[128,384]{1,0:T(8,128)(2,1)S(1)} collective-permute-done((bf16[128,384]{1,0:T(8,128)(2,1)S(1)}, bf16[128,384]{1,0:T(8,128)(2,1)S(1)}, u32[]{:S(2)}, u32[]{:S(2)}) %collective-permute-start.22) | collective-permute-done | bytes 98336 | tf_op jit(solution)/shard_map/ppermute | solution.py:297
  77.2 1.2 %shard_map.91 = (f32[256,512]{1,0:T(8,128)S(1)}, bf16[256,384]{1,0:T(8,128)(2,1)S(1)}) custom-call(s32[3]{0:T(128)S(1)} %pad_add_fusion.place_ref, s32[1]{0:T(128)} %bitcast.1.win_ref, bf16[128,384]{1,0:T(8,128)(2,1)S(1)} %add_convert_fusion.refs_0_, bf16[128,384]{1,0:T(8,128)(2,1)S(1)} %collective-permute-done.16.refs_1_, ...), custom_call_target="tpu_custom_call" | custom-call | bytes 1048576 | tf_op jit(solution)/shard_map/pallas_call | solution.py:24
  78.4 0.7 shard_map.92
  79.1 10.1 %all_to_all.5 = bf16[8,8,512]{2,1,0:T(8,128)(2,1)S(1)} all-to-all(bf16[8,8,512]{2,1,0:T(8,128)(2,1)S(1)} %bitcast.29), channel_id=1, replica_groups=mesh['segment'=2,'win'=4,'mp'=4] {'segment','win'}, dimensions={0} | all-to-all | bytes 131072 | tf_op jit(solution)/shard_map/all_to_all | solution.py:431
  89.3 0.6 log1p.9
  (46 shorter events, 0.6 us)
Async XLA Ops:
  0.0 15.4 %copy-start = (bf16[384,5,384]{2,0,1:T(8,128)(2,1)S(1)}, bf16[384,5,384]{2,0,1:T(8,128)(2,1)}, u32[]{:S(2)}) copy-start(bf16[384,5,384]{2,0,1:T(8,128)(2,1)} %param.9) | copy-start | bytes 4423684
  0.1 1.2 %copy-start.1 = (bf16[1,1536,256]{2,1,0:T(8,128)(2,1)S(1)}, bf16[1,1536,256]{2,1,0:T(8,128)(2,1)}, u32[]{:S(2)}) copy-start(bf16[1,1536,256]{2,1,0:T(8,128)(2,1)} %param.8) | copy-start | bytes 2359300
  2.2 9.1 %collective-permute-start = (bf16[144,384]{1,0:T(8,128)(2,1)S(1)}, bf16[144,384]{1,0:T(8,128)(2,1)S(1)}, u32[]{:S(2)}, u32[]{:S(2)}) collective-permute-start(bf16[144,384]{1,0:T(8,128)(2,1)S(1)} %get-tuple-element.24), channel_id=1, source_target_pairs={{0,4},{1,13},{2,6},{3,15},{4,8},{5,1},{6,10},{7,3},{8,12},{9,5},{1... | collective-permute-start | bytes 331784 | tf_op jit(solution)/shard_map/ppermute | solution.py:331
  5.3 8.5 %collective-permute-start.4 = (bf16[80,384]{1,0:T(8,128)(2,1)S(1)}, bf16[80,384]{1,0:T(8,128)(2,1)S(1)}, u32[]{:S(2)}, u32[]{:S(2)}) collective-permute-start(bf16[80,384]{1,0:T(8,128)(2,1)S(1)} %get-tuple-element.25), channel_id=1, source_target_pairs={{0,8},{1,9},{2,10},{3,11},{4,12},{5,13},{6,14},{7,15},{8,0},{9,1},... | collective-permute-start | bytes 184328 | tf_op jit(solution)/shard_map/ppermute | solution.py:331
  7.8 1.0 %copy-start.2 = (bf16[384,640]{1,0:T(8,128)(2,1)S(1)}, bf16[384,640]{1,0:T(8,128)(2,1)}, u32[]{:S(2)}) copy-start(bf16[384,640]{1,0:T(8,128)(2,1)} %x_ref.2) | copy-start | bytes 1474564
  9.6 15.3 %collective-permute-start.7 = (bf16[320,384]{1,0:T(8,128)(2,1)S(1)}, bf16[320,384]{1,0:T(8,128)(2,1)S(1)}, u32[]{:S(2)}, u32[]{:S(2)}) collective-permute-start(bf16[320,384]{1,0:T(8,128)(2,1)S(1)} %shard_map.87.refs_0_), channel_id=1, source_target_pairs={{0,4},{4,8},{8,12},{12,0},{1,5},{5,9},{9,13},{13,1},{2,6},{6,10},{... | collective-permute-start | bytes 737288 | tf_op jit(solution)/shard_map/ppermute | solution.py:37
  11.2 20.8 %collective-permute-start.8 = (bf16[320,384]{1,0:T(8,128)(2,1)S(1)}, bf16[320,384]{1,0:T(8,128)(2,1)S(1)}, u32[]{:S(2)}, u32[]{:S(2)}) collective-permute-start(bf16[320,384]{1,0:T(8,128)(2,1)S(1)} %shard_map.87.refs_0_), channel_id=1, source_target_pairs={{0,12},{4,0},{8,4},{12,8},{1,13},{5,1},{9,5},{13,9},{2,14},{6,2},{... | collective-permute-start | bytes 737288 | tf_op jit(solution)/shard_map/ppermute | solution.py:37
  13.7 5.6 %collective-permute-start.5 = (bf16[80,384]{1,0:T(8,128)(2,1)S(1)}, bf16[80,384]{1,0:T(8,128)(2,1)S(1)}, u32[]{:S(2)}, u32[]{:S(2)}) collective-permute-start(bf16[80,384]{1,0:T(8,128)(2,1)S(1)} %collective-permute-done.4.own_ref), channel_id=1, source_target_pairs={{0,1},{1,0},{2,3},{3,2},{4,5},{5,4},{6,7},{7,6},{8,9},{9,8},{10,11... | collective-permute-start | bytes 184328 | tf_op jit(solution)/shard_map/ppermute | solution.py:297
  13.7 1.0 %copy-start.3 = (bf16[384,384]{1,0:T(8,128)(2,1)S(1)}, bf16[384,384]{1,0:T(8,128)(2,1)}, u32[]{:S(2)}) copy-start(bf16[384,384]{1,0:T(8,128)(2,1)} %x_ref.3) | copy-start | bytes 884740
  15.4 4.1 %copy-start.4 = (bf16[384,1024]{1,0:T(8,128)(2,1)S(1)}, bf16[384,1024]{1,0:T(8,128)(2,1)}, u32[]{:S(2)}) copy-start(bf16[384,1024]{1,0:T(8,128)(2,1)} %param.13) | copy-start | bytes 2359300
  16.4 13.1 %collective-permute-start.10 = (bf16[192,384]{1,0:T(8,128)(2,1)S(1)}, bf16[192,384]{1,0:T(8,128)(2,1)S(1)}, u32[]{:S(2)}, u32[]{:S(2)}) collective-permute-start(bf16[192,384]{1,0:T(8,128)(2,1)S(1)} %shard_map.88.refs_3_), channel_id=1, source_target_pairs={{0,12},{4,0},{8,4},{12,8},{1,13},{5,1},{9,5},{13,9},{2,14},{6,2},{... | collective-permute-start | bytes 442376 | tf_op jit(solution)/shard_map/ppermute | solution.py:37
  19.3 12.7 %collective-permute-start.9 = (bf16[192,384]{1,0:T(8,128)(2,1)S(1)}, bf16[192,384]{1,0:T(8,128)(2,1)S(1)}, u32[]{:S(2)}, u32[]{:S(2)}) collective-permute-start(bf16[192,384]{1,0:T(8,128)(2,1)S(1)} %shard_map.88.refs_3_), channel_id=1, source_target_pairs={{0,4},{4,8},{8,12},{12,0},{1,5},{5,9},{9,13},{13,1},{2,6},{6,10},{... | collective-permute-start | bytes 442376 | tf_op jit(solution)/shard_map/ppermute | solution.py:37
  19.3 1.3 %collective-permute-start.2 = (bf16[144,384]{1,0:T(8,128)(2,1)S(1)}, bf16[144,384]{1,0:T(8,128)(2,1)S(1)}, u32[]{:S(2)}, u32[]{:S(2)}) collective-permute-start(bf16[144,384]{1,0:T(8,128)(2,1)S(1)} %collective-permute-done.x_ref), channel_id=1, source_target_pairs={{0,1},{1,0},{2,3},{3,2},{4,5},{5,4},{6,7},{7,6},{8,9},{9,8},{10,11... | collective-permute-start | bytes 331784 | tf_op jit(solution)/shard_map/ppermute | solution.py:297
  20.6 19.5 %copy-start.6 = (f32[384]{0:T(512)S(1)}, f32[384]{0:T(512)}, u32[]{:S(2)}) copy-start(f32[384]{0:T(512)} %param.10) | copy-start | bytes 4612
  20.6 19.5 %collective-permute-start.1 = (bf16[128,384]{1,0:T(8,128)(2,1)S(1)}, bf16[128,384]{1,0:T(8,128)(2,1)S(1)}, u32[]{:S(2)}, u32[]{:S(2)}) collective-permute-start(bf16[128,384]{1,0:T(8,128)(2,1)S(1)} %shard_map.84), channel_id=1, source_target_pairs={{0,12},{1,5},{2,14},{3,7},{4,0},{5,9},{6,2},{7,11},{8,4},{9,13},{1... | collective-permute-start | bytes 294920 | tf_op jit(solution)/shard_map/ppermute | solution.py:331
  24.9 15.2 %collective-permute-start.6 = (bf16[128,384]{1,0:T(8,128)(2,1)S(1)}, bf16[128,384]{1,0:T(8,128)(2,1)S(1)}, u32[]{:S(2)}, u32[]{:S(2)}) collective-permute-start(bf16[128,384]{1,0:T(8,128)(2,1)S(1)} %shard_map.86), channel_id=1, source_target_pairs={{0,8},{1,9},{2,10},{3,11},{4,12},{5,13},{6,14},{7,15},{8,0},{9,1},... | collective-permute-start | bytes 294920 | tf_op jit(solution)/shard_map/ppermute | solution.py:331
  29.4 6.9 %collective-permute-start.3 = (bf16[128,384]{1,0:T(8,128)(2,1)S(1)}, bf16[128,384]{1,0:T(8,128)(2,1)S(1)}, u32[]{:S(2)}, u32[]{:S(2)}) collective-permute-start(bf16[128,384]{1,0:T(8,128)(2,1)S(1)} %shard_map.85), channel_id=1, source_target_pairs={{0,4},{1,13},{2,6},{3,15},{4,8},{5,1},{6,10},{7,3},{8,12},{9,5},{1... | collective-permute-start | bytes 294920 | tf_op jit(solution)/shard_map/ppermute | solution.py:331
  36.4 16.4 %collective-permute-start.11 = (bf16[512,384]{1,0:T(8,128)(2,1)S(1)}, bf16[512,384]{1,0:T(8,128)(2,1)S(1)}, u32[]{:S(2)}, u32[]{:S(2)}) collective-permute-start(bf16[512,384]{1,0:T(8,128)(2,1)S(1)} %maximum_select_fusion), channel_id=1, source_target_pairs={{0,8},{4,0},{8,12},{12,4},{1,9},{5,1},{9,13},{13,5},{2,10},{6,2},{... | collective-permute-start | bytes 1179656 | tf_op jit(solution)/shard_map/ppermute | solution.py:278
  40.3 15.4 %copy-start.5 = (s32[3,1,8,8]{3,2,1,0:T(8,128)S(1)}, s32[3,1,8,8]{3,2,1,0:T(8,128)}, u32[]{:S(2)}) copy-start(s32[3,1,8,8]{3,2,1,0:T(8,128)} %param.15) | copy-start | bytes 2308
  40.3 21.2 %collective-permute-start.24 = (bf16[384,512]{1,0:T(8,128)(2,1)S(1)}, bf16[384,512]{1,0:T(8,128)(2,1)S(1)}, u32[]{:S(2)}, u32[]{:S(2)}) collective-permute-start(bf16[384,512]{1,0:T(8,128)(2,1)S(1)} %constant_dynamic-slice_fusion.refs_8_), channel_id=1, source_target_pairs={{0,12},{4,0},{8,4},{12,8},{1,13},{5,1},{9,5},{13,9},{2,14},{6,2},{... | collective-permute-start | bytes 1179656 | tf_op jit(solution)/shard_map/ppermute | solution.py:37
  51.2 15.8 %collective-permute-start.23 = (bf16[384,512]{1,0:T(8,128)(2,1)S(1)}, bf16[384,512]{1,0:T(8,128)(2,1)S(1)}, u32[]{:S(2)}, u32[]{:S(2)}) collective-permute-start(bf16[384,512]{1,0:T(8,128)(2,1)S(1)} %constant_dynamic-slice_fusion.refs_8_), channel_id=1, source_target_pairs={{0,4},{4,8},{8,12},{12,0},{1,5},{5,9},{9,13},{13,1},{2,6},{6,10},{... | collective-permute-start | bytes 1179656 | tf_op jit(solution)/shard_map/ppermute | solution.py:37
  55.5 1.8 %collective-permute-start.12 = (bf16[4,128,384]{2,1,0:T(8,128)(2,1)S(1)}, bf16[4,128,384]{2,1,0:T(8,128)(2,1)S(1)}, u32[]{:S(2)}, u32[]{:S(2)}) collective-permute-start(bf16[4,128,384]{2,1,0:T(8,128)(2,1)S(1)} %get-tuple-element.30), channel_id=1, source_target_pairs={{0,1},{1,0},{2,3},{3,2},{4,5},{5,4},{6,7},{7,6},{8,9},{9,8},{10,11... | collective-permute-start | bytes 1179656 | tf_op jit(solution)/shard_map/ppermute | solution.py:297
  57.3 13.6 %copy-start.7 = (f32[1024]{0:T(1024)S(1)}, f32[1024]{0:T(1024)}, u32[]{:S(2)}) copy-start(f32[1024]{0:T(1024)} %param.14) | copy-start | bytes 12292
  57.9 9.3 %collective-permute-start.13 = (bf16[128,384]{1,0:T(8,128)(2,1)S(1)}, bf16[128,384]{1,0:T(8,128)(2,1)S(1)}, u32[]{:S(2)}, u32[]{:S(2)}) collective-permute-start(bf16[128,384]{1,0:T(8,128)(2,1)S(1)} %get-tuple-element.32), channel_id=1, source_target_pairs={{0,16},{1,17},{2,18},{3,19},{16,0},{17,1},{18,2},{19,3},{4,20},{5,... | collective-permute-start | bytes 294920 | tf_op jit(solution)/shard_map/ppermute | solution.py:394
  59.5 7.7 %collective-permute-start.14 = (bf16[128,384]{1,0:T(8,128)(2,1)S(1)}, bf16[128,384]{1,0:T(8,128)(2,1)S(1)}, u32[]{:S(2)}, u32[]{:S(2)}) collective-permute-start(bf16[128,384]{1,0:T(8,128)(2,1)S(1)} %get-tuple-element.33), channel_id=1, source_target_pairs={{0,2},{1,3},{2,0},{3,1},{16,18},{17,19},{18,16},{19,17},{4,6},{5,7... | collective-permute-start | bytes 294920 | tf_op jit(solution)/shard_map/ppermute | solution.py:394
  60.0 7.2 %collective-permute-start.15 = (bf16[128,384]{1,0:T(8,128)(2,1)S(1)}, bf16[128,384]{1,0:T(8,128)(2,1)S(1)}, u32[]{:S(2)}, u32[]{:S(2)}) collective-permute-start(bf16[128,384]{1,0:T(8,128)(2,1)S(1)} %get-tuple-element.34), channel_id=1, source_target_pairs={{0,18},{1,19},{2,16},{3,17},{16,2},{17,3},{18,0},{19,1},{4,22},{5,... | collective-permute-start | bytes 294920 | tf_op jit(solution)/shard_map/ppermute | solution.py:394
  67.1 11.3 %collective-permute-start.25 = (bf16[384,512]{1,0:T(8,128)(2,1)S(1)}, bf16[384,512]{1,0:T(8,128)(2,1)S(1)}, u32[]{:S(2)}, u32[]{:S(2)}) collective-permute-start(bf16[384,512]{1,0:T(8,128)(2,1)S(1)} %select_select_fusion), channel_id=1, source_target_pairs={{0,8},{4,0},{8,12},{12,4},{1,9},{5,1},{9,13},{13,5},{2,10},{6,2},{... | collective-permute-start | bytes 1179656 | tf_op jit(solution)/shard_map/ppermute | solution.py:278
  67.3 4.7 %collective-permute-start.16 = (bf16[128,384]{1,0:T(8,128)(2,1)S(1)}, bf16[128,384]{1,0:T(8,128)(2,1)S(1)}, u32[]{:S(2)}, u32[]{:S(2)}) collective-permute-start(bf16[128,384]{1,0:T(8,128)(2,1)S(1)} %add_convert_fusion.refs_0_), channel_id=1, source_target_pairs={{0,16},{1,17},{2,18},{3,19},{16,0},{17,1},{18,2},{19,3},{4,20},{5,... | collective-permute-start | bytes 294920 | tf_op jit(solution)/shard_map/ppermute | solution.py:305
  68.9 5.7 %collective-permute-start.19 = (bf16[128,384]{1,0:T(8,128)(2,1)S(1)}, bf16[128,384]{1,0:T(8,128)(2,1)S(1)}, u32[]{:S(2)}, u32[]{:S(2)}) collective-permute-start(bf16[128,384]{1,0:T(8,128)(2,1)S(1)} %add_convert_fusion.refs_0_), channel_id=1, source_target_pairs={{0,2},{1,3},{2,0},{3,1},{16,18},{17,19},{18,16},{19,17},{4,6},{5,7... | collective-permute-start | bytes 294920 | tf_op jit(solution)/shard_map/ppermute | solution.py:305
  70.4 5.5 %collective-permute-start.20 = (bf16[128,384]{1,0:T(8,128)(2,1)S(1)}, bf16[128,384]{1,0:T(8,128)(2,1)S(1)}, u32[]{:S(2)}, u32[]{:S(2)}) collective-permute-start(bf16[128,384]{1,0:T(8,128)(2,1)S(1)} %add_convert_fusion.refs_0_), channel_id=1, source_target_pairs={{0,18},{1,19},{2,16},{3,17},{16,2},{17,3},{18,0},{19,1},{4,22},{5,... | collective-permute-start | bytes 294920 | tf_op jit(solution)/shard_map/ppermute | solution.py:305
  70.9 5.2 %collective-permute-start.17 = (bf16[128,384]{1,0:T(8,128)(2,1)S(1)}, bf16[128,384]{1,0:T(8,128)(2,1)S(1)}, u32[]{:S(2)}, u32[]{:S(2)}) collective-permute-start(bf16[128,384]{1,0:T(8,128)(2,1)S(1)} %add_convert_fusion.refs_0_), channel_id=1, source_target_pairs={{0,1},{1,0},{2,3},{3,2},{4,5},{5,4},{6,7},{7,6},{8,9},{9,8},{10,11... | collective-permute-start | bytes 294920 | tf_op jit(solution)/shard_map/ppermute | solution.py:297
  72.0 4.2 %collective-permute-start.18 = (bf16[128,384]{1,0:T(8,128)(2,1)S(1)}, bf16[128,384]{1,0:T(8,128)(2,1)S(1)}, u32[]{:S(2)}, u32[]{:S(2)}) collective-permute-start(bf16[128,384]{1,0:T(8,128)(2,1)S(1)} %collective-permute-done.16.refs_1_), channel_id=1, source_target_pairs={{0,1},{1,0},{2,3},{3,2},{4,5},{5,4},{6,7},{7,6},{8,9},{9,8},{10,11... | collective-permute-start | bytes 294920 | tf_op jit(solution)/shard_map/ppermute | solution.py:297
  74.6 1.6 %collective-permute-start.21 = (bf16[128,384]{1,0:T(8,128)(2,1)S(1)}, bf16[128,384]{1,0:T(8,128)(2,1)S(1)}, u32[]{:S(2)}, u32[]{:S(2)}) collective-permute-start(bf16[128,384]{1,0:T(8,128)(2,1)S(1)} %collective-permute-done.19.refs_4_), channel_id=1, source_target_pairs={{0,1},{1,0},{2,3},{3,2},{4,5},{5,4},{6,7},{7,6},{8,9},{9,8},{10,11... | collective-permute-start | bytes 294920 | tf_op jit(solution)/shard_map/ppermute | solution.py:297
  75.9 1.3 %collective-permute-start.22 = (bf16[128,384]{1,0:T(8,128)(2,1)S(1)}, bf16[128,384]{1,0:T(8,128)(2,1)S(1)}, u32[]{:S(2)}, u32[]{:S(2)}) collective-permute-start(bf16[128,384]{1,0:T(8,128)(2,1)S(1)} %collective-permute-done.20.refs_5_), channel_id=1, source_target_pairs={{0,1},{1,0},{2,3},{3,2},{4,5},{5,4},{6,7},{7,6},{8,9},{9,8},{10,11... | collective-permute-start | bytes 294920 | tf_op jit(solution)/shard_map/ppermute | solution.py:297

commit v8 on v7

--- a/solution.py
+++ b/solution.py
@@ -280,7 +280,6 @@
     win_ref = win_index.astype(jnp.int32)[None]
     track_cols = head_own.shape[1]
     bias_part = lax.dynamic_slice_in_dim(head_bias, segment_index * track_cols, track_cols, 0)
-    counts = gene_counts(exon_lists[:, 0], bin_count)
 
     tap_weights = jnp.transpose(convolution_kernel_weight, (1, 0, 2))
 
@@ -333,19 +332,20 @@
         next_in, part_in = turned_by(next_rows, 1, -1), turned_by(part_rows, 2, 2)
         arrived = [next_in, part_in]
         swaps = [swapped(next_in), swapped(part_in)]
-        conv_pre = conv_of(F32, own_rows)
         partials = [
             conv_of(BF16, next_in),
             conv_of(BF16, swaps[0]),
             conv_of(BF16, place, part_in, swaps[1]),
         ]
+        late_rows, _ = lax.optimization_barrier((own_rows, partials))
+        conv_pre = conv_of(F32, late_rows)
         returned = [
             turned_by(partials[0], -1, 1),
             turned_by(partials[1], 1, -1),
             turned_by(partials[2], 2, 2),
         ]
         qkv_pieces = first_stage(qkv_own, 1, (), arrived[0])
-        out_pieces = first_stage(out_own, 1, partials[0], partials[0])
+        out_pieces = first_stage(out_own, 1, arrived[0], partials[0])
         both = [jnp.concatenate(x, axis=0) for x in zip(qkv_pieces, out_pieces)]
         attention_pieces = [*qkv_pieces, *out_pieces, across(both, returned[1])]
         for x in returned:
@@ -366,6 +366,8 @@
     if stepwise:
         head_pieces.insert(2, across(head_pieces, ()))
     all_chan = lax.all_gather(conv_out, plane, axis=0)
+    lists, _ = lax.optimization_barrier((exon_lists[:, 0], conv_out))
+    counts = gene_counts(lists, bin_count)
 
     half = jax.ShapeDtypeStruct((segments * models // 2, bins, out_cols), BF16)
     keep, give = call_kernel(

time: 90.2 us -> 90.3 us (level)
    unnamed x16 -> x14, local copies, waits for them, and re-layouts: 3.25 us -> 3.24 us
  transfers between devices with their start and end apart: 26 -> 26, of which waited for: 9 -> 10; matrix products, arithmetic and copies ran while one was open for 1% -> 2% of each run, Pallas kernels for 9% -> 9%
where the time goes in v8:
time: 90.3 us; the launch traced here: 90 us
  starting transfers between devices  32.1 us (36%)
  waiting for transfers between devices  21.4 us (24%)
  blocking collectives  20.7 us (23%)
  Pallas kernels  9.83 us (11%)
  local copies, waits for them, and re-layouts  4.74 us (5%)
  other arithmetic  0.96 us (1%)
    ppermute x5, starting transfers between devices, turned_by(): return lax.ppermute(x, ('win', 'mp'), pairs)  13.1 us
    all_gather x1, blocking collectives, local(): all_chan = lax.all_gather(conv_out, plane, axis=0)  10.5 us
    all_to_all x1, blocking collectives, local(): lax.all_to_all(sums.reshape(owners, GENE_DEV, track_cols), ('segment', 'w...  10.1 us
    pallas_call x11, Pallas kernels, call_kernel(): pl.pallas_call(body, out_shape=out_shape, in_specs=[scalars if x.dtype ==...  9.83 us
    ppermute x6, waiting for transfers between devices, shifted(): return lax.ppermute(x, axis, [(i, (i + by) % size) for i in range(size)])  7.93 us
    ppermute x6, starting transfers between devices, shifted(): return lax.ppermute(x, axis, [(i, (i + by) % size) for i in range(size)])  7.65 us
    ppermute x5, waiting for transfers between devices, turned_by(): return lax.ppermute(x, ('win', 'mp'), pairs)  5.75 us
    ppermute x3, waiting for transfers between devices, over_plane(): return lax.ppermute(x, plane, pairs)  5.04 us
  transfers between devices with their start and end apart: 26, of which 10 were waited for; matrix products, arithmetic and copies ran while one was open for 2% of the time, Pallas kernels for 9%

profile of v8, /device:TPU:0, one launch (start us, length us, event | category | flops | bytes accessed | tf_op | source)
XLA Modules:
  0.0 90.0 jit_solution(4921128930067657000)
XLA Ops:
  0.1 1.2 %copy-done.1 = bf16[1,1536,256]{2,1,0:T(8,128)(2,1)S(1)} copy-done((bf16[1,1536,256]{2,1,0:T(8,128)(2,1)S(1)}, bf16[1,1536,256]{2,1,0:T(8,128)(2,1)}, u32[]{:S(2)}) %copy-start.1) | copy-done | bytes 786456
  1.3 0.9 shard_map.82
  2.2 3.1 %collective-permute-start = (bf16[144,384]{1,0:T(8,128)(2,1)S(1)}, bf16[144,384]{1,0:T(8,128)(2,1)S(1)}, u32[]{:S(2)}, u32[]{:S(2)}) collective-permute-start(bf16[144,384]{1,0:T(8,128)(2,1)S(1)} %get-tuple-element.27), channel_id=1, source_target_pairs={{0,4},{1,13},{2,6},{3,15},{4,8},{5,1},{6,10},{7,3},{8,12},{9,5},{1... | collective-permute-start | bytes 331784 | tf_op jit(solution)/shard_map/ppermute | solution.py:330
  5.3 2.6 %collective-permute-start.2 = (bf16[80,384]{1,0:T(8,128)(2,1)S(1)}, bf16[80,384]{1,0:T(8,128)(2,1)S(1)}, u32[]{:S(2)}, u32[]{:S(2)}) collective-permute-start(bf16[80,384]{1,0:T(8,128)(2,1)S(1)} %get-tuple-element.28), channel_id=1, source_target_pairs={{0,8},{1,9},{2,10},{3,11},{4,12},{5,13},{6,14},{7,15},{8,0},{9,1},... | collective-permute-start | bytes 184328 | tf_op jit(solution)/shard_map/ppermute | solution.py:330
  7.8 1.0 %copy-done.2 = bf16[384,640]{1,0:T(8,128)(2,1)S(1)} copy-done((bf16[384,640]{1,0:T(8,128)(2,1)S(1)}, bf16[384,640]{1,0:T(8,128)(2,1)}, u32[]{:S(2)}) %copy-start.2) | copy-done | bytes 491544
  8.9 0.7 shard_map.87.refs_0_
  9.6 0.1 collective-permute-start.7
  9.7 1.5 %collective-permute-done.x_ref = bf16[144,384]{1,0:T(8,128)(2,1)S(1)} collective-permute-done((bf16[144,384]{1,0:T(8,128)(2,1)S(1)}, bf16[144,384]{1,0:T(8,128)(2,1)S(1)}, u32[]{:S(2)}, u32[]{:S(2)}) %collective-permute-start) | collective-permute-done | bytes 110624 | tf_op jit(solution)/shard_map/ppermute | solution.py:330
  11.2 2.5 %collective-permute-start.8 = (bf16[320,384]{1,0:T(8,128)(2,1)S(1)}, bf16[320,384]{1,0:T(8,128)(2,1)S(1)}, u32[]{:S(2)}, u32[]{:S(2)}) collective-permute-start(bf16[320,384]{1,0:T(8,128)(2,1)S(1)} %shard_map.87.refs_0_), channel_id=1, source_target_pairs={{0,12},{4,0},{8,4},{12,8},{1,13},{5,1},{9,5},{13,9},{2,14},{6,2},{... | collective-permute-start | bytes 737288 | tf_op jit(solution)/shard_map/ppermute | solution.py:37
  13.8 1.0 %copy-done.3 = bf16[384,384]{1,0:T(8,128)(2,1)S(1)} copy-done((bf16[384,384]{1,0:T(8,128)(2,1)S(1)}, bf16[384,384]{1,0:T(8,128)(2,1)}, u32[]{:S(2)}) %copy-start.3) | copy-done | bytes 294936
  14.7 0.7 shard_map.88.refs_3_
  15.4 0.8 dynamic_slice.7
  16.3 0.5 shard_map.83
  16.7 3.0 %collective-permute-start.10 = (bf16[192,384]{1,0:T(8,128)(2,1)S(1)}, bf16[192,384]{1,0:T(8,128)(2,1)S(1)}, u32[]{:S(2)}, u32[]{:S(2)}) collective-permute-start(bf16[192,384]{1,0:T(8,128)(2,1)S(1)} %shard_map.88.refs_3_), channel_id=1, source_target_pairs={{0,12},{4,0},{8,4},{12,8},{1,13},{5,1},{9,5},{13,9},{2,14},{6,2},{... | collective-permute-start | bytes 442376 | tf_op jit(solution)/shard_map/ppermute | solution.py:37
  19.7 0.2 collective-permute-start.1
  19.9 1.0 %shard_map.85 = bf16[128,384]{1,0:T(8,128)(2,1)S(1)} custom-call(s32[3]{0:T(128)S(1)} %pad_add_fusion.place_ref, bf16[80,384]{1,0:T(8,128)(2,1)S(1)} %collective-permute-done.2.own_ref, bf16[80,384]{1,0:T(8,128)(2,1)S(1)} %collective-permute-done.3.other_ref, bf16[5,384,384]{2,1,0:T(8,128)(2,1)S(1)} %bitcast.25), custom_call_target="tpu_custom_call" | custom-call | flops 188743680 | bytes 1048576 | tf_op jit(solution)/shard_map/pallas_call | solution.py:24
  21.0 3.8 %collective-permute-start.4 = (bf16[128,384]{1,0:T(8,128)(2,1)S(1)}, bf16[128,384]{1,0:T(8,128)(2,1)S(1)}, u32[]{:S(2)}, u32[]{:S(2)}) collective-permute-start(bf16[128,384]{1,0:T(8,128)(2,1)S(1)} %shard_map.83), channel_id=1, source_target_pairs={{0,12},{1,5},{2,14},{3,7},{4,0},{5,9},{6,2},{7,11},{8,4},{9,13},{1... | collective-permute-start | bytes 294920 | tf_op jit(solution)/shard_map/ppermute | solution.py:330
  24.8 0.5 shard_map.84
  25.3 0.5 shard_map.86
  25.8 3.7 %collective-permute-start.6 = (bf16[128,384]{1,0:T(8,128)(2,1)S(1)}, bf16[128,384]{1,0:T(8,128)(2,1)S(1)}, u32[]{:S(2)}, u32[]{:S(2)}) collective-permute-start(bf16[128,384]{1,0:T(8,128)(2,1)S(1)} %shard_map.85), channel_id=1, source_target_pairs={{0,8},{1,9},{2,10},{3,11},{4,12},{5,13},{6,14},{7,15},{8,0},{9,1},... | collective-permute-start | bytes 294920 | tf_op jit(solution)/shard_map/ppermute | solution.py:330
  29.4 2.6 %collective-permute-done.9.refs_4_ = bf16[192,384]{1,0:T(8,128)(2,1)S(1)} collective-permute-done((bf16[192,384]{1,0:T(8,128)(2,1)S(1)}, bf16[192,384]{1,0:T(8,128)(2,1)S(1)}, u32[]{:S(2)}, u32[]{:S(2)}) %collective-permute-start.9) | collective-permute-done | bytes 147488 | tf_op jit(solution)/shard_map/ppermute | solution.py:37
  32.0 0.1 maximum_select_fusion
  32.2 4.2 %collective-permute-done.5 = bf16[128,384]{1,0:T(8,128)(2,1)S(1)} collective-permute-done((bf16[128,384]{1,0:T(8,128)(2,1)S(1)}, bf16[128,384]{1,0:T(8,128)(2,1)S(1)}, u32[]{:S(2)}, u32[]{:S(2)}) %collective-permute-start.5) | collective-permute-done | bytes 98336 | tf_op jit(solution)/shard_map/ppermute | solution.py:330
  36.4 3.7 %collective-permute-start.11 = (bf16[512,384]{1,0:T(8,128)(2,1)S(1)}, bf16[512,384]{1,0:T(8,128)(2,1)S(1)}, u32[]{:S(2)}, u32[]{:S(2)}) collective-permute-start(bf16[512,384]{1,0:T(8,128)(2,1)S(1)} %maximum_select_fusion), channel_id=1, source_target_pairs={{0,8},{4,0},{8,12},{12,4},{1,9},{5,1},{9,13},{13,5},{2,10},{6,2},{... | collective-permute-start | bytes 1179656 | tf_op jit(solution)/shard_map/ppermute | solution.py:278
  40.1 0.1 fusion.8
  40.3 0.5 collective-permute-start.24
  40.8 10.5 %all-gather = bf16[1024,384]{1,0:T(8,128)(2,1)S(1)} all-gather(bf16[128,384]{1,0:T(8,128)(2,1)S(1)} %fusion.8), channel_id=2, replica_groups=mesh['segment'=2,'win'=4,'mp'=4] {'segment','mp'}, dimensions={0}, use_global_device_ids=true | all-gather | bytes 884736 | tf_op jit(solution)/shard_map/all_gather | solution.py:368
  51.3 1.6 %collective-permute-start.23 = (bf16[384,512]{1,0:T(8,128)(2,1)S(1)}, bf16[384,512]{1,0:T(8,128)(2,1)S(1)}, u32[]{:S(2)}, u32[]{:S(2)}) collective-permute-start(bf16[384,512]{1,0:T(8,128)(2,1)S(1)} %constant_dynamic-slice_fusion.refs_8_), channel_id=1, source_target_pairs={{0,4},{4,8},{8,12},{12,0},{1,5},{5,9},{9,13},{13,1},{2,6},{6,10},{... | collective-permute-start | bytes 1179656 | tf_op jit(solution)/shard_map/ppermute | solution.py:37
  52.9 2.7 %shard_map.89 = (bf16[4,128,384]{2,1,0:T(8,128)(2,1)S(1)}, bf16[4,128,384]{2,1,0:T(8,128)(2,1)S(1)}) custom-call(s32[3]{0:T(128)S(1)} %pad_add_fusion.place_ref, s32[1]{0:T(128)} %bitcast.1.win_ref, bf16[8,128,384]{2,1,0:T(8,128)(2,1)S(1)} %bitcast.28, bf16[320,384]{1,0:T(8,128)(2,1)S(1)} %shard_map.87.refs_0_, ...), custom_call_target="tpu_custom_call" | custom-call | bytes 1048576 | tf_op jit(solution)/shard_map/pallas_call | solution.py:24
  55.8 1.6 %collective-permute-done.12.got_ref = bf16[4,128,384]{2,1,0:T(8,128)(2,1)S(1)} collective-permute-done((bf16[4,128,384]{2,1,0:T(8,128)(2,1)S(1)}, bf16[4,128,384]{2,1,0:T(8,128)(2,1)S(1)}, u32[]{:S(2)}, u32[]{:S(2)}) %collective-permute-start.12) | collective-permute-done | bytes 393248 | tf_op jit(solution)/shard_map/ppermute | solution.py:296
  57.4 0.6 shard_map.90
  58.0 1.6 %collective-permute-start.13 = (bf16[128,384]{1,0:T(8,128)(2,1)S(1)}, bf16[128,384]{1,0:T(8,128)(2,1)S(1)}, u32[]{:S(2)}, u32[]{:S(2)}) collective-permute-start(bf16[128,384]{1,0:T(8,128)(2,1)S(1)} %get-tuple-element.37), channel_id=1, source_target_pairs={{0,16},{1,17},{2,18},{3,19},{16,0},{17,1},{18,2},{19,3},{4,20},{5,... | collective-permute-start | bytes 294920 | tf_op jit(solution)/shard_map/ppermute | solution.py:396
  59.6 0.5 collective-permute-start.14
  60.1 1.5 %collective-permute-start.15 = (bf16[128,384]{1,0:T(8,128)(2,1)S(1)}, bf16[128,384]{1,0:T(8,128)(2,1)S(1)}, u32[]{:S(2)}, u32[]{:S(2)}) collective-permute-start(bf16[128,384]{1,0:T(8,128)(2,1)S(1)} %get-tuple-element.39), channel_id=1, source_target_pairs={{0,18},{1,19},{2,16},{3,17},{16,2},{17,3},{18,0},{19,1},{4,22},{5,... | collective-permute-start | bytes 294920 | tf_op jit(solution)/shard_map/ppermute | solution.py:396
  61.6 5.3 %collective-permute-done.23.refs_9_ = bf16[384,512]{1,0:T(8,128)(2,1)S(1)} collective-permute-done((bf16[384,512]{1,0:T(8,128)(2,1)S(1)}, bf16[384,512]{1,0:T(8,128)(2,1)S(1)}, u32[]{:S(2)}, u32[]{:S(2)}) %collective-permute-start.23) | collective-permute-done | bytes 393248 | tf_op jit(solution)/shard_map/ppermute | solution.py:37
  66.9 0.2 select_select_fusion
  67.3 1.7 %collective-permute-start.16 = (bf16[128,384]{1,0:T(8,128)(2,1)S(1)}, bf16[128,384]{1,0:T(8,128)(2,1)S(1)}, u32[]{:S(2)}, u32[]{:S(2)}) collective-permute-start(bf16[128,384]{1,0:T(8,128)(2,1)S(1)} %add_convert_fusion.refs_0_), channel_id=1, source_target_pairs={{0,16},{1,17},{2,18},{3,19},{16,0},{17,1},{18,2},{19,3},{4,20},{5,... | collective-permute-start | bytes 294920 | tf_op jit(solution)/shard_map/ppermute | solution.py:304
  68.9 1.5 %collective-permute-start.19 = (bf16[128,384]{1,0:T(8,128)(2,1)S(1)}, bf16[128,384]{1,0:T(8,128)(2,1)S(1)}, u32[]{:S(2)}, u32[]{:S(2)}) collective-permute-start(bf16[128,384]{1,0:T(8,128)(2,1)S(1)} %add_convert_fusion.refs_0_), channel_id=1, source_target_pairs={{0,2},{1,3},{2,0},{3,1},{16,18},{17,19},{18,16},{19,17},{4,6},{5,7... | collective-permute-start | bytes 294920 | tf_op jit(solution)/shard_map/ppermute | solution.py:304
  70.5 0.4 collective-permute-start.20
  70.9 1.1 %collective-permute-done.16.refs_1_ = bf16[128,384]{1,0:T(8,128)(2,1)S(1)} collective-permute-done((bf16[128,384]{1,0:T(8,128)(2,1)S(1)}, bf16[128,384]{1,0:T(8,128)(2,1)S(1)}, u32[]{:S(2)}, u32[]{:S(2)}) %collective-permute-start.16) | collective-permute-done | bytes 98336 | tf_op jit(solution)/shard_map/ppermute | solution.py:304
  72.0 2.6 %collective-permute-done.19.refs_4_ = bf16[128,384]{1,0:T(8,128)(2,1)S(1)} collective-permute-done((bf16[128,384]{1,0:T(8,128)(2,1)S(1)}, bf16[128,384]{1,0:T(8,128)(2,1)S(1)}, u32[]{:S(2)}, u32[]{:S(2)}) %collective-permute-start.19) | collective-permute-done | bytes 98336 | tf_op jit(solution)/shard_map/ppermute | solution.py:304
  74.6 1.4 %collective-permute-done.20.refs_5_ = bf16[128,384]{1,0:T(8,128)(2,1)S(1)} collective-permute-done((bf16[128,384]{1,0:T(8,128)(2,1)S(1)}, bf16[128,384]{1,0:T(8,128)(2,1)S(1)}, u32[]{:S(2)}, u32[]{:S(2)}) %collective-permute-start.20) | collective-permute-done | bytes 98336 | tf_op jit(solution)/shard_map/ppermute | solution.py:304
  76.0 0.2 convert_reduce_fusion
  76.3 1.0 %collective-permute-done.22.refs_7_ = bf16[128,384]{1,0:T(8,128)(2,1)S(1)} collective-permute-done((bf16[128,384]{1,0:T(8,128)(2,1)S(1)}, bf16[128,384]{1,0:T(8,128)(2,1)S(1)}, u32[]{:S(2)}, u32[]{:S(2)}) %collective-permute-start.22) | collective-permute-done | bytes 98336 | tf_op jit(solution)/shard_map/ppermute | solution.py:296
  77.3 1.2 %shard_map.91 = (f32[256,512]{1,0:T(8,128)S(1)}, bf16[256,384]{1,0:T(8,128)(2,1)S(1)}) custom-call(s32[3]{0:T(128)S(1)} %pad_add_fusion.place_ref, s32[1]{0:T(128)} %bitcast.1.win_ref, bf16[128,384]{1,0:T(8,128)(2,1)S(1)} %add_convert_fusion.refs_0_, bf16[128,384]{1,0:T(8,128)(2,1)S(1)} %collective-permute-done.16.refs_1_, ...), custom_call_target="tpu_custom_call" | custom-call | bytes 1048576 | tf_op jit(solution)/shard_map/pallas_call | solution.py:24
  78.5 0.7 shard_map.92
  79.2 10.1 %all_to_all.5 = bf16[8,8,512]{2,1,0:T(8,128)(2,1)S(1)} all-to-all(bf16[8,8,512]{2,1,0:T(8,128)(2,1)S(1)} %bitcast.30), channel_id=1, replica_groups=mesh['segment'=2,'win'=4,'mp'=4] {'segment','win'}, dimensions={0} | all-to-all | bytes 131072 | tf_op jit(solution)/shard_map/all_to_all | solution.py:433
  89.3 0.6 log1p.9
  (44 shorter events, 0.7 us)
Async XLA Ops:
  0.0 16.3 %copy-start = (bf16[384,5,384]{2,0,1:T(8,128)(2,1)S(1)}, bf16[384,5,384]{2,0,1:T(8,128)(2,1)}, u32[]{:S(2)}) copy-start(bf16[384,5,384]{2,0,1:T(8,128)(2,1)} %param.9) | copy-start | bytes 4423684
  0.1 1.2 %copy-start.1 = (bf16[1,1536,256]{2,1,0:T(8,128)(2,1)S(1)}, bf16[1,1536,256]{2,1,0:T(8,128)(2,1)}, u32[]{:S(2)}) copy-start(bf16[1,1536,256]{2,1,0:T(8,128)(2,1)} %param.8) | copy-start | bytes 2359300
  2.2 9.1 %collective-permute-start = (bf16[144,384]{1,0:T(8,128)(2,1)S(1)}, bf16[144,384]{1,0:T(8,128)(2,1)S(1)}, u32[]{:S(2)}, u32[]{:S(2)}) collective-permute-start(bf16[144,384]{1,0:T(8,128)(2,1)S(1)} %get-tuple-element.27), channel_id=1, source_target_pairs={{0,4},{1,13},{2,6},{3,15},{4,8},{5,1},{6,10},{7,3},{8,12},{9,5},{1... | collective-permute-start | bytes 331784 | tf_op jit(solution)/shard_map/ppermute | solution.py:330
  5.3 8.5 %collective-permute-start.2 = (bf16[80,384]{1,0:T(8,128)(2,1)S(1)}, bf16[80,384]{1,0:T(8,128)(2,1)S(1)}, u32[]{:S(2)}, u32[]{:S(2)}) collective-permute-start(bf16[80,384]{1,0:T(8,128)(2,1)S(1)} %get-tuple-element.28), channel_id=1, source_target_pairs={{0,8},{1,9},{2,10},{3,11},{4,12},{5,13},{6,14},{7,15},{8,0},{9,1},... | collective-permute-start | bytes 184328 | tf_op jit(solution)/shard_map/ppermute | solution.py:330
  7.8 1.0 %copy-start.2 = (bf16[384,640]{1,0:T(8,128)(2,1)S(1)}, bf16[384,640]{1,0:T(8,128)(2,1)}, u32[]{:S(2)}) copy-start(bf16[384,640]{1,0:T(8,128)(2,1)} %x_ref.2) | copy-start | bytes 1474564
  9.6 16.2 %collective-permute-start.7 = (bf16[320,384]{1,0:T(8,128)(2,1)S(1)}, bf16[320,384]{1,0:T(8,128)(2,1)S(1)}, u32[]{:S(2)}, u32[]{:S(2)}) collective-permute-start(bf16[320,384]{1,0:T(8,128)(2,1)S(1)} %shard_map.87.refs_0_), channel_id=1, source_target_pairs={{0,4},{4,8},{8,12},{12,0},{1,5},{5,9},{9,13},{13,1},{2,6},{6,10},{... | collective-permute-start | bytes 737288 | tf_op jit(solution)/shard_map/ppermute | solution.py:37
  11.2 20.8 %collective-permute-start.8 = (bf16[320,384]{1,0:T(8,128)(2,1)S(1)}, bf16[320,384]{1,0:T(8,128)(2,1)S(1)}, u32[]{:S(2)}, u32[]{:S(2)}) collective-permute-start(bf16[320,384]{1,0:T(8,128)(2,1)S(1)} %shard_map.87.refs_0_), channel_id=1, source_target_pairs={{0,12},{4,0},{8,4},{12,8},{1,13},{5,1},{9,5},{13,9},{2,14},{6,2},{... | collective-permute-start | bytes 737288 | tf_op jit(solution)/shard_map/ppermute | solution.py:37
  13.7 5.9 %collective-permute-start.3 = (bf16[80,384]{1,0:T(8,128)(2,1)S(1)}, bf16[80,384]{1,0:T(8,128)(2,1)S(1)}, u32[]{:S(2)}, u32[]{:S(2)}) collective-permute-start(bf16[80,384]{1,0:T(8,128)(2,1)S(1)} %collective-permute-done.2.own_ref), channel_id=1, source_target_pairs={{0,1},{1,0},{2,3},{3,2},{4,5},{5,4},{6,7},{7,6},{8,9},{9,8},{10,11... | collective-permute-start | bytes 184328 | tf_op jit(solution)/shard_map/ppermute | solution.py:296
  13.7 1.0 %copy-start.3 = (bf16[384,384]{1,0:T(8,128)(2,1)S(1)}, bf16[384,384]{1,0:T(8,128)(2,1)}, u32[]{:S(2)}) copy-start(bf16[384,384]{1,0:T(8,128)(2,1)} %x_ref.3) | copy-start | bytes 884740
  15.4 4.5 %copy-start.4 = (bf16[384,1024]{1,0:T(8,128)(2,1)S(1)}, bf16[384,1024]{1,0:T(8,128)(2,1)}, u32[]{:S(2)}) copy-start(bf16[384,1024]{1,0:T(8,128)(2,1)} %param.13) | copy-start | bytes 2359300
  16.7 12.7 %collective-permute-start.10 = (bf16[192,384]{1,0:T(8,128)(2,1)S(1)}, bf16[192,384]{1,0:T(8,128)(2,1)S(1)}, u32[]{:S(2)}, u32[]{:S(2)}) collective-permute-start(bf16[192,384]{1,0:T(8,128)(2,1)S(1)} %shard_map.88.refs_3_), channel_id=1, source_target_pairs={{0,12},{4,0},{8,4},{12,8},{1,13},{5,1},{9,5},{13,9},{2,14},{6,2},{... | collective-permute-start | bytes 442376 | tf_op jit(solution)/shard_map/ppermute | solution.py:37
  19.7 12.3 %collective-permute-start.9 = (bf16[192,384]{1,0:T(8,128)(2,1)S(1)}, bf16[192,384]{1,0:T(8,128)(2,1)S(1)}, u32[]{:S(2)}, u32[]{:S(2)}) collective-permute-start(bf16[192,384]{1,0:T(8,128)(2,1)S(1)} %shard_map.88.refs_3_), channel_id=1, source_target_pairs={{0,4},{4,8},{8,12},{12,0},{1,5},{5,9},{9,13},{13,1},{2,6},{6,10},{... | collective-permute-start | bytes 442376 | tf_op jit(solution)/shard_map/ppermute | solution.py:37
  19.7 1.3 %collective-permute-start.1 = (bf16[144,384]{1,0:T(8,128)(2,1)S(1)}, bf16[144,384]{1,0:T(8,128)(2,1)S(1)}, u32[]{:S(2)}, u32[]{:S(2)}) collective-permute-start(bf16[144,384]{1,0:T(8,128)(2,1)S(1)} %collective-permute-done.x_ref), channel_id=1, source_target_pairs={{0,1},{1,0},{2,3},{3,2},{4,5},{5,4},{6,7},{7,6},{8,9},{9,8},{10,11... | collective-permute-start | bytes 331784 | tf_op jit(solution)/shard_map/ppermute | solution.py:296
  21.0 19.1 %collective-permute-start.4 = (bf16[128,384]{1,0:T(8,128)(2,1)S(1)}, bf16[128,384]{1,0:T(8,128)(2,1)S(1)}, u32[]{:S(2)}, u32[]{:S(2)}) collective-permute-start(bf16[128,384]{1,0:T(8,128)(2,1)S(1)} %shard_map.83), channel_id=1, source_target_pairs={{0,12},{1,5},{2,14},{3,7},{4,0},{5,9},{6,2},{7,11},{8,4},{9,13},{1... | collective-permute-start | bytes 294920 | tf_op jit(solution)/shard_map/ppermute | solution.py:330
  25.3 14.8 %copy-start.6 = (f32[384]{0:T(512)S(1)}, f32[384]{0:T(512)}, u32[]{:S(2)}) copy-start(f32[384]{0:T(512)} %param.10) | copy-start | bytes 4612
  25.8 14.3 %collective-permute-start.6 = (bf16[128,384]{1,0:T(8,128)(2,1)S(1)}, bf16[128,384]{1,0:T(8,128)(2,1)S(1)}, u32[]{:S(2)}, u32[]{:S(2)}) collective-permute-start(bf16[128,384]{1,0:T(8,128)(2,1)S(1)} %shard_map.85), channel_id=1, source_target_pairs={{0,8},{1,9},{2,10},{3,11},{4,12},{5,13},{6,14},{7,15},{8,0},{9,1},... | collective-permute-start | bytes 294920 | tf_op jit(solution)/shard_map/ppermute | solution.py:330
  29.4 6.9 %collective-permute-start.5 = (bf16[128,384]{1,0:T(8,128)(2,1)S(1)}, bf16[128,384]{1,0:T(8,128)(2,1)S(1)}, u32[]{:S(2)}, u32[]{:S(2)}) collective-permute-start(bf16[128,384]{1,0:T(8,128)(2,1)S(1)} %shard_map.84), channel_id=1, source_target_pairs={{0,4},{1,13},{2,6},{3,15},{4,8},{5,1},{6,10},{7,3},{8,12},{9,5},{1... | collective-permute-start | bytes 294920 | tf_op jit(solution)/shard_map/ppermute | solution.py:330
  36.4 16.5 %collective-permute-start.11 = (bf16[512,384]{1,0:T(8,128)(2,1)S(1)}, bf16[512,384]{1,0:T(8,128)(2,1)S(1)}, u32[]{:S(2)}, u32[]{:S(2)}) collective-permute-start(bf16[512,384]{1,0:T(8,128)(2,1)S(1)} %maximum_select_fusion), channel_id=1, source_target_pairs={{0,8},{4,0},{8,12},{12,4},{1,9},{5,1},{9,13},{13,5},{2,10},{6,2},{... | collective-permute-start | bytes 1179656 | tf_op jit(solution)/shard_map/ppermute | solution.py:278
  40.3 21.3 %collective-permute-start.24 = (bf16[384,512]{1,0:T(8,128)(2,1)S(1)}, bf16[384,512]{1,0:T(8,128)(2,1)S(1)}, u32[]{:S(2)}, u32[]{:S(2)}) collective-permute-start(bf16[384,512]{1,0:T(8,128)(2,1)S(1)} %constant_dynamic-slice_fusion.refs_8_), channel_id=1, source_target_pairs={{0,12},{4,0},{8,4},{12,8},{1,13},{5,1},{9,5},{13,9},{2,14},{6,2},{... | collective-permute-start | bytes 1179656 | tf_op jit(solution)/shard_map/ppermute | solution.py:37
  40.8 15.0 %copy-start.5 = (s32[3,1,8,8]{3,2,1,0:T(8,128)S(1)}, s32[3,1,8,8]{3,2,1,0:T(8,128)}, u32[]{:S(2)}) copy-start(s32[3,1,8,8]{3,2,1,0:T(8,128)} %param.15) | copy-start | bytes 2308
  51.3 15.6 %collective-permute-start.23 = (bf16[384,512]{1,0:T(8,128)(2,1)S(1)}, bf16[384,512]{1,0:T(8,128)(2,1)S(1)}, u32[]{:S(2)}, u32[]{:S(2)}) collective-permute-start(bf16[384,512]{1,0:T(8,128)(2,1)S(1)} %constant_dynamic-slice_fusion.refs_8_), channel_id=1, source_target_pairs={{0,4},{4,8},{8,12},{12,0},{1,5},{5,9},{9,13},{13,1},{2,6},{6,10},{... | collective-permute-start | bytes 1179656 | tf_op jit(solution)/shard_map/ppermute | solution.py:37
  55.6 1.8 %collective-permute-start.12 = (bf16[4,128,384]{2,1,0:T(8,128)(2,1)S(1)}, bf16[4,128,384]{2,1,0:T(8,128)(2,1)S(1)}, u32[]{:S(2)}, u32[]{:S(2)}) collective-permute-start(bf16[4,128,384]{2,1,0:T(8,128)(2,1)S(1)} %get-tuple-element.35), channel_id=1, source_target_pairs={{0,1},{1,0},{2,3},{3,2},{4,5},{5,4},{6,7},{7,6},{8,9},{9,8},{10,11... | collective-permute-start | bytes 1179656 | tf_op jit(solution)/shard_map/ppermute | solution.py:296
  58.0 9.2 %collective-permute-start.13 = (bf16[128,384]{1,0:T(8,128)(2,1)S(1)}, bf16[128,384]{1,0:T(8,128)(2,1)S(1)}, u32[]{:S(2)}, u32[]{:S(2)}) collective-permute-start(bf16[128,384]{1,0:T(8,128)(2,1)S(1)} %get-tuple-element.37), channel_id=1, source_target_pairs={{0,16},{1,17},{2,18},{3,19},{16,0},{17,1},{18,2},{19,3},{4,20},{5,... | collective-permute-start | bytes 294920 | tf_op jit(solution)/shard_map/ppermute | solution.py:396
  59.6 7.6 %collective-permute-start.14 = (bf16[128,384]{1,0:T(8,128)(2,1)S(1)}, bf16[128,384]{1,0:T(8,128)(2,1)S(1)}, u32[]{:S(2)}, u32[]{:S(2)}) collective-permute-start(bf16[128,384]{1,0:T(8,128)(2,1)S(1)} %get-tuple-element.38), channel_id=1, source_target_pairs={{0,2},{1,3},{2,0},{3,1},{16,18},{17,19},{18,16},{19,17},{4,6},{5,7... | collective-permute-start | bytes 294920 | tf_op jit(solution)/shard_map/ppermute | solution.py:396
  60.1 7.1 %collective-permute-start.15 = (bf16[128,384]{1,0:T(8,128)(2,1)S(1)}, bf16[128,384]{1,0:T(8,128)(2,1)S(1)}, u32[]{:S(2)}, u32[]{:S(2)}) collective-permute-start(bf16[128,384]{1,0:T(8,128)(2,1)S(1)} %get-tuple-element.39), channel_id=1, source_target_pairs={{0,18},{1,19},{2,16},{3,17},{16,2},{17,3},{18,0},{19,1},{4,22},{5,... | collective-permute-start | bytes 294920 | tf_op jit(solution)/shard_map/ppermute | solution.py:396
  67.1 11.3 %collective-permute-start.25 = (bf16[384,512]{1,0:T(8,128)(2,1)S(1)}, bf16[384,512]{1,0:T(8,128)(2,1)S(1)}, u32[]{:S(2)}, u32[]{:S(2)}) collective-permute-start(bf16[384,512]{1,0:T(8,128)(2,1)S(1)} %select_select_fusion), channel_id=1, source_target_pairs={{0,8},{4,0},{8,12},{12,4},{1,9},{5,1},{9,13},{13,5},{2,10},{6,2},{... | collective-permute-start | bytes 1179656 | tf_op jit(solution)/shard_map/ppermute | solution.py:278
  67.3 4.7 %collective-permute-start.16 = (bf16[128,384]{1,0:T(8,128)(2,1)S(1)}, bf16[128,384]{1,0:T(8,128)(2,1)S(1)}, u32[]{:S(2)}, u32[]{:S(2)}) collective-permute-start(bf16[128,384]{1,0:T(8,128)(2,1)S(1)} %add_convert_fusion.refs_0_), channel_id=1, source_target_pairs={{0,16},{1,17},{2,18},{3,19},{16,0},{17,1},{18,2},{19,3},{4,20},{5,... | collective-permute-start | bytes 294920 | tf_op jit(solution)/shard_map/ppermute | solution.py:304
  68.9 5.7 %collective-permute-start.19 = (bf16[128,384]{1,0:T(8,128)(2,1)S(1)}, bf16[128,384]{1,0:T(8,128)(2,1)S(1)}, u32[]{:S(2)}, u32[]{:S(2)}) collective-permute-start(bf16[128,384]{1,0:T(8,128)(2,1)S(1)} %add_convert_fusion.refs_0_), channel_id=1, source_target_pairs={{0,2},{1,3},{2,0},{3,1},{16,18},{17,19},{18,16},{19,17},{4,6},{5,7... | collective-permute-start | bytes 294920 | tf_op jit(solution)/shard_map/ppermute | solution.py:304
  70.5 5.5 %collective-permute-start.20 = (bf16[128,384]{1,0:T(8,128)(2,1)S(1)}, bf16[128,384]{1,0:T(8,128)(2,1)S(1)}, u32[]{:S(2)}, u32[]{:S(2)}) collective-permute-start(bf16[128,384]{1,0:T(8,128)(2,1)S(1)} %add_convert_fusion.refs_0_), channel_id=1, source_target_pairs={{0,18},{1,19},{2,16},{3,17},{16,2},{17,3},{18,0},{19,1},{4,22},{5,... | collective-permute-start | bytes 294920 | tf_op jit(solution)/shard_map/ppermute | solution.py:304
  70.9 5.4 %collective-permute-start.17 = (bf16[128,384]{1,0:T(8,128)(2,1)S(1)}, bf16[128,384]{1,0:T(8,128)(2,1)S(1)}, u32[]{:S(2)}, u32[]{:S(2)}) collective-permute-start(bf16[128,384]{1,0:T(8,128)(2,1)S(1)} %add_convert_fusion.refs_0_), channel_id=1, source_target_pairs={{0,1},{1,0},{2,3},{3,2},{4,5},{5,4},{6,7},{7,6},{8,9},{9,8},{10,11... | collective-permute-start | bytes 294920 | tf_op jit(solution)/shard_map/ppermute | solution.py:296
  72.0 4.2 %collective-permute-start.18 = (bf16[128,384]{1,0:T(8,128)(2,1)S(1)}, bf16[128,384]{1,0:T(8,128)(2,1)S(1)}, u32[]{:S(2)}, u32[]{:S(2)}) collective-permute-start(bf16[128,384]{1,0:T(8,128)(2,1)S(1)} %collective-permute-done.16.refs_1_), channel_id=1, source_target_pairs={{0,1},{1,0},{2,3},{3,2},{4,5},{5,4},{6,7},{7,6},{8,9},{9,8},{10,11... | collective-permute-start | bytes 294920 | tf_op jit(solution)/shard_map/ppermute | solution.py:296
  74.6 1.6 %collective-permute-start.21 = (bf16[128,384]{1,0:T(8,128)(2,1)S(1)}, bf16[128,384]{1,0:T(8,128)(2,1)S(1)}, u32[]{:S(2)}, u32[]{:S(2)}) collective-permute-start(bf16[128,384]{1,0:T(8,128)(2,1)S(1)} %collective-permute-done.19.refs_4_), channel_id=1, source_target_pairs={{0,1},{1,0},{2,3},{3,2},{4,5},{5,4},{6,7},{7,6},{8,9},{9,8},{10,11... | collective-permute-start | bytes 294920 | tf_op jit(solution)/shard_map/ppermute | solution.py:296
  76.0 1.3 %collective-permute-start.22 = (bf16[128,384]{1,0:T(8,128)(2,1)S(1)}, bf16[128,384]{1,0:T(8,128)(2,1)S(1)}, u32[]{:S(2)}, u32[]{:S(2)}) collective-permute-start(bf16[128,384]{1,0:T(8,128)(2,1)S(1)} %collective-permute-done.20.refs_5_), channel_id=1, source_target_pairs={{0,1},{1,0},{2,3},{3,2},{4,5},{5,4},{6,7},{7,6},{8,9},{9,8},{10,11... | collective-permute-start | bytes 294920 | tf_op jit(solution)/shard_map/ppermute | solution.py:296

commit v9 on v8

--- a/solution.py
+++ b/solution.py
@@ -345,9 +345,9 @@
             turned_by(partials[2], 2, 2),
         ]
         qkv_pieces = first_stage(qkv_own, 1, (), arrived[0])
-        out_pieces = first_stage(out_own, 1, arrived[0], partials[0])
+        out_pieces = first_stage(out_own, 1, arrived[0], ())
         both = [jnp.concatenate(x, axis=0) for x in zip(qkv_pieces, out_pieces)]
-        attention_pieces = [*qkv_pieces, *out_pieces, across(both, returned[1])]
+        attention_pieces = [*qkv_pieces, *out_pieces, across(both, returned[:2])]
         for x in returned:
             conv_pre = conv_pre + x.astype(F32)
     else:

time: 90.3 us -> 95.9 us (1.062)
  waiting for transfers between devices: 21.4 us -> 28 us
  starting transfers between devices: 32.1 us -> 28.9 us
  blocking collectives: 20.7 us -> 22 us
    ppermute x5, waiting for transfers between devices: 5.75 us -> 10.5 us  [turned_by(): return lax.ppermute(x, ('win', 'mp'), pairs)]
    ppermute x6, waiting for transfers between devices: 7.93 us -> 9.96 us  [shifted(): return lax.ppermute(x, axis, [(i, (i + by) % size) for i in range(size)])]
    ppermute x5, starting transfers between devices: 13.1 us -> 11.3 us  [turned_by(): return lax.ppermute(x, ('win', 'mp'), pairs)]
    all_gather x1, blocking collectives: 10.5 us -> 12.2 us  [local(): all_chan = lax.all_gather(conv_out, plane, axis=0)]
    ppermute x6, starting transfers between devices: 7.65 us -> 6.62 us  [shifted(): return lax.ppermute(x, axis, [(i, (i + by) % size) for i in range(size)])]
    dynamic_slice x1, local copies, waits for them, and re-layouts: 0.03 us -> 1.02 us  [local(): lax.dynamic_slice_in_dim(head_weight, segment_index * head_cols, head_col...]
  transfers between devices with their start and end apart: 26 -> 26, of which waited for: 10 -> 10; matrix products, arithmetic and copies ran while one was open for 2% -> 3% of each run, Pallas kernels for 9% -> 9%
where the time goes in v9:
time: 95.9 us; the launch traced here: 95.5 us
  starting transfers between devices  28.9 us (30%)
  waiting for transfers between devices  28 us (29%)
  blocking collectives  22 us (23%)
  Pallas kernels  9.81 us (10%)
  local copies, waits for them, and re-layouts  5.65 us (6%)
    all_gather x1, blocking collectives, local(): all_chan = lax.all_gather(conv_out, plane, axis=0)  12.2 us
    ppermute x5, starting transfers between devices, turned_by(): return lax.ppermute(x, ('win', 'mp'), pairs)  11.3 us
    ppermute x5, waiting for transfers between devices, turned_by(): return lax.ppermute(x, ('win', 'mp'), pairs)  10.5 us
    ppermute x6, waiting for transfers between devices, shifted(): return lax.ppermute(x, axis, [(i, (i + by) % size) for i in range(size)])  9.96 us
    all_to_all x1, blocking collectives, local(): lax.all_to_all(sums.reshape(owners, GENE_DEV, track_cols), ('segment', 'w...  9.82 us
    pallas_call x11, Pallas kernels, call_kernel(): pl.pallas_call(body, out_shape=out_shape, in_specs=[scalars if x.dtype ==...  9.81 us
    ppermute x6, starting transfers between devices, shifted(): return lax.ppermute(x, axis, [(i, (i + by) % size) for i in range(size)])  6.62 us
    ppermute x3, waiting for transfers between devices, over_plane(): return lax.ppermute(x, plane, pairs)  5.03 us
  transfers between devices with their start and end apart: 26, of which 10 were waited for; matrix products, arithmetic and copies ran while one was open for 3% of the time, Pallas kernels for 9%

profile of v9, /device:TPU:0, one launch (start us, length us, event | category | flops | bytes accessed | tf_op | source)
XLA Modules:
  0.0 95.5 jit_solution(10591816711241770944)
XLA Ops:
  0.1 1.2 %copy-done.1 = bf16[1,1536,256]{2,1,0:T(8,128)(2,1)S(1)} copy-done((bf16[1,1536,256]{2,1,0:T(8,128)(2,1)S(1)}, bf16[1,1536,256]{2,1,0:T(8,128)(2,1)}, u32[]{:S(2)}) %copy-start.1) | copy-done | bytes 786456
  1.3 0.9 shard_map.82
  2.2 3.1 %collective-permute-start = (bf16[144,384]{1,0:T(8,128)(2,1)S(1)}, bf16[144,384]{1,0:T(8,128)(2,1)S(1)}, u32[]{:S(2)}, u32[]{:S(2)}) collective-permute-start(bf16[144,384]{1,0:T(8,128)(2,1)S(1)} %get-tuple-element.26), channel_id=1, source_target_pairs={{0,4},{1,13},{2,6},{3,15},{4,8},{5,1},{6,10},{7,3},{8,12},{9,5},{1... | collective-permute-start | bytes 331784 | tf_op jit(solution)/shard_map/ppermute | solution.py:330
  5.3 2.6 %collective-permute-start.2 = (bf16[80,384]{1,0:T(8,128)(2,1)S(1)}, bf16[80,384]{1,0:T(8,128)(2,1)S(1)}, u32[]{:S(2)}, u32[]{:S(2)}) collective-permute-start(bf16[80,384]{1,0:T(8,128)(2,1)S(1)} %get-tuple-element.27), channel_id=1, source_target_pairs={{0,8},{1,9},{2,10},{3,11},{4,12},{5,13},{6,14},{7,15},{8,0},{9,1},... | collective-permute-start | bytes 184328 | tf_op jit(solution)/shard_map/ppermute | solution.py:330
  7.8 5.1 %collective-permute-done.2.own_ref = bf16[80,384]{1,0:T(8,128)(2,1)S(1)} collective-permute-done((bf16[80,384]{1,0:T(8,128)(2,1)S(1)}, bf16[80,384]{1,0:T(8,128)(2,1)S(1)}, u32[]{:S(2)}, u32[]{:S(2)}) %collective-permute-start.2) | collective-permute-done | bytes 61472 | tf_op jit(solution)/shard_map/ppermute | solution.py:330
  13.0 1.0 %copy-done.2 = bf16[384,640]{1,0:T(8,128)(2,1)S(1)} copy-done((bf16[384,640]{1,0:T(8,128)(2,1)S(1)}, bf16[384,640]{1,0:T(8,128)(2,1)}, u32[]{:S(2)}) %copy-start.2) | copy-done | bytes 491544
  14.0 0.7 shard_map.87.refs_0_
  14.8 3.8 %collective-permute-start.8 = (bf16[320,384]{1,0:T(8,128)(2,1)S(1)}, bf16[320,384]{1,0:T(8,128)(2,1)S(1)}, u32[]{:S(2)}, u32[]{:S(2)}) collective-permute-start(bf16[320,384]{1,0:T(8,128)(2,1)S(1)} %shard_map.87.refs_0_), channel_id=1, source_target_pairs={{0,12},{4,0},{8,4},{12,8},{1,13},{5,1},{9,5},{13,9},{2,14},{6,2},{... | collective-permute-start | bytes 737288 | tf_op jit(solution)/shard_map/ppermute | solution.py:37
  18.7 1.0 %copy-done.3 = bf16[384,384]{1,0:T(8,128)(2,1)S(1)} copy-done((bf16[384,384]{1,0:T(8,128)(2,1)S(1)}, bf16[384,384]{1,0:T(8,128)(2,1)}, u32[]{:S(2)}) %copy-start.3) | copy-done | bytes 294936
  19.6 0.7 shard_map.88.refs_3_
  20.3 0.9 collective-permute-start.10
  21.3 0.8 dynamic_slice.7
  22.0 1.1 %collective-permute-start.9 = (bf16[192,384]{1,0:T(8,128)(2,1)S(1)}, bf16[192,384]{1,0:T(8,128)(2,1)S(1)}, u32[]{:S(2)}, u32[]{:S(2)}) collective-permute-start(bf16[192,384]{1,0:T(8,128)(2,1)S(1)} %shard_map.88.refs_3_), channel_id=1, source_target_pairs={{0,4},{4,8},{8,12},{12,0},{1,5},{5,9},{9,13},{13,1},{2,6},{6,10},{... | collective-permute-start | bytes 442376 | tf_op jit(solution)/shard_map/ppermute | solution.py:37
  23.2 1.0 %constant_dynamic-slice_fusion.refs_8_ = bf16[384,512]{1,0:T(8,128)(2,1)S(1)} fusion(bf16[384,1024]{1,0:T(8,128)(2,1)} %param.13, s32[]{:T(128)S(6)} %select_n.36), kind=kLoop, calls=%fused_computation.25 | loop fusion | bytes 786436 | tf_op jit(solution)/shard_map/dynamic_slice | solution.py:263
  24.2 0.5 shard_map.83
  24.7 1.0 %shard_map.85 = bf16[128,384]{1,0:T(8,128)(2,1)S(1)} custom-call(s32[3]{0:T(128)S(1)} %pad_add_fusion.place_ref, bf16[80,384]{1,0:T(8,128)(2,1)S(1)} %collective-permute-done.2.own_ref, bf16[80,384]{1,0:T(8,128)(2,1)S(1)} %collective-permute-done.3.other_ref, bf16[5,384,384]{2,1,0:T(8,128)(2,1)S(1)} %bitcast.25), custom_call_target="tpu_custom_call" | custom-call | flops 188743680 | bytes 1048576 | tf_op jit(solution)/shard_map/pallas_call | solution.py:24
  25.7 2.7 %collective-permute-start.4 = (bf16[128,384]{1,0:T(8,128)(2,1)S(1)}, bf16[128,384]{1,0:T(8,128)(2,1)S(1)}, u32[]{:S(2)}, u32[]{:S(2)}) collective-permute-start(bf16[128,384]{1,0:T(8,128)(2,1)S(1)} %shard_map.83), channel_id=1, source_target_pairs={{0,12},{1,5},{2,14},{3,7},{4,0},{5,9},{6,2},{7,11},{8,4},{9,13},{1... | collective-permute-start | bytes 294920 | tf_op jit(solution)/shard_map/ppermute | solution.py:330
  28.4 0.5 shard_map.84
  28.9 0.5 shard_map.86
  29.4 2.2 %collective-permute-done.10.refs_5_ = bf16[192,384]{1,0:T(8,128)(2,1)S(1)} collective-permute-done((bf16[192,384]{1,0:T(8,128)(2,1)S(1)}, bf16[192,384]{1,0:T(8,128)(2,1)S(1)}, u32[]{:S(2)}, u32[]{:S(2)}) %collective-permute-start.10) | collective-permute-done | bytes 147488 | tf_op jit(solution)/shard_map/ppermute | solution.py:37
  31.6 2.9 %collective-permute-start.6 = (bf16[128,384]{1,0:T(8,128)(2,1)S(1)}, bf16[128,384]{1,0:T(8,128)(2,1)S(1)}, u32[]{:S(2)}, u32[]{:S(2)}) collective-permute-start(bf16[128,384]{1,0:T(8,128)(2,1)S(1)} %shard_map.85), channel_id=1, source_target_pairs={{0,8},{1,9},{2,10},{3,11},{4,12},{5,13},{6,14},{7,15},{8,0},{9,1},... | collective-permute-start | bytes 294920 | tf_op jit(solution)/shard_map/ppermute | solution.py:330
  34.5 2.8 %collective-permute-done.9.refs_4_ = bf16[192,384]{1,0:T(8,128)(2,1)S(1)} collective-permute-done((bf16[192,384]{1,0:T(8,128)(2,1)S(1)}, bf16[192,384]{1,0:T(8,128)(2,1)S(1)}, u32[]{:S(2)}, u32[]{:S(2)}) %collective-permute-start.9) | collective-permute-done | bytes 147488 | tf_op jit(solution)/shard_map/ppermute | solution.py:37
  37.4 5.5 %collective-permute-done.5 = bf16[128,384]{1,0:T(8,128)(2,1)S(1)} collective-permute-done((bf16[128,384]{1,0:T(8,128)(2,1)S(1)}, bf16[128,384]{1,0:T(8,128)(2,1)S(1)}, u32[]{:S(2)}, u32[]{:S(2)}) %collective-permute-start.5) | collective-permute-done | bytes 98336 | tf_op jit(solution)/shard_map/ppermute | solution.py:330
  42.9 1.4 %collective-permute-start.11 = (bf16[512,384]{1,0:T(8,128)(2,1)S(1)}, bf16[512,384]{1,0:T(8,128)(2,1)S(1)}, u32[]{:S(2)}, u32[]{:S(2)}) collective-permute-start(bf16[512,384]{1,0:T(8,128)(2,1)S(1)} %maximum_select_fusion), channel_id=1, source_target_pairs={{0,8},{4,0},{8,12},{12,4},{1,9},{5,1},{9,13},{13,5},{2,10},{6,2},{... | collective-permute-start | bytes 1179656 | tf_op jit(solution)/shard_map/ppermute | solution.py:278
  44.4 0.5 collective-permute-start.24
  44.9 12.2 %all-gather = bf16[1024,384]{1,0:T(8,128)(2,1)S(1)} all-gather(bf16[128,384]{1,0:T(8,128)(2,1)S(1)} %fusion.8), channel_id=2, replica_groups=mesh['segment'=2,'win'=4,'mp'=4] {'segment','mp'}, dimensions={0}, use_global_device_ids=true | all-gather | bytes 884736 | tf_op jit(solution)/shard_map/all_gather | solution.py:368
  57.3 2.7 %shard_map.89 = (bf16[4,128,384]{2,1,0:T(8,128)(2,1)S(1)}, bf16[4,128,384]{2,1,0:T(8,128)(2,1)S(1)}) custom-call(s32[3]{0:T(128)S(1)} %pad_add_fusion.place_ref, s32[1]{0:T(128)} %bitcast.1.win_ref, bf16[8,128,384]{2,1,0:T(8,128)(2,1)S(1)} %bitcast.28, bf16[320,384]{1,0:T(8,128)(2,1)S(1)} %shard_map.87.refs_0_, ...), custom_call_target="tpu_custom_call" | custom-call | bytes 1048576 | tf_op jit(solution)/shard_map/pallas_call | solution.py:24
  60.0 0.3 collective-permute-start.12
  60.3 1.4 %collective-permute-done.12.got_ref = bf16[4,128,384]{2,1,0:T(8,128)(2,1)S(1)} collective-permute-done((bf16[4,128,384]{2,1,0:T(8,128)(2,1)S(1)}, bf16[4,128,384]{2,1,0:T(8,128)(2,1)S(1)}, u32[]{:S(2)}, u32[]{:S(2)}) %collective-permute-start.12) | collective-permute-done | bytes 393248 | tf_op jit(solution)/shard_map/ppermute | solution.py:296
  61.7 0.6 shard_map.90
  62.4 1.6 %collective-permute-start.13 = (bf16[128,384]{1,0:T(8,128)(2,1)S(1)}, bf16[128,384]{1,0:T(8,128)(2,1)S(1)}, u32[]{:S(2)}, u32[]{:S(2)}) collective-permute-start(bf16[128,384]{1,0:T(8,128)(2,1)S(1)} %get-tuple-element.35), channel_id=1, source_target_pairs={{0,16},{1,17},{2,18},{3,19},{16,0},{17,1},{18,2},{19,3},{4,20},{5,... | collective-permute-start | bytes 294920 | tf_op jit(solution)/shard_map/ppermute | solution.py:396
  64.0 0.5 collective-permute-start.14
  64.5 1.5 %collective-permute-start.15 = (bf16[128,384]{1,0:T(8,128)(2,1)S(1)}, bf16[128,384]{1,0:T(8,128)(2,1)S(1)}, u32[]{:S(2)}, u32[]{:S(2)}) collective-permute-start(bf16[128,384]{1,0:T(8,128)(2,1)S(1)} %get-tuple-element.37), channel_id=1, source_target_pairs={{0,18},{1,19},{2,16},{3,17},{16,2},{17,3},{18,0},{19,1},{4,22},{5,... | collective-permute-start | bytes 294920 | tf_op jit(solution)/shard_map/ppermute | solution.py:396
  66.0 5.0 %collective-permute-done.23.refs_9_ = bf16[384,512]{1,0:T(8,128)(2,1)S(1)} collective-permute-done((bf16[384,512]{1,0:T(8,128)(2,1)S(1)}, bf16[384,512]{1,0:T(8,128)(2,1)S(1)}, u32[]{:S(2)}, u32[]{:S(2)}) %collective-permute-start.23) | collective-permute-done | bytes 393248 | tf_op jit(solution)/shard_map/ppermute | solution.py:37
  70.9 0.2 select_select_fusion
  71.1 2.0 %collective-permute-start.25 = (bf16[384,512]{1,0:T(8,128)(2,1)S(1)}, bf16[384,512]{1,0:T(8,128)(2,1)S(1)}, u32[]{:S(2)}, u32[]{:S(2)}) collective-permute-start(bf16[384,512]{1,0:T(8,128)(2,1)S(1)} %select_select_fusion), channel_id=1, source_target_pairs={{0,8},{4,0},{8,12},{12,4},{1,9},{5,1},{9,13},{13,5},{2,10},{6,2},{... | collective-permute-start | bytes 1179656 | tf_op jit(solution)/shard_map/ppermute | solution.py:278
  73.2 1.6 %collective-permute-start.16 = (bf16[128,384]{1,0:T(8,128)(2,1)S(1)}, bf16[128,384]{1,0:T(8,128)(2,1)S(1)}, u32[]{:S(2)}, u32[]{:S(2)}) collective-permute-start(bf16[128,384]{1,0:T(8,128)(2,1)S(1)} %add_convert_fusion.refs_0_), channel_id=1, source_target_pairs={{0,16},{1,17},{2,18},{3,19},{16,0},{17,1},{18,2},{19,3},{4,20},{5,... | collective-permute-start | bytes 294920 | tf_op jit(solution)/shard_map/ppermute | solution.py:304
  74.8 1.5 %collective-permute-start.19 = (bf16[128,384]{1,0:T(8,128)(2,1)S(1)}, bf16[128,384]{1,0:T(8,128)(2,1)S(1)}, u32[]{:S(2)}, u32[]{:S(2)}) collective-permute-start(bf16[128,384]{1,0:T(8,128)(2,1)S(1)} %add_convert_fusion.refs_0_), channel_id=1, source_target_pairs={{0,2},{1,3},{2,0},{3,1},{16,18},{17,19},{18,16},{19,17},{4,6},{5,7... | collective-permute-start | bytes 294920 | tf_op jit(solution)/shard_map/ppermute | solution.py:304
  76.4 0.4 collective-permute-start.20
  76.8 1.0 %collective-permute-done.16.refs_1_ = bf16[128,384]{1,0:T(8,128)(2,1)S(1)} collective-permute-done((bf16[128,384]{1,0:T(8,128)(2,1)S(1)}, bf16[128,384]{1,0:T(8,128)(2,1)S(1)}, u32[]{:S(2)}, u32[]{:S(2)}) %collective-permute-start.16) | collective-permute-done | bytes 98336 | tf_op jit(solution)/shard_map/ppermute | solution.py:304
  77.9 2.6 %collective-permute-done.19.refs_4_ = bf16[128,384]{1,0:T(8,128)(2,1)S(1)} collective-permute-done((bf16[128,384]{1,0:T(8,128)(2,1)S(1)}, bf16[128,384]{1,0:T(8,128)(2,1)S(1)}, u32[]{:S(2)}, u32[]{:S(2)}) %collective-permute-start.19) | collective-permute-done | bytes 98336 | tf_op jit(solution)/shard_map/ppermute | solution.py:304
  80.5 1.4 %collective-permute-done.20.refs_5_ = bf16[128,384]{1,0:T(8,128)(2,1)S(1)} collective-permute-done((bf16[128,384]{1,0:T(8,128)(2,1)S(1)}, bf16[128,384]{1,0:T(8,128)(2,1)S(1)}, u32[]{:S(2)}, u32[]{:S(2)}) %collective-permute-start.20) | collective-permute-done | bytes 98336 | tf_op jit(solution)/shard_map/ppermute | solution.py:304
  81.9 0.2 convert_reduce_fusion
  82.2 1.0 %collective-permute-done.22.refs_7_ = bf16[128,384]{1,0:T(8,128)(2,1)S(1)} collective-permute-done((bf16[128,384]{1,0:T(8,128)(2,1)S(1)}, bf16[128,384]{1,0:T(8,128)(2,1)S(1)}, u32[]{:S(2)}, u32[]{:S(2)}) %collective-permute-start.22) | collective-permute-done | bytes 98336 | tf_op jit(solution)/shard_map/ppermute | solution.py:296
  83.2 1.2 %shard_map.91 = (f32[256,512]{1,0:T(8,128)S(1)}, bf16[256,384]{1,0:T(8,128)(2,1)S(1)}) custom-call(s32[3]{0:T(128)S(1)} %pad_add_fusion.place_ref, s32[1]{0:T(128)} %bitcast.1.win_ref, bf16[128,384]{1,0:T(8,128)(2,1)S(1)} %add_convert_fusion.refs_0_, bf16[128,384]{1,0:T(8,128)(2,1)S(1)} %collective-permute-done.16.refs_1_, ...), custom_call_target="tpu_custom_call" | custom-call | bytes 1048576 | tf_op jit(solution)/shard_map/pallas_call | solution.py:24
  84.4 0.7 shard_map.92
  85.1 9.8 %all_to_all.5 = bf16[8,8,512]{2,1,0:T(8,128)(2,1)S(1)} all-to-all(bf16[8,8,512]{2,1,0:T(8,128)(2,1)S(1)} %bitcast.30), channel_id=1, replica_groups=mesh['segment'=2,'win'=4,'mp'=4] {'segment','win'}, dimensions={0} | all-to-all | bytes 131072 | tf_op jit(solution)/shard_map/all_to_all | solution.py:433
  94.9 0.6 log1p.9
  (44 shorter events, 1.0 us)
Async XLA Ops:
  0.0 24.2 %copy-start = (bf16[384,5,384]{2,0,1:T(8,128)(2,1)S(1)}, bf16[384,5,384]{2,0,1:T(8,128)(2,1)}, u32[]{:S(2)}) copy-start(bf16[384,5,384]{2,0,1:T(8,128)(2,1)} %param.9) | copy-start | bytes 4423684
  0.1 1.2 %copy-start.1 = (bf16[1,1536,256]{2,1,0:T(8,128)(2,1)S(1)}, bf16[1,1536,256]{2,1,0:T(8,128)(2,1)}, u32[]{:S(2)}) copy-start(bf16[1,1536,256]{2,1,0:T(8,128)(2,1)} %param.8) | copy-start | bytes 2359300
  2.2 12.6 %collective-permute-start = (bf16[144,384]{1,0:T(8,128)(2,1)S(1)}, bf16[144,384]{1,0:T(8,128)(2,1)S(1)}, u32[]{:S(2)}, u32[]{:S(2)}) collective-permute-start(bf16[144,384]{1,0:T(8,128)(2,1)S(1)} %get-tuple-element.26), channel_id=1, source_target_pairs={{0,4},{1,13},{2,6},{3,15},{4,8},{5,1},{6,10},{7,3},{8,12},{9,5},{1... | collective-permute-start | bytes 331784 | tf_op jit(solution)/shard_map/ppermute | solution.py:330
  5.3 7.6 %collective-permute-start.2 = (bf16[80,384]{1,0:T(8,128)(2,1)S(1)}, bf16[80,384]{1,0:T(8,128)(2,1)S(1)}, u32[]{:S(2)}, u32[]{:S(2)}) collective-permute-start(bf16[80,384]{1,0:T(8,128)(2,1)S(1)} %get-tuple-element.27), channel_id=1, source_target_pairs={{0,8},{1,9},{2,10},{3,11},{4,12},{5,13},{6,14},{7,15},{8,0},{9,1},... | collective-permute-start | bytes 184328 | tf_op jit(solution)/shard_map/ppermute | solution.py:330
  12.9 10.3 %collective-permute-start.3 = (bf16[80,384]{1,0:T(8,128)(2,1)S(1)}, bf16[80,384]{1,0:T(8,128)(2,1)S(1)}, u32[]{:S(2)}, u32[]{:S(2)}) collective-permute-start(bf16[80,384]{1,0:T(8,128)(2,1)S(1)} %collective-permute-done.2.own_ref), channel_id=1, source_target_pairs={{0,1},{1,0},{2,3},{3,2},{4,5},{5,4},{6,7},{7,6},{8,9},{9,8},{10,11... | collective-permute-start | bytes 184328 | tf_op jit(solution)/shard_map/ppermute | solution.py:296
  13.0 1.0 %copy-start.2 = (bf16[384,640]{1,0:T(8,128)(2,1)S(1)}, bf16[384,640]{1,0:T(8,128)(2,1)}, u32[]{:S(2)}) copy-start(bf16[384,640]{1,0:T(8,128)(2,1)} %x_ref.2) | copy-start | bytes 1474564
  14.8 19.7 %collective-permute-start.7 = (bf16[320,384]{1,0:T(8,128)(2,1)S(1)}, bf16[320,384]{1,0:T(8,128)(2,1)S(1)}, u32[]{:S(2)}, u32[]{:S(2)}) collective-permute-start(bf16[320,384]{1,0:T(8,128)(2,1)S(1)} %shard_map.87.refs_0_), channel_id=1, source_target_pairs={{0,4},{4,8},{8,12},{12,0},{1,5},{5,9},{9,13},{13,1},{2,6},{6,10},{... | collective-permute-start | bytes 737288 | tf_op jit(solution)/shard_map/ppermute | solution.py:37
  14.8 22.4 %collective-permute-start.8 = (bf16[320,384]{1,0:T(8,128)(2,1)S(1)}, bf16[320,384]{1,0:T(8,128)(2,1)S(1)}, u32[]{:S(2)}, u32[]{:S(2)}) collective-permute-start(bf16[320,384]{1,0:T(8,128)(2,1)S(1)} %shard_map.87.refs_0_), channel_id=1, source_target_pairs={{0,12},{4,0},{8,4},{12,8},{1,13},{5,1},{9,5},{13,9},{2,14},{6,2},{... | collective-permute-start | bytes 737288 | tf_op jit(solution)/shard_map/ppermute | solution.py:37
  18.7 1.0 %copy-start.3 = (bf16[384,384]{1,0:T(8,128)(2,1)S(1)}, bf16[384,384]{1,0:T(8,128)(2,1)}, u32[]{:S(2)}) copy-start(bf16[384,384]{1,0:T(8,128)(2,1)} %x_ref.3) | copy-start | bytes 884740
  20.3 11.2 %collective-permute-start.10 = (bf16[192,384]{1,0:T(8,128)(2,1)S(1)}, bf16[192,384]{1,0:T(8,128)(2,1)S(1)}, u32[]{:S(2)}, u32[]{:S(2)}) collective-permute-start(bf16[192,384]{1,0:T(8,128)(2,1)S(1)} %shard_map.88.refs_3_), channel_id=1, source_target_pairs={{0,12},{4,0},{8,4},{12,8},{1,13},{5,1},{9,5},{13,9},{2,14},{6,2},{... | collective-permute-start | bytes 442376 | tf_op jit(solution)/shard_map/ppermute | solution.py:37
  22.0 15.2 %collective-permute-start.9 = (bf16[192,384]{1,0:T(8,128)(2,1)S(1)}, bf16[192,384]{1,0:T(8,128)(2,1)S(1)}, u32[]{:S(2)}, u32[]{:S(2)}) collective-permute-start(bf16[192,384]{1,0:T(8,128)(2,1)S(1)} %shard_map.88.refs_3_), channel_id=1, source_target_pairs={{0,4},{4,8},{8,12},{12,0},{1,5},{5,9},{9,13},{13,1},{2,6},{6,10},{... | collective-permute-start | bytes 442376 | tf_op jit(solution)/shard_map/ppermute | solution.py:37
  23.2 2.5 %collective-permute-start.1 = (bf16[144,384]{1,0:T(8,128)(2,1)S(1)}, bf16[144,384]{1,0:T(8,128)(2,1)S(1)}, u32[]{:S(2)}, u32[]{:S(2)}) collective-permute-start(bf16[144,384]{1,0:T(8,128)(2,1)S(1)} %collective-permute-done.x_ref), channel_id=1, source_target_pairs={{0,1},{1,0},{2,3},{3,2},{4,5},{5,4},{6,7},{7,6},{8,9},{9,8},{10,11... | collective-permute-start | bytes 331784 | tf_op jit(solution)/shard_map/ppermute | solution.py:296
  25.7 11.7 %collective-permute-start.4 = (bf16[128,384]{1,0:T(8,128)(2,1)S(1)}, bf16[128,384]{1,0:T(8,128)(2,1)S(1)}, u32[]{:S(2)}, u32[]{:S(2)}) collective-permute-start(bf16[128,384]{1,0:T(8,128)(2,1)S(1)} %shard_map.83), channel_id=1, source_target_pairs={{0,12},{1,5},{2,14},{3,7},{4,0},{5,9},{6,2},{7,11},{8,4},{9,13},{1... | collective-permute-start | bytes 294920 | tf_op jit(solution)/shard_map/ppermute | solution.py:330
  28.9 15.4 %copy-start.6 = (f32[384]{0:T(512)S(1)}, f32[384]{0:T(512)}, u32[]{:S(2)}) copy-start(f32[384]{0:T(512)} %param.10) | copy-start | bytes 4612
  31.6 12.7 %collective-permute-start.6 = (bf16[128,384]{1,0:T(8,128)(2,1)S(1)}, bf16[128,384]{1,0:T(8,128)(2,1)S(1)}, u32[]{:S(2)}, u32[]{:S(2)}) collective-permute-start(bf16[128,384]{1,0:T(8,128)(2,1)S(1)} %shard_map.85), channel_id=1, source_target_pairs={{0,8},{1,9},{2,10},{3,11},{4,12},{5,13},{6,14},{7,15},{8,0},{9,1},... | collective-permute-start | bytes 294920 | tf_op jit(solution)/shard_map/ppermute | solution.py:330
  34.5 8.4 %collective-permute-start.5 = (bf16[128,384]{1,0:T(8,128)(2,1)S(1)}, bf16[128,384]{1,0:T(8,128)(2,1)S(1)}, u32[]{:S(2)}, u32[]{:S(2)}) collective-permute-start(bf16[128,384]{1,0:T(8,128)(2,1)S(1)} %shard_map.84), channel_id=1, source_target_pairs={{0,4},{1,13},{2,6},{3,15},{4,8},{5,1},{6,10},{7,3},{8,12},{9,5},{1... | collective-permute-start | bytes 294920 | tf_op jit(solution)/shard_map/ppermute | solution.py:330
  42.9 14.4 %collective-permute-start.11 = (bf16[512,384]{1,0:T(8,128)(2,1)S(1)}, bf16[512,384]{1,0:T(8,128)(2,1)S(1)}, u32[]{:S(2)}, u32[]{:S(2)}) collective-permute-start(bf16[512,384]{1,0:T(8,128)(2,1)S(1)} %maximum_select_fusion), channel_id=1, source_target_pairs={{0,8},{4,0},{8,12},{12,4},{1,9},{5,1},{9,13},{13,5},{2,10},{6,2},{... | collective-permute-start | bytes 1179656 | tf_op jit(solution)/shard_map/ppermute | solution.py:278
  44.4 21.5 %collective-permute-start.24 = (bf16[384,512]{1,0:T(8,128)(2,1)S(1)}, bf16[384,512]{1,0:T(8,128)(2,1)S(1)}, u32[]{:S(2)}, u32[]{:S(2)}) collective-permute-start(bf16[384,512]{1,0:T(8,128)(2,1)S(1)} %constant_dynamic-slice_fusion.refs_8_), channel_id=1, source_target_pairs={{0,12},{4,0},{8,4},{12,8},{1,13},{5,1},{9,5},{13,9},{2,14},{6,2},{... | collective-permute-start | bytes 1179656 | tf_op jit(solution)/shard_map/ppermute | solution.py:37
  44.9 15.3 %copy-start.5 = (s32[3,1,8,8]{3,2,1,0:T(8,128)S(1)}, s32[3,1,8,8]{3,2,1,0:T(8,128)}, u32[]{:S(2)}) copy-start(s32[3,1,8,8]{3,2,1,0:T(8,128)} %param.15) | copy-start | bytes 2308
  57.1 13.8 %collective-permute-start.23 = (bf16[384,512]{1,0:T(8,128)(2,1)S(1)}, bf16[384,512]{1,0:T(8,128)(2,1)S(1)}, u32[]{:S(2)}, u32[]{:S(2)}) collective-permute-start(bf16[384,512]{1,0:T(8,128)(2,1)S(1)} %constant_dynamic-slice_fusion.refs_8_), channel_id=1, source_target_pairs={{0,4},{4,8},{8,12},{12,0},{1,5},{5,9},{9,13},{13,1},{2,6},{6,10},{... | collective-permute-start | bytes 1179656 | tf_op jit(solution)/shard_map/ppermute | solution.py:37
  57.3 13.7 %copy-start.4 = (bf16[384,1024]{1,0:T(8,128)(2,1)S(1)}, bf16[384,1024]{1,0:T(8,128)(2,1)}, u32[]{:S(2)}) copy-start(bf16[384,1024]{1,0:T(8,128)(2,1)} %param.13) | copy-start | bytes 2359300
  60.0 1.8 %collective-permute-start.12 = (bf16[4,128,384]{2,1,0:T(8,128)(2,1)S(1)}, bf16[4,128,384]{2,1,0:T(8,128)(2,1)S(1)}, u32[]{:S(2)}, u32[]{:S(2)}) collective-permute-start(bf16[4,128,384]{2,1,0:T(8,128)(2,1)S(1)} %get-tuple-element.33), channel_id=1, source_target_pairs={{0,1},{1,0},{2,3},{3,2},{4,5},{5,4},{6,7},{7,6},{8,9},{9,8},{10,11... | collective-permute-start | bytes 1179656 | tf_op jit(solution)/shard_map/ppermute | solution.py:296
  62.4 10.7 %collective-permute-start.13 = (bf16[128,384]{1,0:T(8,128)(2,1)S(1)}, bf16[128,384]{1,0:T(8,128)(2,1)S(1)}, u32[]{:S(2)}, u32[]{:S(2)}) collective-permute-start(bf16[128,384]{1,0:T(8,128)(2,1)S(1)} %get-tuple-element.35), channel_id=1, source_target_pairs={{0,16},{1,17},{2,18},{3,19},{16,0},{17,1},{18,2},{19,3},{4,20},{5,... | collective-permute-start | bytes 294920 | tf_op jit(solution)/shard_map/ppermute | solution.py:396
  64.0 9.1 %collective-permute-start.14 = (bf16[128,384]{1,0:T(8,128)(2,1)S(1)}, bf16[128,384]{1,0:T(8,128)(2,1)S(1)}, u32[]{:S(2)}, u32[]{:S(2)}) collective-permute-start(bf16[128,384]{1,0:T(8,128)(2,1)S(1)} %get-tuple-element.36), channel_id=1, source_target_pairs={{0,2},{1,3},{2,0},{3,1},{16,18},{17,19},{18,16},{19,17},{4,6},{5,7... | collective-permute-start | bytes 294920 | tf_op jit(solution)/shard_map/ppermute | solution.py:396
  64.5 8.6 %collective-permute-start.15 = (bf16[128,384]{1,0:T(8,128)(2,1)S(1)}, bf16[128,384]{1,0:T(8,128)(2,1)S(1)}, u32[]{:S(2)}, u32[]{:S(2)}) collective-permute-start(bf16[128,384]{1,0:T(8,128)(2,1)S(1)} %get-tuple-element.37), channel_id=1, source_target_pairs={{0,18},{1,19},{2,16},{3,17},{16,2},{17,3},{18,0},{19,1},{4,22},{5,... | collective-permute-start | bytes 294920 | tf_op jit(solution)/shard_map/ppermute | solution.py:396
  71.1 13.2 %collective-permute-start.25 = (bf16[384,512]{1,0:T(8,128)(2,1)S(1)}, bf16[384,512]{1,0:T(8,128)(2,1)S(1)}, u32[]{:S(2)}, u32[]{:S(2)}) collective-permute-start(bf16[384,512]{1,0:T(8,128)(2,1)S(1)} %select_select_fusion), channel_id=1, source_target_pairs={{0,8},{4,0},{8,12},{12,4},{1,9},{5,1},{9,13},{13,5},{2,10},{6,2},{... | collective-permute-start | bytes 1179656 | tf_op jit(solution)/shard_map/ppermute | solution.py:278
  73.2 4.7 %collective-permute-start.16 = (bf16[128,384]{1,0:T(8,128)(2,1)S(1)}, bf16[128,384]{1,0:T(8,128)(2,1)S(1)}, u32[]{:S(2)}, u32[]{:S(2)}) collective-permute-start(bf16[128,384]{1,0:T(8,128)(2,1)S(1)} %add_convert_fusion.refs_0_), channel_id=1, source_target_pairs={{0,16},{1,17},{2,18},{3,19},{16,0},{17,1},{18,2},{19,3},{4,20},{5,... | collective-permute-start | bytes 294920 | tf_op jit(solution)/shard_map/ppermute | solution.py:304
  74.8 5.7 %collective-permute-start.19 = (bf16[128,384]{1,0:T(8,128)(2,1)S(1)}, bf16[128,384]{1,0:T(8,128)(2,1)S(1)}, u32[]{:S(2)}, u32[]{:S(2)}) collective-permute-start(bf16[128,384]{1,0:T(8,128)(2,1)S(1)} %add_convert_fusion.refs_0_), channel_id=1, source_target_pairs={{0,2},{1,3},{2,0},{3,1},{16,18},{17,19},{18,16},{19,17},{4,6},{5,7... | collective-permute-start | bytes 294920 | tf_op jit(solution)/shard_map/ppermute | solution.py:304
  76.4 5.5 %collective-permute-start.20 = (bf16[128,384]{1,0:T(8,128)(2,1)S(1)}, bf16[128,384]{1,0:T(8,128)(2,1)S(1)}, u32[]{:S(2)}, u32[]{:S(2)}) collective-permute-start(bf16[128,384]{1,0:T(8,128)(2,1)S(1)} %add_convert_fusion.refs_0_), channel_id=1, source_target_pairs={{0,18},{1,19},{2,16},{3,17},{16,2},{17,3},{18,0},{19,1},{4,22},{5,... | collective-permute-start | bytes 294920 | tf_op jit(solution)/shard_map/ppermute | solution.py:304
  76.8 5.4 %collective-permute-start.17 = (bf16[128,384]{1,0:T(8,128)(2,1)S(1)}, bf16[128,384]{1,0:T(8,128)(2,1)S(1)}, u32[]{:S(2)}, u32[]{:S(2)}) collective-permute-start(bf16[128,384]{1,0:T(8,128)(2,1)S(1)} %add_convert_fusion.refs_0_), channel_id=1, source_target_pairs={{0,1},{1,0},{2,3},{3,2},{4,5},{5,4},{6,7},{7,6},{8,9},{9,8},{10,11... | collective-permute-start | bytes 294920 | tf_op jit(solution)/shard_map/ppermute | solution.py:296
  77.9 4.3 %collective-permute-start.18 = (bf16[128,384]{1,0:T(8,128)(2,1)S(1)}, bf16[128,384]{1,0:T(8,128)(2,1)S(1)}, u32[]{:S(2)}, u32[]{:S(2)}) collective-permute-start(bf16[128,384]{1,0:T(8,128)(2,1)S(1)} %collective-permute-done.16.refs_1_), channel_id=1, source_target_pairs={{0,1},{1,0},{2,3},{3,2},{4,5},{5,4},{6,7},{7,6},{8,9},{9,8},{10,11... | collective-permute-start | bytes 294920 | tf_op jit(solution)/shard_map/ppermute | solution.py:296
  80.5 1.6 %collective-permute-start.21 = (bf16[128,384]{1,0:T(8,128)(2,1)S(1)}, bf16[128,384]{1,0:T(8,128)(2,1)S(1)}, u32[]{:S(2)}, u32[]{:S(2)}) collective-permute-start(bf16[128,384]{1,0:T(8,128)(2,1)S(1)} %collective-permute-done.19.refs_4_), channel_id=1, source_target_pairs={{0,1},{1,0},{2,3},{3,2},{4,5},{5,4},{6,7},{7,6},{8,9},{9,8},{10,11... | collective-permute-start | bytes 294920 | tf_op jit(solution)/shard_map/ppermute | solution.py:296
  81.9 1.3 %collective-permute-start.22 = (bf16[128,384]{1,0:T(8,128)(2,1)S(1)}, bf16[128,384]{1,0:T(8,128)(2,1)S(1)}, u32[]{:S(2)}, u32[]{:S(2)}) collective-permute-start(bf16[128,384]{1,0:T(8,128)(2,1)S(1)} %collective-permute-done.20.refs_5_), channel_id=1, source_target_pairs={{0,1},{1,0},{2,3},{3,2},{4,5},{5,4},{6,7},{7,6},{8,9},{9,8},{10,11... | collective-permute-start | bytes 294920 | tf_op jit(solution)/shard_map/ppermute | solution.py:296
